TPU v7x, 32 devices: a whole 2x2x4 slice. The times are simulated.
32 devices in a mesh: rep: 2 (over x), grp: 8 (over z, y), tp: 2 (over core).
Axes of the slice: x: 2, y: 2, z: 4, core: 2. Of those that a mesh axis runs over, the one named last changes fastest.
Arguments:
- hidden: bfloat16 [4, 3584, 8192], P(None, ('rep', 'grp'), 'tp'), parts along dimension 1, may hold values from -6 to 6
- base_weight: bfloat16 [8192, 512], P('tp'), may hold values from -0.0625 to 0.0625
- pool_down: bfloat16 [8, 8192, 64], P('grp', 'tp'), may hold values from -0.0625 to 0.0625
- pool_up: bfloat16 [8, 64, 512], P('grp'), may hold values from -0.75 to 0.75
- adapter_home: int32 [8], replicated, may hold values from 0 to 7, each once
- block_adapter: int32 [16, 2], P('rep'), parts along dimension 0, may hold values from 0 to 7
- block_count: int32 [16], P('rep'), parts along dimension 0, may hold values from 1 to 2, as said below
Outputs:
- projected: bfloat16 [4, 3584, 512], P(None, ('rep', 'grp'), 'tp'), parts along dimension 1
There are 2 independent parts, one for each index of `rep`. A program takes and returns all parts, laid end to end along the dimension named above; an argument that names none is the same for every part. Nothing has to cross between parts.
Inputs may be any that keep to these rules, and one draw needn't show every extreme that they name: `block_count`: every group uses 1 to 2 blocks and some group uses all 2; entries of block_adapter past a group's count are ignored. An adapter may fill several blocks of a group. `adapter_home`: A permutation of the pool positions; position q is held by owner group q.
All inputs are finite; a program needn't handle non-finite values.
Results may differ from a plain program's by a relative error of at most 0.001.
Values may be sent and summed in bfloat16 or wider, within the bound.
No kernel may reach another device: no remote copies, remote signals or barrier semaphores. Data moves between devices by JAX's collectives and lax.ppermute only.
A program may use at most 64 MiB of HBM per device.

v0:
```python
import jax
import jax.numpy as jnp
from jax import lax
from jax.sharding import PartitionSpec as P

adapter_scale_factor = 0.5


def local(hidden, base_weight, pool_down, pool_up, adapter_home, block_adapter, block_count):
    step_count, row_count, half_width = hidden.shape
    group_count = lax.axis_size("grp")
    tp_count = lax.axis_size("tp")
    own_count, _, rank_width = pool_down.shape
    col_count = pool_up.shape[2]
    slot_count = block_adapter.shape[1]
    block_rows = row_count // slot_count
    piece_rows = half_width // group_count
    up_flat = rank_width * col_count // group_count
    down_parts = pool_down.reshape(own_count, group_count, piece_rows * rank_width)
    up_parts = pool_up.reshape(own_count, group_count, up_flat)
    down_slices, up_slices = (
        lax.all_to_all(down_parts, "grp", split_axis=1, concat_axis=0, tiled=True),
        lax.all_to_all(up_parts, "grp", split_axis=1, concat_axis=0, tiled=True),
    )
    down_slices = down_slices.reshape(own_count * group_count, piece_rows * rank_width)
    up_slices = up_slices.reshape(own_count * group_count, up_flat)
    position = adapter_home[block_adapter]
    group_index = lax.axis_index("grp")
    live_count = block_count[group_index]
    live_slots = jnp.arange(slot_count, dtype=jnp.int32) < live_count
    base_projection_output = jnp.dot(
        hidden.reshape(step_count * row_count, half_width),
        base_weight,
        preferred_element_type=jnp.float32,
    )
    base_projection_output = base_projection_output.reshape(
        step_count, slot_count, block_rows, col_count
    )
    row_blocks = hidden.reshape(step_count, slot_count, block_rows, half_width)
    send_down = down_slices[position].reshape(group_count, slot_count, 1, piece_rows * rank_width)
    send_up = up_slices[position].reshape(group_count, slot_count, 1, up_flat)
    got_down, got_up = (
        lax.all_to_all(send_down, "grp", split_axis=0, concat_axis=2, tiled=True),
        lax.all_to_all(send_up, "grp", split_axis=0, concat_axis=2, tiled=True),
    )
    down_mine = got_down.reshape(slot_count, half_width, rank_width)
    local_up_weight = got_up.reshape(slot_count, rank_width, col_count)
    adapter_shrunk_rows = jnp.einsum(
        "scbd,cdr->scbr", row_blocks, down_mine, preferred_element_type=jnp.float32
    )
    adapter_shrunk_rows = jnp.where(
        live_slots[None, :, None, None], adapter_shrunk_rows, jnp.float32(0.0)
    )
    adapter_shrunk_rows = lax.psum(adapter_shrunk_rows, "tp")
    base_output_portion = lax.psum_scatter(
        base_projection_output, "tp", scatter_dimension=3, tiled=True
    )
    share_width = col_count // tp_count
    up_cols = lax.dynamic_slice_in_dim(
        local_up_weight, lax.axis_index("tp") * share_width, share_width, 2
    )
    adapter_expanded_rows = jnp.einsum(
        "scbr,crn->scbn",
        adapter_shrunk_rows,
        up_cols.astype(jnp.float32),
        precision=lax.Precision.HIGHEST,
    )
    final_output_rows = base_output_portion + adapter_scale_factor * adapter_expanded_rows
    return final_output_rows.reshape(step_count, row_count, final_output_rows.shape[3]).astype(
        jnp.bfloat16
    )


def solution(mesh):
    in_specs = (
        P(None, ("rep", "grp"), "tp"),
        P("tp", None),
        P("grp", "tp", None),
        P("grp", None, None),
        P(),
        P("rep", None),
        P("rep"),
    )
    out_specs = P(None, ("rep", "grp"), "tp")
    return jax.shard_map(local, mesh=mesh, in_specs=in_specs, out_specs=out_specs, check_vma=False)
```

profile of v0, /device:TPU:0, one launch (start us, length us, event | category | flops | bytes accessed | tf_op | source)
XLA Modules:
  0.0 121.8 jit_solution(1983749834197484137)
XLA Ops:
  6.5 1.5 %copy.31 = bf16[1,4096,64]{2,1,0:T(8,128)(2,1)S(1)} copy(bf16[1,4096,64]{1,2,0:T(8,128)(2,1)} %param.9) | data formatting | bytes 1048576 | tf_op args[2]
  8.1 0.7 reshape.101
  8.8 0.6 broadcast.51
  9.4 4.0 %reduce = bf16[8,32768]{1,0:T(8,128)(2,1)S(1)} reduce(bf16[8,1,32768]{2,1,0:T(2,128)(2,1)S(1)} %bitcast.61, bf16[]{:T(256)} %broadcast.51), dimensions={1}, to_apply=%bitcast.50.reduce_sub_computation | reduce | bytes 1048578
  13.3 1.2 reshape.102
  14.5 7.3 %all-to-all-start.2 = ((bf16[8,2,16384]{2,1,0:T(2,128)(2,1)}), bf16[8,2,16384]{2,1,0:T(2,128)(2,1)S(1)}, u32[]{:S(2)}, u32[]{:S(2)}) async-start(bf16[8,2,16384]{2,1,0:T(2,128)(2,1)} %reshape.102), calls=%async_computation.3 | async-start | bytes 1048576 | tf_op jit(solution)/shard_map/all_to_all | solution.py:22
  22.0 0.7 gather_fusion
  22.8 13.4 %all-to-all-done.2 = bf16[8,2,16384]{2,1,0:T(2,128)(2,1)S(1)} async-done(((bf16[8,2,16384]{2,1,0:T(2,128)(2,1)}), bf16[8,2,16384]{2,1,0:T(2,128)(2,1)S(1)}, u32[]{:S(2)}, u32[]{:S(2)}) %all-to-all-start.2) | async-done | bytes 524320 | tf_op jit(solution)/shard_map/all_to_all | solution.py:22
  37.4 1.2 %gather_fusion.2 = bf16[16,32768]{1,0:T(8,128)(2,1)S(1)} fusion(bf16[8,32768]{1,0:T(8,128)(2,1)S(1)} %bitcast.57, s32[1024]{0:T(1024)S(1)} %pad_clamp_fusion), kind=kCustom, calls=%fused_computation.2 | custom fusion | bytes 2097216 | tf_op jit(solution)/shard_map/gather | solution.py:40
  38.7 1.5 %reshape.64 = bf16[8,2,1,32768]{3,1,0,2:T(2,128)(2,1)} reshape(bf16[16,32768]{1,0:T(8,128)(2,1)S(1)} %gather_fusion.2) | data formatting | bytes 2097152 | tf_op jit(solution)/shard_map/reshape | solution.py:40
  40.2 3.6 %all-to-all-start.3 = ((bf16[8,2,1,32768]{3,1,2,0:T(2,128)(2,1)}), bf16[8,2,1,32768]{3,1,2,0:T(2,128)(2,1)S(1)}, u32[]{:S(2)}, u32[]{:S(2)}) async-start(bf16[8,2,1,32768]{3,1,2,0:T(2,128)(2,1)} %bitcast.8), calls=%async_computation.4 | async-start | bytes 2097152 | tf_op jit(solution)/shard_map/all_to_all | solution.py:43
  43.9 0.6 dynamic_slice.7
  44.4 0.6 iota_compare_fusion
  45.1 24.6 %all-to-all-done.3 = bf16[8,2,1,32768]{3,1,2,0:T(2,128)(2,1)S(1)} async-done(((bf16[8,2,1,32768]{3,1,2,0:T(2,128)(2,1)}), bf16[8,2,1,32768]{3,1,2,0:T(2,128)(2,1)S(1)}, u32[]{:S(2)}, u32[]{:S(2)}) %all-to-all-start.3) | async-done | bytes 1048608 | tf_op jit(solution)/shard_map/all_to_all | solution.py:43
  70.3 2.3 %reshape.65 = bf16[2,4096,64]{2,1,0:T(8,128)(2,1)S(1)} reshape(bf16[1,2,8,1,32768]{4,2,1,3,0:T(8,128)(2,1)S(1)} %copy.34) | data formatting | bytes 2097152 | tf_op jit(solution)/shard_map/reshape | solution.py:46
  72.6 6.1 %fusion.13 = f32[4,2,112,64]{2,3,0,1:T(8,128)} fusion(bf16[4,2,112,4096]{3,2,1,0:T(8,128)(2,1)} %bitcast.65, bf16[2,4096,64]{2,1,0:T(8,128)(2,1)S(1)} %reshape.65, pred[2]{0:T(512)(128)(4,1)S(1)} %iota_compare_fusion), kind=kOutput, calls=%fused_computation.13 | convolution fusion | flops 469819392 | bytes 8617986 | tf_op jit(solution)/shard_map/scbd,cdr->scbr/dot_general | solution.py:48
  79.0 9.5 %fusion.2 = f32[4,2,112,512]{3,2,1,0:T(8,128)} fusion(bf16[4,2,112,4096]{3,2,1,0:T(8,128)(2,1)} %bitcast.66, bf16[4096,512]{1,0:T(8,128)(2,1)} %param.8), kind=kOutput, calls=%fused_computation.5 | convolution fusion | flops 3758096384 | bytes 13369344 | tf_op jit(solution)/shard_map/dot_general | solution.py:31
  88.5 1.1 reduce.1
  89.6 10.3 %all_to_all.48 = bf16[8,2,2048]{2,1,0:T(2,128)(2,1)S(1)} all-to-all(bf16[8,2,2048]{2,1,0:T(2,128)(2,1)S(1)} %reshape.104), channel_id=1, replica_groups=mesh['rep'=2,'grp'=8,'tp'=2] {'grp'}, dimensions={0} | all-to-all | bytes 131072 | tf_op jit(solution)/shard_map/all_to_all | solution.py:23
  100.1 0.6 gather_fusion.1
  100.7 0.8 reshape.60
  101.5 3.4 %all-to-all-start.1 = ((bf16[8,2,1,4096]{3,1,2,0:T(2,128)(2,1)}), bf16[8,2,1,4096]{3,1,2,0:T(2,128)(2,1)S(1)}, u32[]{:S(2)}, u32[]{:S(2)}) async-start(bf16[8,2,1,4096]{3,1,2,0:T(2,128)(2,1)} %bitcast.3), calls=%async_computation.2 | async-start | bytes 262144 | tf_op jit(solution)/shard_map/all_to_all | solution.py:44
  104.9 7.3 %all-to-all-done.1 = bf16[8,2,1,4096]{3,1,2,0:T(2,128)(2,1)S(1)} async-done(((bf16[8,2,1,4096]{3,1,2,0:T(2,128)(2,1)}), bf16[8,2,1,4096]{3,1,2,0:T(2,128)(2,1)S(1)}, u32[]{:S(2)}, u32[]{:S(2)}) %all-to-all-start.1) | async-done | bytes 131104 | tf_op jit(solution)/shard_map/all_to_all | solution.py:44
  112.4 2.6 %fusion.7 = bf16[4,2,112,256]{3,2,1,0:T(8,128)(2,1)} fusion(f32[4,2,112,256]{3,2,1,0:T(8,128)} %reduce-scatter.2.cloned.1.call-done, f32[4,2,112,64]{2,3,0,1:T(8,128)} %all-reduce.2.cloned.1.call-done, bf16[2,64,512]{2,1,0:T(8,128)(2,1)S(1)} %reshape.61, s32[]{:T(128)S(6)} %select_n.29), kind=kOutput, calls=%fused_computation.11 | convolution fusion | flops 176848896 | bytes 1671172 | tf_op jit(solution)/shard_map/scbr,crn->scbn/dot_general | solution.py:62
  (31 shorter events, 2.7 us)
Async XLA Ops:
  6.5 15.5 %copy-start = (s32[8]{0:T(128)S(1)}, s32[8]{0:T(128)}, u32[]{:S(2)}) copy-start(s32[8]{0:T(128)} %param.11) | copy-start | bytes 100
  6.5 15.3 %copy-start.2 = (s32[8,2]{0,1:T(2,128)S(1)}, s32[8,2]{0,1:T(2,128)}, u32[]{:S(2)}) copy-start(s32[8,2]{0,1:T(2,128)} %param.12) | copy-start | bytes 196
  14.5 21.8 %all-to-all-start.2 = ((bf16[8,2,16384]{2,1,0:T(2,128)(2,1)}), bf16[8,2,16384]{2,1,0:T(2,128)(2,1)S(1)}, u32[]{:S(2)}, u32[]{:S(2)}) async-start(bf16[8,2,16384]{2,1,0:T(2,128)(2,1)} %reshape.102), calls=%async_computation.3 | async-start | bytes 1048576 | tf_op jit(solution)/shard_map/all_to_all | solution.py:22
  38.6 5.2 %copy-start.3 = (s32[8]{0:T(128)S(1)}, s32[8]{0:T(128)}, u32[]{:S(2)}) copy-start(s32[8]{0:T(128)} %param.13) | copy-start | bytes 100
  40.2 29.6 %all-to-all-start.3 = ((bf16[8,2,1,32768]{3,1,2,0:T(2,128)(2,1)}), bf16[8,2,1,32768]{3,1,2,0:T(2,128)(2,1)S(1)}, u32[]{:S(2)}, u32[]{:S(2)}) async-start(bf16[8,2,1,32768]{3,1,2,0:T(2,128)(2,1)} %bitcast.8), calls=%async_computation.4 | async-start | bytes 2097152 | tf_op jit(solution)/shard_map/all_to_all | solution.py:43
  43.8 68.6 %all-reduce.2.cloned.1.call-start = ((), (), s32[]{:S(2)}) async-start(), calls=%async_computation.6 | async-start | bytes 524288 | tf_op jit(solution)/shard_map/psum | solution.py:54
  78.7 9.7 %copy-start.1 = (bf16[1,64,512]{2,1,0:T(8,128)(2,1)S(1)}, bf16[1,64,512]{2,1,0:T(8,128)(2,1)}, u32[]{:S(2)}) copy-start(bf16[1,64,512]{2,1,0:T(8,128)(2,1)} %param.10) | copy-start | bytes 196612
  78.7 33.6 %reduce-scatter.2.cloned.1.call-start = ((), (), s32[]{:S(2)}) async-start(), calls=%async_computation.5 | async-start | bytes 2752512 | tf_op jit(solution)/shard_map/reduce_scatter | solution.py:55
  101.5 10.7 %all-to-all-start.1 = ((bf16[8,2,1,4096]{3,1,2,0:T(2,128)(2,1)}), bf16[8,2,1,4096]{3,1,2,0:T(2,128)(2,1)S(1)}, u32[]{:S(2)}, u32[]{:S(2)}) async-start(bf16[8,2,1,4096]{3,1,2,0:T(2,128)(2,1)} %bitcast.3), calls=%async_computation.2 | async-start | bytes 262144 | tf_op jit(solution)/shard_map/all_to_all | solution.py:44
Sparse Core Ops, SparseCore 0:
  78.8 17.3 all-reduce.1
  98.5 10.5 reduce-scatter.1
where the time goes:
time: 122 us
  waiting for transfers between devices  45.4 us (37%)
  matrix products  18.2 us (15%)
  starting transfers between devices  14.5 us (12%)
  local copies, waits for them, and re-layouts  14 us (11%)
  between operations  13.6 us (11%)
  blocking collectives  10.3 us (8%)
  other arithmetic  5.7 us (5%)
    all_to_all x1, waiting for transfers between devices, local(): lax.all_to_all(send_down, 'grp', split_axis=0, concat_axis=2, tiled=True)  24.6 us
    all_to_all x1, waiting for transfers between devices, local(): lax.all_to_all(down_parts, 'grp', split_axis=1, concat_axis=0, tiled=True)  13.4 us
    all_to_all x1, blocking collectives, local(): lax.all_to_all(up_parts, 'grp', split_axis=1, concat_axis=0, tiled=True)  10.3 us
    dot_general x1, matrix products, local(): jnp.dot(hidden.reshape(step_count * row_count, half_width), base_weight,...  9.48 us
    all_to_all x1, starting transfers between devices, local(): lax.all_to_all(down_parts, 'grp', split_axis=1, concat_axis=0, tiled=True)  7.28 us
    all_to_all x1, waiting for transfers between devices, local(): lax.all_to_all(send_up, 'grp', split_axis=0, concat_axis=2, tiled=True)  7.28 us
    dot_general x1, matrix products, local(): jnp.einsum('scbd,cdr->scbr', row_blocks, down_mine, preferred_element_typ...  6.08 us
    unnamed x2, other arithmetic  5.03 us
  transfers between devices with their start and end apart: 5, of which 3 were waited for; matrix products, arithmetic and copies ran while one was open for 12% of the time, Pallas kernels for 0%

commit v1 on v0

v1 whole, which is shorter than its diff:
```python
import functools

import jax
import jax.numpy as jnp
from jax import lax
from jax.experimental import pallas as pl
from jax.experimental.pallas import tpu as pltpu
from jax.sharding import PartitionSpec as P

adapter_scale_factor = 0.5
MEMBERS = 8
PIECE_ROWS = 16

ANY = pl.BlockSpec(memory_space=pl.ANY)
SMEM = pl.BlockSpec(memory_space=pltpu.SMEM)
VMEM = pl.BlockSpec(memory_space=pltpu.VMEM)


def pack_kernel(near, halves, down_ref, up_ref, *refs):
    outs, sem = refs[:near], refs[near]
    member_base = lax.axis_index("rep") * near
    low = lax.rem(lax.axis_index("grp"), near)
    tp_index = lax.axis_index("tp")
    wide = down_ref.shape[1] // halves
    up_own = up_ref.shape[1] // lax.axis_size("tp")
    up_wide = up_own // halves
    copies = []
    for flip in range(near):
        member = member_base + (low ^ flip)
        rows = pl.ds(pl.multiple_of(member // halves * PIECE_ROWS, PIECE_ROWS), PIECE_ROWS)
        half = lax.rem(member, halves)
        copies.append(
            pltpu.make_async_copy(
                down_ref.at[rows, pl.ds(pl.multiple_of(half * wide, 128), wide)],
                outs[flip].at[:, pl.ds(0, wide)],
                sem.at[2 * flip],
            )
        )
        copies.append(
            pltpu.make_async_copy(
                up_ref.at[
                    rows, pl.ds(pl.multiple_of(tp_index * up_own + half * up_wide, 128), up_wide)
                ],
                outs[flip].at[:, pl.ds(wide, up_wide)],
                sem.at[2 * flip + 1],
            )
        )
    for copy in copies:
        copy.start()
    for copy in copies:
        copy.wait()


def select_kernel(near, rep_count, part_count, home_ref, *refs):
    wanted, refs = refs[:rep_count], refs[rep_count:]
    held, refs = refs[:part_count], refs[part_count:]
    outs, sem = refs[: near * rep_count], refs[near * rep_count]
    group_index = lax.axis_index("grp")
    slot_count = outs[0].shape[0]
    depth = held[0].shape[0]
    pool_size = home_ref.shape[0]
    for flip in range(near * rep_count):
        other = group_index ^ (flip % near)
        for slot in range(slot_count):
            adapter = jnp.clip(wanted[flip // near][other, slot], 0, pool_size - 1)
            place = jnp.clip(home_ref[adapter], 0, pool_size - 1) ^ group_index
            for part in range(part_count):

                @pl.when(place // depth == part)
                def _():
                    pltpu.make_async_copy(
                        held[part].at[lax.rem(place, depth)],
                        outs[flip].at[slot],
                        sem.at[flip * slot_count + slot],
                    ).start()

    for flip in range(near * rep_count):
        for slot in range(slot_count):
            pltpu.make_async_copy(
                held[0].at[0], outs[flip].at[slot], sem.at[flip * slot_count + slot]
            ).wait()


def base_kernel(x_ref, weight_ref, mine_ref, theirs_ref):
    share = mine_ref.shape[2]
    product = jnp.dot(x_ref[0], weight_ref[...], preferred_element_type=jnp.float32)
    tp_index = lax.axis_index("tp")

    @pl.when(tp_index == 0)
    def _():
        mine_ref[0] = product[:, :share]
        theirs_ref[0] = product[:, share:]

    @pl.when(tp_index == 1)
    def _():
        mine_ref[0] = product[:, share:]
        theirs_ref[0] = product[:, :share]


def shrink_kernel(member_count, halves, rank, count_ref, x_ref, *refs):
    pieces, refs = refs[:member_count], refs[member_count:]
    shrunk_ref, up_ref, down = refs
    slot_count = pieces[0].shape[0]
    wide = down.shape[1] // halves
    up_wide = up_ref.shape[1] // halves
    group_index = lax.axis_index("grp")

    @pl.when(pl.program_id(0) == 0)
    def _():
        for flip in range(member_count):
            half = lax.rem(group_index ^ flip, halves)
            for slot in range(slot_count):
                rows = pl.ds(slot * rank + flip // halves * PIECE_ROWS, PIECE_ROWS)
                down[rows, pl.ds(pl.multiple_of(half * wide, 128), wide)] = pieces[flip][
                    slot, :, :wide
                ]
                up_ref[rows, pl.ds(pl.multiple_of(half * up_wide, 128), up_wide)] = pieces[flip][
                    slot, :, wide:
                ]

    product = lax.dot_general(
        x_ref[0], down[...], (((1,), (1,)), ((), ())), preferred_element_type=jnp.float32
    )
    rows = product.shape[0] // slot_count
    slot_of = lax.broadcasted_iota(jnp.int32, (rows, product.shape[1]), 1) // rank
    live_count = count_ref[group_index]
    packed = jnp.zeros((rows, product.shape[1]), jnp.float32)
    for slot in range(slot_count):
        keep = (slot_of == slot) & (slot < live_count)
        packed = jnp.where(keep, product[slot * rows : (slot + 1) * rows], packed)
    shrunk_ref[0] = packed


def expand_kernel(slot_count, rank, mine_ref, theirs_ref, up_ref, base_ref, out_ref):
    shrunk = mine_ref[0] + theirs_ref[0]
    rows = shrunk.shape[0]
    slot_of = lax.broadcasted_iota(jnp.int32, shrunk.shape, 1) // rank
    up = up_ref[...]
    top = shrunk.astype(jnp.bfloat16)
    rest = shrunk - top.astype(jnp.float32)
    mid = rest.astype(jnp.bfloat16)
    low = (rest - mid.astype(jnp.float32)).astype(jnp.bfloat16)
    up_thrice = jnp.concatenate([up, up, up], axis=0)
    for slot in range(slot_count):
        zero = jnp.zeros_like(top)
        terms = jnp.concatenate(
            [jnp.where(slot_of == slot, term, zero) for term in (top, mid, low)], axis=1
        )
        expanded = jnp.dot(terms, up_thrice, preferred_element_type=jnp.float32)
        at = pl.ds(slot * rows, rows)
        out_ref[0, at, :] = (base_ref[0, at, :] + adapter_scale_factor * expanded).astype(
            out_ref.dtype
        )


def local(hidden, base_weight, pool_down, pool_up, adapter_home, block_adapter, block_count):
    step_count, row_count, half_width = hidden.shape
    rep_count = lax.axis_size("rep")
    group_count = lax.axis_size("grp")
    rank = pool_up.shape[1]
    col_count = pool_up.shape[2]
    slot_count = block_adapter.shape[1]
    block_rows = row_count // slot_count
    share = col_count // lax.axis_size("tp")
    near = MEMBERS // rep_count
    halves = MEMBERS * PIECE_ROWS // rank
    piece_width = (half_width + share) // halves
    bf16, f32 = jnp.bfloat16, jnp.float32

    down = jnp.swapaxes(pool_down[0], 0, 1)
    pieces = pl.pallas_call(
        functools.partial(pack_kernel, near, halves),
        out_shape=[jax.ShapeDtypeStruct((PIECE_ROWS, piece_width), bf16)] * near,
        in_specs=[ANY, ANY],
        out_specs=[ANY] * near,
        scratch_shapes=[pltpu.SemaphoreType.DMA((2 * near,))],
        name="pack",
    )(down, pool_up[0])

    held = [pieces[0]] + [None] * (group_count - 1)
    for flip in sorted(range(1, group_count), key=lambda f: -f):
        pairs = [(g, g ^ flip) for g in range(group_count)]
        held[flip] = lax.ppermute(pieces[flip % near], "grp", pairs)
    wanted = [block_adapter]
    for flip in range(1, rep_count):
        pairs = [(r, r ^ flip) for r in range(rep_count)]
        wanted.append(lax.ppermute(block_adapter, "rep", pairs))
    if group_count <= MEMBERS:
        held = [piece[None] for piece in held]
    else:
        held = [jnp.stack(held)]

    mine, theirs = pl.pallas_call(
        base_kernel,
        grid=(step_count,),
        out_shape=[jax.ShapeDtypeStruct((step_count, row_count, share), f32)] * 2,
        in_specs=[
            pl.BlockSpec((1, row_count, half_width), lambda s: (s, 0, 0)),
            pl.BlockSpec((half_width, col_count), lambda s: (0, 0)),
        ],
        out_specs=[pl.BlockSpec((1, row_count, share), lambda s: (s, 0, 0))] * 2,
        compiler_params=pltpu.CompilerParams(vmem_limit_bytes=24 << 20),
        cost_estimate=pl.CostEstimate(
            flops=2 * step_count * row_count * half_width * col_count,
            bytes_accessed=2 * step_count * row_count * (half_width + 4 * share),
            transcendentals=0,
        ),
        name="base",
    )(hidden, base_weight)
    swap = [(0, 1), (1, 0)]
    base = mine + lax.ppermute(theirs, "tp", swap)

    sends = pl.pallas_call(
        functools.partial(select_kernel, near, rep_count, len(held)),
        out_shape=[jax.ShapeDtypeStruct((slot_count, PIECE_ROWS, piece_width), bf16)] * MEMBERS,
        in_specs=[SMEM] * (1 + rep_count) + [ANY] * len(held),
        out_specs=[ANY] * MEMBERS,
        scratch_shapes=[pltpu.SemaphoreType.DMA((MEMBERS * slot_count,))],
        name="select",
    )(adapter_home, *wanted, *held)
    got = [sends[0]] + [None] * (MEMBERS - 1)
    for flip in sorted(range(1, MEMBERS), key=lambda f: -f):
        pairs = [
            (r * group_count + g, (r ^ flip // near) * group_count + (g ^ flip % near))
            for r in range(rep_count)
            for g in range(group_count)
        ]
        got[flip] = lax.ppermute(sends[flip], ("rep", "grp"), pairs)

    both = slot_count * rank
    shrunk, up = pl.pallas_call(
        functools.partial(shrink_kernel, MEMBERS, halves, rank),
        grid=(step_count,),
        out_shape=[
            jax.ShapeDtypeStruct((step_count, block_rows, both), f32),
            jax.ShapeDtypeStruct((both, share), bf16),
        ],
        in_specs=[SMEM, pl.BlockSpec((1, row_count, half_width), lambda s: (s, 0, 0))]
        + [pl.BlockSpec((slot_count, PIECE_ROWS, piece_width), lambda s: (0, 0, 0))] * MEMBERS,
        out_specs=[
            pl.BlockSpec((1, block_rows, both), lambda s: (s, 0, 0)),
            pl.BlockSpec((both, share), lambda s: (0, 0)),
        ],
        scratch_shapes=[pltpu.VMEM((both, half_width), bf16)],
        compiler_params=pltpu.CompilerParams(vmem_limit_bytes=24 << 20),
        cost_estimate=pl.CostEstimate(
            flops=2 * step_count * row_count * half_width * both,
            bytes_accessed=2 * step_count * row_count * half_width,
            transcendentals=0,
        ),
        name="shrink",
    )(block_count, hidden, *got)
    shrunk_other = lax.ppermute(shrunk, "tp", swap)

    return pl.pallas_call(
        functools.partial(expand_kernel, slot_count, rank),
        grid=(step_count,),
        out_shape=jax.ShapeDtypeStruct((step_count, row_count, share), bf16),
        in_specs=[
            pl.BlockSpec((1, block_rows, both), lambda s: (s, 0, 0)),
            pl.BlockSpec((1, block_rows, both), lambda s: (s, 0, 0)),
            pl.BlockSpec((both, share), lambda s: (0, 0)),
            pl.BlockSpec((1, row_count, share), lambda s: (s, 0, 0)),
        ],
        out_specs=pl.BlockSpec((1, row_count, share), lambda s: (s, 0, 0)),
        name="expand",
    )(shrunk, shrunk_other, up, base)


def solution(mesh):
    in_specs = (
        P(None, ("rep", "grp"), "tp"),
        P("tp", None),
        P("grp", "tp", None),
        P("grp", None, None),
        P(),
        P("rep", None),
        P("rep"),
    )
    out_specs = P(None, ("rep", "grp"), "tp")
    return jax.shard_map(local, mesh=mesh, in_specs=in_specs, out_specs=out_specs, check_vma=False)
```

time: 122 us -> 110 us (0.902)
  Pallas kernels: 0 us -> 57.1 us
  waiting for transfers between devices: 45.4 us -> 15.1 us
  matrix products: 18.2 us -> 0 us
  between operations: 13.6 us -> 0.17 us
  starting transfers between devices: 14.5 us -> 25.5 us
  blocking collectives: 10.3 us -> 0 us
  other arithmetic: 5.7 us -> 1.05 us
  local copies, waits for them, and re-layouts: 14 us -> 10.6 us
    pallas_call x0 -> x5, Pallas kernels: none -> 57.1 us  [the longest x1 35.8 us: local(): pl.pallas_call(functools.partial(select_kernel, near, rep_count, len(held...]
    all_to_all x3 -> x0, waiting for transfers between devices: 45.4 us -> none  [the longest x1 24.6 us: local(): lax.all_to_all(send_down, 'grp', split_axis=0, concat_axis=2, tiled=True)]
    ppermute x0 -> x17, starting transfers between devices: none -> 25.5 us  [the longest x7 12.1 us: local(): held[flip] = lax.ppermute(pieces[flip % near], 'grp', pairs)]
    dot_general x3 -> x0, matrix products: 18.2 us -> none  [the longest x1 9.48 us: local(): jnp.dot(hidden.reshape(step_count * row_count, half_width), base_weight,...]
    ppermute x0 -> x17, waiting for transfers between devices: none -> 15.1 us  [the longest x7 7.3 us: local(): got[flip] = lax.ppermute(sends[flip], ('rep', 'grp'), pairs)]
    all_to_all x3 -> x0, starting transfers between devices: 14.3 us -> none  [the longest x1 7.28 us: local(): lax.all_to_all(down_parts, 'grp', split_axis=1, concat_axis=0, tiled=True)]
    all_to_all x1 -> x0, blocking collectives: 10.3 us -> none  [local(): lax.all_to_all(up_parts, 'grp', split_axis=1, concat_axis=0, tiled=True)]
    unnamed x16 -> x37, local copies, waits for them, and re-layouts: 4.61 us -> 10.6 us
  transfers between devices with their start and end apart: 5 -> 17, of which waited for: 3 -> 8; matrix products, arithmetic and copies ran while one was open for 12% -> 1% of each run, Pallas kernels for 0% -> 44%
where the time goes in v1:
time: 110 us
  Pallas kernels  57.1 us (52%)
  starting transfers between devices  25.5 us (23%)
  waiting for transfers between devices  15.1 us (14%)
  local copies, waits for them, and re-layouts  10.6 us (10%)
    pallas_call x1, Pallas kernels, local(): pl.pallas_call(functools.partial(select_kernel, near, rep_count, len(held...  35.8 us
    ppermute x7, starting transfers between devices, local(): held[flip] = lax.ppermute(pieces[flip % near], 'grp', pairs)  12.1 us
    ppermute x7, starting transfers between devices, local(): got[flip] = lax.ppermute(sends[flip], ('rep', 'grp'), pairs)  11 us
    unnamed x37, local copies, waits for them, and re-layouts  10.6 us
    pallas_call x1, Pallas kernels, local(): pl.pallas_call(functools.partial(pack_kernel, near, halves), out_shape=[j...  9.61 us
    ppermute x7, waiting for transfers between devices, local(): got[flip] = lax.ppermute(sends[flip], ('rep', 'grp'), pairs)  7.3 us
    ppermute x7, waiting for transfers between devices, local(): held[flip] = lax.ppermute(pieces[flip % near], 'grp', pairs)  5.49 us
    pallas_call x1, Pallas kernels, local(): pl.pallas_call(base_kernel, grid=(step_count,), out_shape=[jax.ShapeDtype...  4.55 us
  transfers between devices with their start and end apart: 17, of which 8 were waited for; matrix products, arithmetic and copies ran while one was open for 1% of the time, Pallas kernels for 44%

profile of v1, /device:TPU:0, one launch (start us, length us, event | category | flops | bytes accessed | tf_op | source)
XLA Modules:
  0.0 109.5 jit_solution(16594615603247707642)
XLA Ops:
  0.0 3.1 %copy-done = bf16[4,224,4096]{2,1,0:T(8,128)(2,1)S(1)} copy-done((bf16[4,224,4096]{2,1,0:T(8,128)(2,1)S(1)}, bf16[4,224,4096]{2,1,0:T(8,128)(2,1)}, u32[]{:S(2)}) %copy-start) | copy-done | bytes 7340056
  3.1 2.2 %copy-done.6 = bf16[4096,512]{1,0:T(8,128)(2,1)S(1)} copy-done((bf16[4096,512]{1,0:T(8,128)(2,1)S(1)}, bf16[4096,512]{1,0:T(8,128)(2,1)}, u32[]{:S(2)}) %copy-start.6) | copy-done | bytes 4194328
  5.3 4.5 %base.1 = (f32[4,224,256]{2,1,0:T(8,128)S(1)}, f32[4,224,256]{2,1,0:T(8,128)S(1)}) custom-call(bf16[4,224,4096]{2,1,0:T(8,128)(2,1)S(1)} %copy-done, bf16[4096,512]{1,0:T(8,128)(2,1)S(1)} %copy-done.6), custom_call_target="tpu_custom_call" | custom-call | flops 3758096384 | bytes 9175040 | tf_op jit(solution)/shard_map/base/pallas_call | solution.py:193
  10.4 9.6 %pack.1 = (bf16[16,2176]{1,0:T(8,128)(2,1)}, bf16[16,2176]{1,0:T(8,128)(2,1)}, bf16[16,2176]{1,0:T(8,128)(2,1)}, bf16[16,2176]{1,0:T(8,128)(2,1)}) custom-call(bf16[64,4096]{1,0:T(8,128)(2,1)} %bitcast.12, bf16[64,512]{1,0:T(8,128)(2,1)} %bitcast.21), custom_call_target="tpu_custom_call" | custom-call | tf_op jit(solution)/shard_map/pack/pallas_call | solution.py:171
  20.0 3.6 %collective-permute-start.4 = (bf16[16,2176]{1,0:T(8,128)(2,1)}, bf16[16,2176]{1,0:T(8,128)(2,1)S(1)}, u32[]{:S(2)}, u32[]{:S(2)}) collective-permute-start(bf16[16,2176]{1,0:T(8,128)(2,1)} %get-tuple-element.21), channel_id=1, source_target_pairs={{0,8},{2,10},{4,12},{6,14},{8,0},{10,2},{12,4},{14,6},{1,9},{3,11}... | collective-permute-start | bytes 208904 | tf_op jit(solution)/shard_map/ppermute | solution.py:183
  23.7 1.3 %collective-permute-start.5 = (bf16[16,2176]{1,0:T(8,128)(2,1)}, bf16[16,2176]{1,0:T(8,128)(2,1)S(1)}, u32[]{:S(2)}, u32[]{:S(2)}) collective-permute-start(bf16[16,2176]{1,0:T(8,128)(2,1)} %get-tuple-element.22), channel_id=1, source_target_pairs={{0,10},{2,8},{4,14},{6,12},{8,2},{10,0},{12,6},{14,4},{1,11},{3,9}... | collective-permute-start | bytes 208904 | tf_op jit(solution)/shard_map/ppermute | solution.py:183
  25.3 1.7 %collective-permute-start = (s32[8,2]{1,0:T(8,128)S(1)}, s32[8,2]{1,0:T(8,128)S(1)}, u32[]{:S(2)}, u32[]{:S(2)}) collective-permute-start(s32[8,2]{1,0:T(8,128)S(1)} %copy.9.refs_0_), channel_id=1, source_target_pairs={{0,16},{16,0},{1,17},{17,1},{2,18},{18,2},{3,19},{19,3},{4,20},{20... | collective-permute-start | bytes 200 | tf_op jit(solution)/shard_map/ppermute | solution.py:187
  27.0 1.9 %collective-permute-done.refs_1_ = s32[8,2]{1,0:T(8,128)S(1)} collective-permute-done((s32[8,2]{1,0:T(8,128)S(1)}, s32[8,2]{1,0:T(8,128)S(1)}, u32[]{:S(2)}, u32[]{:S(2)}) %collective-permute-start) | collective-permute-done | bytes 96 | tf_op jit(solution)/shard_map/ppermute | solution.py:187
  28.9 3.9 %collective-permute-start.6 = (bf16[16,2176]{1,0:T(8,128)(2,1)}, bf16[16,2176]{1,0:T(8,128)(2,1)S(1)}, u32[]{:S(2)}, u32[]{:S(2)}) collective-permute-start(bf16[16,2176]{1,0:T(8,128)(2,1)} %get-tuple-element.23), channel_id=1, source_target_pairs={{0,12},{2,14},{4,8},{6,10},{8,4},{10,6},{12,0},{14,2},{1,13},{3,15... | collective-permute-start | bytes 208904 | tf_op jit(solution)/shard_map/ppermute | solution.py:183
  32.8 2.9 %collective-permute-start.7 = (bf16[16,2176]{1,0:T(8,128)(2,1)}, bf16[16,2176]{1,0:T(8,128)(2,1)S(1)}, u32[]{:S(2)}, u32[]{:S(2)}) collective-permute-start(bf16[16,2176]{1,0:T(8,128)(2,1)} %get-tuple-element.24), channel_id=1, source_target_pairs={{0,14},{2,12},{4,10},{6,8},{8,6},{10,4},{12,2},{14,0},{1,15},{3,13... | collective-permute-start | bytes 208904 | tf_op jit(solution)/shard_map/ppermute | solution.py:183
  35.8 2.2 %collective-permute-done.2 = bf16[16,2176]{1,0:T(8,128)(2,1)S(1)} collective-permute-done((bf16[16,2176]{1,0:T(8,128)(2,1)}, bf16[16,2176]{1,0:T(8,128)(2,1)S(1)}, u32[]{:S(2)}, u32[]{:S(2)}) %collective-permute-start.2) | collective-permute-done | bytes 69664 | tf_op jit(solution)/shard_map/ppermute | solution.py:183
  38.0 2.1 %collective-permute-done.7 = bf16[16,2176]{1,0:T(8,128)(2,1)S(1)} collective-permute-done((bf16[16,2176]{1,0:T(8,128)(2,1)}, bf16[16,2176]{1,0:T(8,128)(2,1)S(1)}, u32[]{:S(2)}, u32[]{:S(2)}) %collective-permute-start.7) | collective-permute-done | bytes 69664 | tf_op jit(solution)/shard_map/ppermute | solution.py:183
  40.2 1.2 %collective-permute-done.3 = bf16[16,2176]{1,0:T(8,128)(2,1)S(1)} collective-permute-done((bf16[16,2176]{1,0:T(8,128)(2,1)}, bf16[16,2176]{1,0:T(8,128)(2,1)S(1)}, u32[]{:S(2)}, u32[]{:S(2)}) %collective-permute-start.3) | collective-permute-done | bytes 69664 | tf_op jit(solution)/shard_map/ppermute | solution.py:183
  42.0 35.8 %select.1 = (bf16[2,16,2176]{2,1,0:T(8,128)(2,1)}, bf16[2,16,2176]{2,1,0:T(8,128)(2,1)}, bf16[2,16,2176]{2,1,0:T(8,128)(2,1)}, bf16[2,16,2176]{2,1,0:T(8,128)(2,...) custom-call(s32[8]{0:T(128)} %home_ref.1, ...), custom_call_target="tpu_custom_call" | custom-call | tf_op jit(solution)/shard_map/select/pallas_call | solution.py:213
  77.8 1.6 %collective-permute-start.8 = (bf16[2,16,2176]{2,1,0:T(8,128)(2,1)}, bf16[2,16,2176]{2,1,0:T(8,128)(2,1)S(1)}, u32[]{:S(2)}, u32[]{:S(2)}) collective-permute-start(bf16[2,16,2176]{2,1,0:T(8,128)(2,1)} %get-tuple-element.26), channel_id=1, source_target_pairs={{0,2},{2,0},{4,6},{6,4},{8,10},{10,8},{12,14},{14,12},{16,18},{18,... | collective-permute-start | bytes 417800 | tf_op jit(solution)/shard_map/ppermute | solution.py:228
  79.7 1.7 %collective-permute-start.10 = (bf16[2,16,2176]{2,1,0:T(8,128)(2,1)}, bf16[2,16,2176]{2,1,0:T(8,128)(2,1)S(1)}, u32[]{:S(2)}, u32[]{:S(2)}) collective-permute-start(bf16[2,16,2176]{2,1,0:T(8,128)(2,1)} %get-tuple-element.28), channel_id=1, source_target_pairs={{0,6},{2,4},{4,2},{6,0},{8,14},{10,12},{12,10},{14,8},{16,22},{18,... | collective-permute-start | bytes 417800 | tf_op jit(solution)/shard_map/ppermute | solution.py:228
  81.3 1.5 %collective-permute-start.11 = (bf16[2,16,2176]{2,1,0:T(8,128)(2,1)}, bf16[2,16,2176]{2,1,0:T(8,128)(2,1)S(1)}, u32[]{:S(2)}, u32[]{:S(2)}) collective-permute-start(bf16[2,16,2176]{2,1,0:T(8,128)(2,1)} %get-tuple-element.29), channel_id=1, source_target_pairs={{0,16},{2,18},{4,20},{6,22},{8,24},{10,26},{12,28},{14,30},{16,0},... | collective-permute-start | bytes 417800 | tf_op jit(solution)/shard_map/ppermute | solution.py:228
  83.8 2.4 %collective-permute-start.12 = (bf16[2,16,2176]{2,1,0:T(8,128)(2,1)}, bf16[2,16,2176]{2,1,0:T(8,128)(2,1)S(1)}, u32[]{:S(2)}, u32[]{:S(2)}) collective-permute-start(bf16[2,16,2176]{2,1,0:T(8,128)(2,1)} %get-tuple-element.30), channel_id=1, source_target_pairs={{0,18},{2,16},{4,22},{6,20},{8,26},{10,24},{12,30},{14,28},{16,2},... | collective-permute-start | bytes 417800 | tf_op jit(solution)/shard_map/ppermute | solution.py:228
  87.2 1.3 %collective-permute-done.10.refs_3_ = bf16[2,16,2176]{2,1,0:T(8,128)(2,1)S(1)} collective-permute-done((bf16[2,16,2176]{2,1,0:T(8,128)(2,1)}, bf16[2,16,2176]{2,1,0:T(8,128)(2,1)S(1)}, u32[]{:S(2)}, u32[]{:S(2)}) %collective-permute-start.10) | collective-permute-done | bytes 139296 | tf_op jit(solution)/shard_map/ppermute | solution.py:228
  88.5 2.6 %collective-permute-start.14 = (bf16[2,16,2176]{2,1,0:T(8,128)(2,1)}, bf16[2,16,2176]{2,1,0:T(8,128)(2,1)S(1)}, u32[]{:S(2)}, u32[]{:S(2)}) collective-permute-start(bf16[2,16,2176]{2,1,0:T(8,128)(2,1)} %get-tuple-element.32), channel_id=1, source_target_pairs={{0,22},{2,20},{4,18},{6,16},{8,30},{10,28},{12,26},{14,24},{16,6},... | collective-permute-start | bytes 417800 | tf_op jit(solution)/shard_map/ppermute | solution.py:228
  91.0 5.1 %collective-permute-done.12.refs_5_ = bf16[2,16,2176]{2,1,0:T(8,128)(2,1)S(1)} collective-permute-done((bf16[2,16,2176]{2,1,0:T(8,128)(2,1)}, bf16[2,16,2176]{2,1,0:T(8,128)(2,1)S(1)}, u32[]{:S(2)}, u32[]{:S(2)}) %collective-permute-start.12) | collective-permute-done | bytes 139296 | tf_op jit(solution)/shard_map/ppermute | solution.py:228
  96.1 3.1 %copy-done.1 = bf16[4,224,4096]{2,1,0:T(8,128)(2,1)S(1)} copy-done((bf16[4,224,4096]{2,1,0:T(8,128)(2,1)S(1)}, bf16[4,224,4096]{2,1,0:T(8,128)(2,1)}, u32[]{:S(2)}) %copy-start.1) | copy-done | bytes 7340056
  100.1 3.3 %shrink.1 = (f32[4,112,128]{2,1,0:T(8,128)S(1)}, bf16[128,256]{1,0:T(8,128)(2,1)S(1)}) custom-call(s32[8]{0:T(128)S(1)} %copy-done.5, bf16[4,224,4096]{2,1,0:T(8,128)(2,1)S(1)} %copy-done.1, bf16[2,16,2176]{2,1,0:T(8,128)(2,1)S(1)} %copy-done.3, bf16[2,16,2176]{2,1,0:T(8,128)(2,1)S(1)} %collective-permute-done.8.refs_1_, ...), custom_call_target="tpu_custom_call" | custom-call | flops 939524096 | bytes 7340032 | tf_op jit(solution)/shard_map/shrink/pallas_call | solution.py:231
  105.7 3.8 %expand.1 = bf16[4,224,256]{2,1,0:T(8,128)(2,1)} custom-call(f32[4,112,128]{2,1,0:T(8,128)} %copy-done.2, f32[4,112,128]{2,1,0:T(8,128)} %copy-done.7, bf16[128,256]{1,0:T(8,128)(2,1)} %copy-done.4, f32[4,224,256]{2,1,0:T(8,128)} %add.3.base_ref), custom_call_target="tpu_custom_call" | custom-call | tf_op jit(solution)/shard_map/expand/pallas_call | solution.py:255
  (53 shorter events, 7.1 us)
Async XLA Ops:
  5.3 19.9 %copy-start.17 = (s32[8,2]{0,1:T(2,128)S(1)}, s32[8,2]{0,1:T(2,128)}, u32[]{:S(2)}) copy-start(s32[8,2]{0,1:T(2,128)} %param.12) | copy-start | bytes 196
  5.3 90.8 %copy-start.5 = (s32[8]{0:T(128)S(1)}, s32[8]{0:T(128)}, u32[]{:S(2)}) copy-start(s32[8]{0:T(128)} %count_ref.1) | copy-start | bytes 100
  9.8 93.7 %collective-permute-start.16 = (f32[4,224,256]{2,1,0:T(8,128)S(1)}, f32[4,224,256]{2,1,0:T(8,128)S(1)}, u32[]{:S(2)}, u32[]{:S(2)}) collective-permute-start(f32[4,224,256]{2,1,0:T(8,128)S(1)} %get-tuple-element.36), channel_id=1, source_target_pairs={{0,1},{1,0},{2,3},{3,2},{4,5},{5,4},{6,7},{7,6},{8,9},{9,8},{10,11... | collective-permute-start | bytes 2752520 | tf_op jit(solution)/shard_map/ppermute | solution.py:211
  20.0 12.7 %collective-permute-start.4 = (bf16[16,2176]{1,0:T(8,128)(2,1)}, bf16[16,2176]{1,0:T(8,128)(2,1)S(1)}, u32[]{:S(2)}, u32[]{:S(2)}) collective-permute-start(bf16[16,2176]{1,0:T(8,128)(2,1)} %get-tuple-element.21), channel_id=1, source_target_pairs={{0,8},{2,10},{4,12},{6,14},{8,0},{10,2},{12,4},{14,6},{1,9},{3,11}... | collective-permute-start | bytes 208904 | tf_op jit(solution)/shard_map/ppermute | solution.py:183
  23.7 9.1 %collective-permute-start.5 = (bf16[16,2176]{1,0:T(8,128)(2,1)}, bf16[16,2176]{1,0:T(8,128)(2,1)S(1)}, u32[]{:S(2)}, u32[]{:S(2)}) collective-permute-start(bf16[16,2176]{1,0:T(8,128)(2,1)} %get-tuple-element.22), channel_id=1, source_target_pairs={{0,10},{2,8},{4,14},{6,12},{8,2},{10,0},{12,6},{14,4},{1,11},{3,9}... | collective-permute-start | bytes 208904 | tf_op jit(solution)/shard_map/ppermute | solution.py:183
  24.9 10.7 %collective-permute-start.1 = (bf16[16,2176]{1,0:T(8,128)(2,1)}, bf16[16,2176]{1,0:T(8,128)(2,1)S(1)}, u32[]{:S(2)}, u32[]{:S(2)}) collective-permute-start(bf16[16,2176]{1,0:T(8,128)(2,1)} %get-tuple-element.22), channel_id=1, source_target_pairs={{0,2},{2,0},{4,6},{6,4},{8,10},{10,8},{12,14},{14,12},{1,3},{3,1},... | collective-permute-start | bytes 208904 | tf_op jit(solution)/shard_map/ppermute | solution.py:183
  25.3 16.1 %copy-start.15 = (s32[8,2]{1,0:T(8,128)}, s32[8,2]{1,0:T(8,128)S(1)}, u32[]{:S(2)}) copy-start(s32[8,2]{1,0:T(8,128)S(1)} %copy.9.refs_0_) | copy-start | bytes 196
  25.3 3.6 %collective-permute-start = (s32[8,2]{1,0:T(8,128)S(1)}, s32[8,2]{1,0:T(8,128)S(1)}, u32[]{:S(2)}, u32[]{:S(2)}) collective-permute-start(s32[8,2]{1,0:T(8,128)S(1)} %copy.9.refs_0_), channel_id=1, source_target_pairs={{0,16},{16,0},{1,17},{17,1},{2,18},{18,2},{3,19},{19,3},{4,20},{20... | collective-permute-start | bytes 200 | tf_op jit(solution)/shard_map/ppermute | solution.py:187
  28.9 12.4 %copy-start.16 = (s32[8,2]{1,0:T(8,128)}, s32[8,2]{1,0:T(8,128)S(1)}, u32[]{:S(2)}) copy-start(s32[8,2]{1,0:T(8,128)S(1)} %collective-permute-done.refs_1_) | copy-start | bytes 196
  28.9 6.9 %collective-permute-start.6 = (bf16[16,2176]{1,0:T(8,128)(2,1)}, bf16[16,2176]{1,0:T(8,128)(2,1)S(1)}, u32[]{:S(2)}, u32[]{:S(2)}) collective-permute-start(bf16[16,2176]{1,0:T(8,128)(2,1)} %get-tuple-element.23), channel_id=1, source_target_pairs={{0,12},{2,14},{4,8},{6,10},{8,4},{10,6},{12,0},{14,2},{1,13},{3,15... | collective-permute-start | bytes 208904 | tf_op jit(solution)/shard_map/ppermute | solution.py:183
  32.8 8.6 %copy-start.8 = (bf16[16,2176]{1,0:T(8,128)(2,1)}, bf16[16,2176]{1,0:T(8,128)(2,1)S(1)}, u32[]{:S(2)}) copy-start(bf16[16,2176]{1,0:T(8,128)(2,1)S(1)} %collective-permute-done.4) | copy-start | bytes 208900
  32.8 5.3 %collective-permute-start.2 = (bf16[16,2176]{1,0:T(8,128)(2,1)}, bf16[16,2176]{1,0:T(8,128)(2,1)S(1)}, u32[]{:S(2)}, u32[]{:S(2)}) collective-permute-start(bf16[16,2176]{1,0:T(8,128)(2,1)} %get-tuple-element.23), channel_id=1, source_target_pairs={{0,4},{2,6},{4,0},{6,2},{8,12},{10,14},{12,8},{14,10},{1,5},{3,7},... | collective-permute-start | bytes 208904 | tf_op jit(solution)/shard_map/ppermute | solution.py:183
  32.8 8.6 %copy-start.9 = (bf16[16,2176]{1,0:T(8,128)(2,1)}, bf16[16,2176]{1,0:T(8,128)(2,1)S(1)}, u32[]{:S(2)}) copy-start(bf16[16,2176]{1,0:T(8,128)(2,1)S(1)} %collective-permute-done.5) | copy-start | bytes 208900
  32.8 7.4 %collective-permute-start.7 = (bf16[16,2176]{1,0:T(8,128)(2,1)}, bf16[16,2176]{1,0:T(8,128)(2,1)S(1)}, u32[]{:S(2)}, u32[]{:S(2)}) collective-permute-start(bf16[16,2176]{1,0:T(8,128)(2,1)} %get-tuple-element.24), channel_id=1, source_target_pairs={{0,14},{2,12},{4,10},{6,8},{8,6},{10,4},{12,2},{14,0},{1,15},{3,13... | collective-permute-start | bytes 208904 | tf_op jit(solution)/shard_map/ppermute | solution.py:183
  35.6 5.7 %copy-start.10 = (bf16[16,2176]{1,0:T(8,128)(2,1)}, bf16[16,2176]{1,0:T(8,128)(2,1)S(1)}, u32[]{:S(2)}) copy-start(bf16[16,2176]{1,0:T(8,128)(2,1)S(1)} %collective-permute-done.1) | copy-start | bytes 208900
  35.6 5.7 %collective-permute-start.3 = (bf16[16,2176]{1,0:T(8,128)(2,1)}, bf16[16,2176]{1,0:T(8,128)(2,1)S(1)}, u32[]{:S(2)}, u32[]{:S(2)}) collective-permute-start(bf16[16,2176]{1,0:T(8,128)(2,1)} %get-tuple-element.24), channel_id=1, source_target_pairs={{0,6},{2,4},{4,2},{6,0},{8,14},{10,12},{12,10},{14,8},{1,7},{3,5},... | collective-permute-start | bytes 208904 | tf_op jit(solution)/shard_map/ppermute | solution.py:183
  77.8 6.0 %collective-permute-start.8 = (bf16[2,16,2176]{2,1,0:T(8,128)(2,1)}, bf16[2,16,2176]{2,1,0:T(8,128)(2,1)S(1)}, u32[]{:S(2)}, u32[]{:S(2)}) collective-permute-start(bf16[2,16,2176]{2,1,0:T(8,128)(2,1)} %get-tuple-element.26), channel_id=1, source_target_pairs={{0,2},{2,0},{4,6},{6,4},{8,10},{10,8},{12,14},{14,12},{16,18},{18,... | collective-permute-start | bytes 417800 | tf_op jit(solution)/shard_map/ppermute | solution.py:228
  79.4 6.8 %collective-permute-start.9 = (bf16[2,16,2176]{2,1,0:T(8,128)(2,1)}, bf16[2,16,2176]{2,1,0:T(8,128)(2,1)S(1)}, u32[]{:S(2)}, u32[]{:S(2)}) collective-permute-start(bf16[2,16,2176]{2,1,0:T(8,128)(2,1)} %get-tuple-element.27), channel_id=1, source_target_pairs={{0,4},{2,6},{4,0},{6,2},{8,12},{10,14},{12,8},{14,10},{16,20},{18,... | collective-permute-start | bytes 417800 | tf_op jit(solution)/shard_map/ppermute | solution.py:228
  79.7 8.8 %collective-permute-start.10 = (bf16[2,16,2176]{2,1,0:T(8,128)(2,1)}, bf16[2,16,2176]{2,1,0:T(8,128)(2,1)S(1)}, u32[]{:S(2)}, u32[]{:S(2)}) collective-permute-start(bf16[2,16,2176]{2,1,0:T(8,128)(2,1)} %get-tuple-element.28), channel_id=1, source_target_pairs={{0,6},{2,4},{4,2},{6,0},{8,14},{10,12},{12,10},{14,8},{16,22},{18,... | collective-permute-start | bytes 417800 | tf_op jit(solution)/shard_map/ppermute | solution.py:228
  81.3 9.7 %collective-permute-start.11 = (bf16[2,16,2176]{2,1,0:T(8,128)(2,1)}, bf16[2,16,2176]{2,1,0:T(8,128)(2,1)S(1)}, u32[]{:S(2)}, u32[]{:S(2)}) collective-permute-start(bf16[2,16,2176]{2,1,0:T(8,128)(2,1)} %get-tuple-element.29), channel_id=1, source_target_pairs={{0,16},{2,18},{4,20},{6,22},{8,24},{10,26},{12,28},{14,30},{16,0},... | collective-permute-start | bytes 417800 | tf_op jit(solution)/shard_map/ppermute | solution.py:228
  83.8 12.3 %collective-permute-start.12 = (bf16[2,16,2176]{2,1,0:T(8,128)(2,1)}, bf16[2,16,2176]{2,1,0:T(8,128)(2,1)S(1)}, u32[]{:S(2)}, u32[]{:S(2)}) collective-permute-start(bf16[2,16,2176]{2,1,0:T(8,128)(2,1)} %get-tuple-element.30), channel_id=1, source_target_pairs={{0,18},{2,16},{4,22},{6,20},{8,26},{10,24},{12,30},{14,28},{16,2},... | collective-permute-start | bytes 417800 | tf_op jit(solution)/shard_map/ppermute | solution.py:228
  86.2 9.9 %collective-permute-start.13 = (bf16[2,16,2176]{2,1,0:T(8,128)(2,1)}, bf16[2,16,2176]{2,1,0:T(8,128)(2,1)S(1)}, u32[]{:S(2)}, u32[]{:S(2)}) collective-permute-start(bf16[2,16,2176]{2,1,0:T(8,128)(2,1)} %get-tuple-element.31), channel_id=1, source_target_pairs={{0,20},{2,22},{4,16},{6,18},{8,28},{10,30},{12,24},{14,26},{16,4},... | collective-permute-start | bytes 417800 | tf_op jit(solution)/shard_map/ppermute | solution.py:228
  88.5 7.6 %collective-permute-start.14 = (bf16[2,16,2176]{2,1,0:T(8,128)(2,1)}, bf16[2,16,2176]{2,1,0:T(8,128)(2,1)S(1)}, u32[]{:S(2)}, u32[]{:S(2)}) collective-permute-start(bf16[2,16,2176]{2,1,0:T(8,128)(2,1)} %get-tuple-element.32), channel_id=1, source_target_pairs={{0,22},{2,20},{4,18},{6,16},{8,30},{10,28},{12,26},{14,24},{16,6},... | collective-permute-start | bytes 417800 | tf_op jit(solution)/shard_map/ppermute | solution.py:228
  103.4 1.6 %collective-permute-start.15 = (f32[4,112,128]{2,1,0:T(8,128)S(1)}, f32[4,112,128]{2,1,0:T(8,128)S(1)}, u32[]{:S(2)}, u32[]{:S(2)}) collective-permute-start(f32[4,112,128]{2,1,0:T(8,128)S(1)} %get-tuple-element.33.mine_ref), channel_id=1, source_target_pairs={{0,1},{1,0},{2,3},{3,2},{4,5},{5,4},{6,7},{7,6},{8,9},{9,8},{10,11... | collective-permute-start | bytes 688136 | tf_op jit(solution)/shard_map/ppermute | solution.py:253
  (11 other events, 23.8 us)

commit v2 on v1

v2 whole, which is shorter than its diff:
```python
import functools

import jax
import jax.numpy as jnp
from jax import lax
from jax.experimental import pallas as pl
from jax.experimental.pallas import tpu as pltpu
from jax.sharding import PartitionSpec as P

adapter_scale_factor = 0.5
MEMBERS = 8
PIECE_ROWS = 16

ANY = pl.BlockSpec(memory_space=pl.ANY)
SMEM = pl.BlockSpec(memory_space=pltpu.SMEM)
VMEM = pl.BlockSpec(memory_space=pltpu.VMEM)


def pack_kernel(near, halves, down_ref, up_ref, *outs):
    member_base = lax.axis_index("rep") * near
    low = lax.rem(lax.axis_index("grp"), near)
    tp_index = lax.axis_index("tp")
    wide = down_ref.shape[1] // halves
    up_own = up_ref.shape[1] // lax.axis_size("tp")
    up_wide = up_own // halves
    for flip in range(near):
        member = member_base + (low ^ flip)
        rows = pl.ds(pl.multiple_of(member // halves * PIECE_ROWS, PIECE_ROWS), PIECE_ROWS)
        half = lax.rem(member, halves)
        outs[flip][:, :wide] = down_ref[rows, pl.ds(pl.multiple_of(half * wide, 128), wide)]
        outs[flip][:, wide:] = up_ref[
            rows, pl.ds(pl.multiple_of(tp_index * up_own + half * up_wide, 128), up_wide)
        ]


def select_kernel(near, rep_count, part_count, home_ref, *refs):
    wanted, refs = refs[:rep_count], refs[rep_count:]
    held, refs = refs[:part_count], refs[part_count:]
    outs = refs[: near * rep_count]
    group_index = lax.axis_index("grp")
    slot_count = outs[0].shape[0]
    pool_size = home_ref.shape[0]
    if part_count == 1:
        stack = held[0]
    else:
        stack = refs[near * rep_count]
        for part in range(part_count):
            stack[part] = held[part][...]
    for flip in range(near * rep_count):
        other = group_index ^ (flip % near)
        for slot in range(slot_count):
            adapter = jnp.clip(wanted[flip // near][other, slot], 0, pool_size - 1)
            place = jnp.clip(home_ref[adapter], 0, pool_size - 1) ^ group_index
            outs[flip][slot] = stack[place]


def base_kernel(x_ref, weight_ref, mine_ref, theirs_ref):
    share = mine_ref.shape[2]
    tp_index = lax.axis_index("tp")
    for step in range(x_ref.shape[0]):
        product = jnp.dot(x_ref[step], weight_ref[...], preferred_element_type=jnp.float32)

        @pl.when(tp_index == 0)
        def _():
            mine_ref[step] = product[:, :share]
            theirs_ref[step] = product[:, share:]

        @pl.when(tp_index == 1)
        def _():
            mine_ref[step] = product[:, share:]
            theirs_ref[step] = product[:, :share]


def shrink_kernel(member_count, halves, rank, count_ref, x_ref, *refs):
    pieces, refs = refs[:member_count], refs[member_count:]
    shrunk_ref, up_ref, down = refs
    slot_count = pieces[0].shape[0]
    wide = down.shape[1] // halves
    up_wide = up_ref.shape[1] // halves
    group_index = lax.axis_index("grp")
    for flip in range(member_count):
        half = lax.rem(group_index ^ flip, halves)
        for slot in range(slot_count):
            rows = pl.ds(slot * rank + flip // halves * PIECE_ROWS, PIECE_ROWS)
            down[rows, pl.ds(pl.multiple_of(half * wide, 128), wide)] = pieces[flip][slot, :, :wide]
            up_ref[rows, pl.ds(pl.multiple_of(half * up_wide, 128), up_wide)] = pieces[flip][
                slot, :, wide:
            ]
    rows = shrunk_ref.shape[1]
    slot_of = lax.broadcasted_iota(jnp.int32, shrunk_ref.shape[1:], 1) // rank
    live_count = count_ref[group_index]
    for step in range(x_ref.shape[0]):
        product = lax.dot_general(
            x_ref[step], down[...], (((1,), (1,)), ((), ())), preferred_element_type=jnp.float32
        )
        packed = jnp.zeros(shrunk_ref.shape[1:], jnp.float32)
        for slot in range(slot_count):
            keep = (slot_of == slot) & (slot < live_count)
            packed = jnp.where(keep, product[slot * rows : (slot + 1) * rows], packed)
        shrunk_ref[step] = packed


def expand_kernel(
    slot_count, rank, mine_ref, theirs_ref, up_ref, base_ref, base_other_ref, out_ref, done, sem
):
    rows = mine_ref.shape[1]
    slot_of = lax.broadcasted_iota(jnp.int32, mine_ref.shape[1:], 1) // rank
    up = up_ref[...]
    up_thrice = jnp.concatenate([up, up, up], axis=0)
    for step in range(mine_ref.shape[0]):
        shrunk = mine_ref[step] + theirs_ref[step]
        top = shrunk.astype(jnp.bfloat16)
        rest = shrunk - top.astype(jnp.float32)
        mid = rest.astype(jnp.bfloat16)
        low = (rest - mid.astype(jnp.float32)).astype(jnp.bfloat16)
        zero = jnp.zeros_like(top)
        for slot in range(slot_count):
            terms = jnp.concatenate(
                [jnp.where(slot_of == slot, term, zero) for term in (top, mid, low)], axis=1
            )
            expanded = jnp.dot(terms, up_thrice, preferred_element_type=jnp.float32)
            at = pl.ds(slot * rows, rows)
            total = base_ref[step, at, :] + base_other_ref[step, at, :]
            done[step, at, :] = (total + adapter_scale_factor * expanded).astype(done.dtype)
        pltpu.make_async_copy(done.at[step], out_ref.at[step], sem.at[step]).start()
    for step in range(mine_ref.shape[0]):
        pltpu.make_async_copy(done.at[step], out_ref.at[step], sem.at[step]).wait()


def local(hidden, base_weight, pool_down, pool_up, adapter_home, block_adapter, block_count):
    step_count, row_count, half_width = hidden.shape
    rep_count = lax.axis_size("rep")
    group_count = lax.axis_size("grp")
    rank = pool_up.shape[1]
    col_count = pool_up.shape[2]
    slot_count = block_adapter.shape[1]
    block_rows = row_count // slot_count
    share = col_count // lax.axis_size("tp")
    near = MEMBERS // rep_count
    halves = MEMBERS * PIECE_ROWS // rank
    piece_width = (half_width + share) // halves
    bf16, f32 = jnp.bfloat16, jnp.float32

    down = jnp.swapaxes(pool_down[0], 0, 1)
    pieces = pl.pallas_call(
        functools.partial(pack_kernel, near, halves),
        out_shape=[jax.ShapeDtypeStruct((PIECE_ROWS, piece_width), bf16)] * near,
        in_specs=[VMEM, VMEM],
        out_specs=[VMEM] * near,
        name="pack",
    )(down, pool_up[0])

    held = [pieces[0]] + [None] * (group_count - 1)
    for flip in range(group_count - 1, 0, -1):
        pairs = [(g, g ^ flip) for g in range(group_count)]
        held[flip] = lax.ppermute(pieces[flip % near], "grp", pairs)
    wanted = [block_adapter]
    for flip in range(1, rep_count):
        pairs = [(r, r ^ flip) for r in range(rep_count)]
        wanted.append(lax.ppermute(block_adapter, "rep", pairs))

    mine, theirs = pl.pallas_call(
        base_kernel,
        out_shape=[jax.ShapeDtypeStruct((step_count, row_count, share), f32)] * 2,
        in_specs=[VMEM, VMEM],
        out_specs=[VMEM, VMEM],
        compiler_params=pltpu.CompilerParams(vmem_limit_bytes=24 << 20),
        cost_estimate=pl.CostEstimate(
            flops=2 * step_count * row_count * half_width * col_count,
            bytes_accessed=2 * step_count * row_count * (half_width + 4 * share),
            transcendentals=0,
        ),
        name="base",
    )(hidden, base_weight)
    held[1:], wanted[1:], mine, theirs = lax.optimization_barrier(
        (held[1:], wanted[1:], mine, theirs)
    )

    if group_count <= MEMBERS:
        parts = held
        stack = [pltpu.VMEM((group_count, PIECE_ROWS, piece_width), bf16)]
    else:
        parts, stack = [jnp.stack(held)], []
    sends = pl.pallas_call(
        functools.partial(select_kernel, near, rep_count, len(parts)),
        out_shape=[jax.ShapeDtypeStruct((slot_count, PIECE_ROWS, piece_width), bf16)] * MEMBERS,
        in_specs=[SMEM] * (1 + rep_count) + [VMEM] * len(parts),
        out_specs=[VMEM] * MEMBERS,
        scratch_shapes=stack,
        compiler_params=pltpu.CompilerParams(vmem_limit_bytes=24 << 20),
        name="select",
    )(adapter_home, *wanted, *parts)
    swap = [(0, 1), (1, 0)]
    theirs, sends = lax.optimization_barrier((theirs, sends))
    base_other = lax.ppermute(theirs, "tp", swap)
    got = [sends[0]] + [None] * (MEMBERS - 1)
    for flip in range(MEMBERS - 1, 0, -1):
        pairs = [
            (r * group_count + g, (r ^ flip // near) * group_count + (g ^ flip % near))
            for r in range(rep_count)
            for g in range(group_count)
        ]
        got[flip] = lax.ppermute(sends[flip], ("rep", "grp"), pairs)

    both = slot_count * rank
    shrunk, up = pl.pallas_call(
        functools.partial(shrink_kernel, MEMBERS, halves, rank),
        out_shape=[
            jax.ShapeDtypeStruct((step_count, block_rows, both), f32),
            jax.ShapeDtypeStruct((both, share), bf16),
        ],
        in_specs=[SMEM] + [VMEM] * (1 + MEMBERS),
        out_specs=[VMEM, VMEM],
        scratch_shapes=[pltpu.VMEM((both, half_width), bf16)],
        compiler_params=pltpu.CompilerParams(vmem_limit_bytes=24 << 20),
        cost_estimate=pl.CostEstimate(
            flops=2 * step_count * row_count * half_width * both,
            bytes_accessed=2 * step_count * row_count * half_width,
            transcendentals=0,
        ),
        name="shrink",
    )(block_count, hidden, *got)
    shrunk_other = lax.ppermute(shrunk, "tp", swap)

    return pl.pallas_call(
        functools.partial(expand_kernel, slot_count, rank),
        out_shape=jax.ShapeDtypeStruct((step_count, row_count, share), bf16),
        in_specs=[VMEM] * 5,
        out_specs=ANY,
        scratch_shapes=[
            pltpu.VMEM((step_count, row_count, share), bf16),
            pltpu.SemaphoreType.DMA((step_count,)),
        ],
        compiler_params=pltpu.CompilerParams(vmem_limit_bytes=24 << 20),
        name="expand",
    )(shrunk, shrunk_other, up, mine, base_other)


def solution(mesh):
    in_specs = (
        P(None, ("rep", "grp"), "tp"),
        P("tp", None),
        P("grp", "tp", None),
        P("grp", None, None),
        P(),
        P("rep", None),
        P("rep"),
    )
    out_specs = P(None, ("rep", "grp"), "tp")
    return jax.shard_map(local, mesh=mesh, in_specs=in_specs, out_specs=out_specs, check_vma=False)
```

time: 110 us -> 52.2 us (0.47)
  Pallas kernels: 57.1 us -> 10.8 us
  waiting for transfers between devices: 15.1 us -> 9.32 us
  local copies, waits for them, and re-layouts: 10.6 us -> 6.04 us
    pallas_call x4, Pallas kernels: 47.5 us -> 9.07 us  [the longest x1 4.5 us: local(): pl.pallas_call(base_kernel, out_shape=[jax.ShapeDtypeStruct((step_count,...]
    pallas_call x1, Pallas kernels: 9.61 us -> 1.78 us  [local(): pl.pallas_call(functools.partial(pack_kernel, near, halves), out_shape=[j...]
    ppermute x7, waiting for transfers between devices: 5.49 us -> 0.02 us  [local(): held[flip] = lax.ppermute(pieces[flip % near], 'grp', pairs)]
    unnamed x37 -> x13, local copies, waits for them, and re-layouts: 10.6 us -> 6.04 us
    ppermute x1, waiting for transfers between devices: 1.86 us -> 0.54 us  [local(): wanted.append(lax.ppermute(block_adapter, 'rep', pairs))]
  transfers between devices with their start and end apart: 17 -> 17, of which waited for: 8 -> 5; matrix products, arithmetic and copies ran while one was open for 1% -> 1% of each run, Pallas kernels for 44% -> 14%
where the time goes in v2:
time: 52.2 us; the launch traced here: 52 us
  starting transfers between devices  25.7 us (49%)
  Pallas kernels  10.8 us (21%)
  waiting for transfers between devices  9.32 us (18%)
  local copies, waits for them, and re-layouts  6.04 us (12%)
    ppermute x7, starting transfers between devices, local(): held[flip] = lax.ppermute(pieces[flip % near], 'grp', pairs)  12.4 us
    ppermute x7, starting transfers between devices, local(): got[flip] = lax.ppermute(sends[flip], ('rep', 'grp'), pairs)  11.7 us
    ppermute x7, waiting for transfers between devices, local(): got[flip] = lax.ppermute(sends[flip], ('rep', 'grp'), pairs)  7.29 us
    unnamed x13, local copies, waits for them, and re-layouts  6.04 us
    pallas_call x1, Pallas kernels, local(): pl.pallas_call(base_kernel, out_shape=[jax.ShapeDtypeStruct((step_count,...  4.5 us
    pallas_call x1, Pallas kernels, local(): pl.pallas_call(functools.partial(shrink_kernel, MEMBERS, halves, rank), o...  2.64 us
    pallas_call x1, Pallas kernels, local(): pl.pallas_call(functools.partial(pack_kernel, near, halves), out_shape=[j...  1.78 us
    ppermute x1, starting transfers between devices, local(): wanted.append(lax.ppermute(block_adapter, 'rep', pairs))  1.49 us
  transfers between devices with their start and end apart: 17, of which 5 were waited for; matrix products, arithmetic and copies ran while one was open for 1% of the time, Pallas kernels for 14%

profile of v2, /device:TPU:0, one launch (start us, length us, event | category | flops | bytes accessed | tf_op | source)
XLA Modules:
  0.0 52.0 jit_solution(17972666567394537113)
XLA Ops:
  0.0 1.8 %pack.1 = (bf16[16,2176]{1,0:T(8,128)(2,1)}, bf16[16,2176]{1,0:T(8,128)(2,1)}, bf16[16,2176]{1,0:T(8,128)(2,1)}, bf16[16,2176]{1,0:T(8,128)(2,1)}) custom-call(bf16[64,4096]{1,0:T(8,128)(2,1)} %bitcast.4, bf16[64,512]{1,0:T(8,128)(2,1)} %bitcast.5), custom_call_target="tpu_custom_call" | custom-call | tf_op jit(solution)/shard_map/pack/pallas_call | solution.py:145
  1.8 5.0 %collective-permute-start.4 = (bf16[16,2176]{1,0:T(8,128)(2,1)}, bf16[16,2176]{1,0:T(8,128)(2,1)S(1)}, u32[]{:S(2)}, u32[]{:S(2)}) collective-permute-start(bf16[16,2176]{1,0:T(8,128)(2,1)} %get-tuple-element.40), channel_id=1, source_target_pairs={{0,10},{2,8},{4,14},{6,12},{8,2},{10,0},{12,6},{14,4},{1,11},{3,9}... | collective-permute-start | bytes 208904 | tf_op jit(solution)/shard_map/ppermute | solution.py:156
  7.3 0.8 %copy.8.refs_0_ = s32[8,2]{1,0:T(8,128)S(1)} copy(s32[8,2]{0,1:T(2,128)} %param.12) | data formatting | bytes 128 | tf_op args[5]
  8.0 1.5 %collective-permute-start.7 = (s32[8,2]{1,0:T(8,128)S(1)}, s32[8,2]{1,0:T(8,128)S(1)}, u32[]{:S(2)}, u32[]{:S(2)}) collective-permute-start(s32[8,2]{1,0:T(8,128)S(1)} %copy.8.refs_0_), channel_id=1, source_target_pairs={{0,16},{16,0},{1,17},{17,1},{2,18},{18,2},{3,19},{19,3},{4,20},{20... | collective-permute-start | bytes 200 | tf_op jit(solution)/shard_map/ppermute | solution.py:160
  9.5 1.3 %collective-permute-start.5 = (bf16[16,2176]{1,0:T(8,128)(2,1)}, bf16[16,2176]{1,0:T(8,128)(2,1)S(1)}, u32[]{:S(2)}, u32[]{:S(2)}) collective-permute-start(bf16[16,2176]{1,0:T(8,128)(2,1)} %get-tuple-element.41), channel_id=1, source_target_pairs={{0,12},{2,14},{4,8},{6,10},{8,4},{10,6},{12,0},{14,2},{1,13},{3,15... | collective-permute-start | bytes 208904 | tf_op jit(solution)/shard_map/ppermute | solution.py:156
  11.6 3.3 %collective-permute-start.6 = (bf16[16,2176]{1,0:T(8,128)(2,1)}, bf16[16,2176]{1,0:T(8,128)(2,1)S(1)}, u32[]{:S(2)}, u32[]{:S(2)}) collective-permute-start(bf16[16,2176]{1,0:T(8,128)(2,1)} %get-tuple-element.42), channel_id=1, source_target_pairs={{0,14},{2,12},{4,10},{6,8},{8,6},{10,4},{12,2},{14,0},{1,15},{3,13... | collective-permute-start | bytes 208904 | tf_op jit(solution)/shard_map/ppermute | solution.py:156
  15.4 1.5 %collective-permute-start.3 = (bf16[16,2176]{1,0:T(8,128)(2,1)}, bf16[16,2176]{1,0:T(8,128)(2,1)S(1)}, u32[]{:S(2)}, u32[]{:S(2)}) collective-permute-start(bf16[16,2176]{1,0:T(8,128)(2,1)} %get-tuple-element.43.refs_2_), channel_id=1, source_target_pairs={{0,8},{2,10},{4,12},{6,14},{8,0},{10,2},{12,4},{14,6},{1,9},{3,11}... | collective-permute-start | bytes 208904 | tf_op jit(solution)/shard_map/ppermute | solution.py:156
  16.9 3.1 %copy-done = bf16[4,224,4096]{2,1,0:T(8,128)(2,1)S(1)} copy-done((bf16[4,224,4096]{2,1,0:T(8,128)(2,1)S(1)}, bf16[4,224,4096]{2,1,0:T(8,128)(2,1)}, u32[]{:S(2)}) %copy-start) | copy-done | bytes 7340056
  20.0 2.2 %copy-done.5 = bf16[4096,512]{1,0:T(8,128)(2,1)S(1)} copy-done((bf16[4096,512]{1,0:T(8,128)(2,1)S(1)}, bf16[4096,512]{1,0:T(8,128)(2,1)}, u32[]{:S(2)}) %copy-start.5) | copy-done | bytes 4194328
  22.2 4.5 %base.1 = (f32[4,224,256]{2,1,0:T(8,128)S(1)}, f32[4,224,256]{2,1,0:T(8,128)S(1)}) custom-call(bf16[4,224,4096]{2,1,0:T(8,128)(2,1)S(1)} %copy-done, bf16[4096,512]{1,0:T(8,128)(2,1)S(1)} %copy-done.5), custom_call_target="tpu_custom_call" | custom-call | flops 3758096384 | bytes 9175040 | tf_op jit(solution)/shard_map/base/pallas_call | solution.py:162
  26.8 0.8 %select.1 = (bf16[2,16,2176]{2,1,0:T(8,128)(2,1)S(1)}, bf16[2,16,2176]{2,1,0:T(8,128)(2,1)S(1)}, bf16[2,16,2176]{2,1,0:T(8,128)(2,1)S(1)}, bf16[2,16,2176]{2,1,0...) custom-call(s32[8]{0:T(128)S(1)} %copy-done.3, ...), custom_call_target="tpu_custom_call" | custom-call | tf_op jit(solution)/shard_map/select/pallas_call | solution.py:184
  27.7 1.6 %collective-permute-start.8 = (bf16[2,16,2176]{2,1,0:T(8,128)(2,1)S(1)}, bf16[2,16,2176]{2,1,0:T(8,128)(2,1)S(1)}, u32[]{:S(2)}, u32[]{:S(2)}) collective-permute-start(bf16[2,16,2176]{2,1,0:T(8,128)(2,1)S(1)} %get-tuple-element.64), channel_id=1, source_target_pairs={{0,2},{2,0},{4,6},{6,4},{8,10},{10,8},{12,14},{14,12},{16,18},{18,... | collective-permute-start | bytes 417800 | tf_op jit(solution)/shard_map/ppermute | solution.py:203
  29.3 0.7 %collective-permute-start.9 = (bf16[2,16,2176]{2,1,0:T(8,128)(2,1)S(1)}, bf16[2,16,2176]{2,1,0:T(8,128)(2,1)S(1)}, u32[]{:S(2)}, u32[]{:S(2)}) collective-permute-start(bf16[2,16,2176]{2,1,0:T(8,128)(2,1)S(1)} %get-tuple-element.65), channel_id=1, source_target_pairs={{0,4},{2,6},{4,0},{6,2},{8,12},{10,14},{12,8},{14,10},{16,20},{18,... | collective-permute-start | bytes 417800 | tf_op jit(solution)/shard_map/ppermute | solution.py:203
  29.9 1.3 %collective-permute-start.10 = (bf16[2,16,2176]{2,1,0:T(8,128)(2,1)S(1)}, bf16[2,16,2176]{2,1,0:T(8,128)(2,1)S(1)}, u32[]{:S(2)}, u32[]{:S(2)}) collective-permute-start(bf16[2,16,2176]{2,1,0:T(8,128)(2,1)S(1)} %get-tuple-element.66), channel_id=1, source_target_pairs={{0,6},{2,4},{4,2},{6,0},{8,14},{10,12},{12,10},{14,8},{16,22},{18,... | collective-permute-start | bytes 417800 | tf_op jit(solution)/shard_map/ppermute | solution.py:203
  31.2 1.5 %collective-permute-start.11 = (bf16[2,16,2176]{2,1,0:T(8,128)(2,1)S(1)}, bf16[2,16,2176]{2,1,0:T(8,128)(2,1)S(1)}, u32[]{:S(2)}, u32[]{:S(2)}) collective-permute-start(bf16[2,16,2176]{2,1,0:T(8,128)(2,1)S(1)} %get-tuple-element.67), channel_id=1, source_target_pairs={{0,16},{2,18},{4,20},{6,22},{8,24},{10,26},{12,28},{14,30},{16,0},... | collective-permute-start | bytes 417800 | tf_op jit(solution)/shard_map/ppermute | solution.py:203
  32.7 1.0 %collective-permute-done.8.refs_1_ = bf16[2,16,2176]{2,1,0:T(8,128)(2,1)S(1)} collective-permute-done((bf16[2,16,2176]{2,1,0:T(8,128)(2,1)S(1)}, bf16[2,16,2176]{2,1,0:T(8,128)(2,1)S(1)}, u32[]{:S(2)}, u32[]{:S(2)}) %collective-permute-start.8) | collective-permute-done | bytes 139296 | tf_op jit(solution)/shard_map/ppermute | solution.py:203
  33.8 2.4 %collective-permute-start.12 = (bf16[2,16,2176]{2,1,0:T(8,128)(2,1)S(1)}, bf16[2,16,2176]{2,1,0:T(8,128)(2,1)S(1)}, u32[]{:S(2)}, u32[]{:S(2)}) collective-permute-start(bf16[2,16,2176]{2,1,0:T(8,128)(2,1)S(1)} %get-tuple-element.68), channel_id=1, source_target_pairs={{0,18},{2,16},{4,22},{6,20},{8,26},{10,24},{12,30},{14,28},{16,2},... | collective-permute-start | bytes 417800 | tf_op jit(solution)/shard_map/ppermute | solution.py:203
  36.2 1.2 %collective-permute-start.13 = (bf16[2,16,2176]{2,1,0:T(8,128)(2,1)S(1)}, bf16[2,16,2176]{2,1,0:T(8,128)(2,1)S(1)}, u32[]{:S(2)}, u32[]{:S(2)}) collective-permute-start(bf16[2,16,2176]{2,1,0:T(8,128)(2,1)S(1)} %get-tuple-element.69), channel_id=1, source_target_pairs={{0,20},{2,22},{4,16},{6,18},{8,28},{10,30},{12,24},{14,26},{16,4},... | collective-permute-start | bytes 417800 | tf_op jit(solution)/shard_map/ppermute | solution.py:203
  37.4 1.1 %collective-permute-done.10.refs_3_ = bf16[2,16,2176]{2,1,0:T(8,128)(2,1)S(1)} collective-permute-done((bf16[2,16,2176]{2,1,0:T(8,128)(2,1)S(1)}, bf16[2,16,2176]{2,1,0:T(8,128)(2,1)S(1)}, u32[]{:S(2)}, u32[]{:S(2)}) %collective-permute-start.10) | collective-permute-done | bytes 139296 | tf_op jit(solution)/shard_map/ppermute | solution.py:203
  38.5 3.0 %collective-permute-start.14 = (bf16[2,16,2176]{2,1,0:T(8,128)(2,1)S(1)}, bf16[2,16,2176]{2,1,0:T(8,128)(2,1)S(1)}, u32[]{:S(2)}, u32[]{:S(2)}) collective-permute-start(bf16[2,16,2176]{2,1,0:T(8,128)(2,1)S(1)} %get-tuple-element.70), channel_id=1, source_target_pairs={{0,22},{2,20},{4,18},{6,16},{8,30},{10,28},{12,26},{14,24},{16,6},... | collective-permute-start | bytes 417800 | tf_op jit(solution)/shard_map/ppermute | solution.py:203
  41.5 5.1 %collective-permute-done.12.refs_5_ = bf16[2,16,2176]{2,1,0:T(8,128)(2,1)S(1)} collective-permute-done((bf16[2,16,2176]{2,1,0:T(8,128)(2,1)S(1)}, bf16[2,16,2176]{2,1,0:T(8,128)(2,1)S(1)}, u32[]{:S(2)}, u32[]{:S(2)}) %collective-permute-start.12) | collective-permute-done | bytes 139296 | tf_op jit(solution)/shard_map/ppermute | solution.py:203
  46.7 2.6 %shrink.1 = (f32[4,112,128]{2,1,0:T(8,128)S(1)}, bf16[128,256]{1,0:T(8,128)(2,1)S(1)}) custom-call(s32[8]{0:T(128)S(1)} %copy-done.4, bf16[4,224,4096]{2,1,0:T(8,128)(2,1)S(1)} %copy-done.1, bf16[2,16,2176]{2,1,0:T(8,128)(2,1)S(1)} %get-tuple-element.63.refs_0_, bf16[2,16,2176]{2,1,0:T(8,128)(2,1)S(1)} %collective-permute-done.8.refs_1_, ...), custom_call_target="tpu_custom_call" | custom-call | flops 939524096 | bytes 7340032 | tf_op jit(solution)/shard_map/shrink/pallas_call | solution.py:206
  49.4 1.5 %collective-permute-done.15.theirs_ref = f32[4,112,128]{2,1,0:T(8,128)S(1)} collective-permute-done((f32[4,112,128]{2,1,0:T(8,128)S(1)}, f32[4,112,128]{2,1,0:T(8,128)S(1)}, u32[]{:S(2)}, u32[]{:S(2)}) %collective-permute-start.15) | collective-permute-done | bytes 229408 | tf_op jit(solution)/shard_map/ppermute | solution.py:223
  50.9 1.1 %expand.1 = bf16[4,224,256]{2,1,0:T(8,128)(2,1)} custom-call(f32[4,112,128]{2,1,0:T(8,128)S(1)} %get-tuple-element.71.mine_ref, f32[4,112,128]{2,1,0:T(8,128)S(1)} %collective-permute-done.15.theirs_ref, bf16[128,256]{1,0:T(8,128)(2,1)S(1)} %get-tuple-element.72.up_ref, f32[4,224,256]{2,1,0:T(8,128)S(1)} %get-tuple-element.73.base_ref, ...), custom_call_target="tpu_custom_call" | custom-call | tf_op jit(solution)/shard_map/expand/pallas_call | solution.py:225
  (28 shorter events, 1.9 us)
Async XLA Ops:
  0.0 26.8 %copy-start.3 = (s32[8]{0:T(128)S(1)}, s32[8]{0:T(128)}, u32[]{:S(2)}) copy-start(s32[8]{0:T(128)} %home_ref.1) | copy-start | bytes 100
  1.8 44.9 %copy-start.4 = (s32[8]{0:T(128)S(1)}, s32[8]{0:T(128)}, u32[]{:S(2)}) copy-start(s32[8]{0:T(128)} %count_ref.1) | copy-start | bytes 100
  1.8 13.2 %collective-permute-start.4 = (bf16[16,2176]{1,0:T(8,128)(2,1)}, bf16[16,2176]{1,0:T(8,128)(2,1)S(1)}, u32[]{:S(2)}, u32[]{:S(2)}) collective-permute-start(bf16[16,2176]{1,0:T(8,128)(2,1)} %get-tuple-element.40), channel_id=1, source_target_pairs={{0,10},{2,8},{4,14},{6,12},{8,2},{10,0},{12,6},{14,4},{1,11},{3,9}... | collective-permute-start | bytes 208904 | tf_op jit(solution)/shard_map/ppermute | solution.py:156
  6.8 8.6 %collective-permute-start = (bf16[16,2176]{1,0:T(8,128)(2,1)}, bf16[16,2176]{1,0:T(8,128)(2,1)S(1)}, u32[]{:S(2)}, u32[]{:S(2)}) collective-permute-start(bf16[16,2176]{1,0:T(8,128)(2,1)} %get-tuple-element.40), channel_id=1, source_target_pairs={{0,2},{2,0},{4,6},{6,4},{8,10},{10,8},{12,14},{14,12},{1,3},{3,1},... | collective-permute-start | bytes 208904 | tf_op jit(solution)/shard_map/ppermute | solution.py:156
  8.0 3.6 %collective-permute-start.7 = (s32[8,2]{1,0:T(8,128)S(1)}, s32[8,2]{1,0:T(8,128)S(1)}, u32[]{:S(2)}, u32[]{:S(2)}) collective-permute-start(s32[8,2]{1,0:T(8,128)S(1)} %copy.8.refs_0_), channel_id=1, source_target_pairs={{0,16},{16,0},{1,17},{17,1},{2,18},{18,2},{3,19},{19,3},{4,20},{20... | collective-permute-start | bytes 200 | tf_op jit(solution)/shard_map/ppermute | solution.py:160
  9.5 17.2 %collective-permute-start.5 = (bf16[16,2176]{1,0:T(8,128)(2,1)}, bf16[16,2176]{1,0:T(8,128)(2,1)S(1)}, u32[]{:S(2)}, u32[]{:S(2)}) collective-permute-start(bf16[16,2176]{1,0:T(8,128)(2,1)} %get-tuple-element.41), channel_id=1, source_target_pairs={{0,12},{2,14},{4,8},{6,10},{8,4},{10,6},{12,0},{14,2},{1,13},{3,15... | collective-permute-start | bytes 208904 | tf_op jit(solution)/shard_map/ppermute | solution.py:156
  10.9 15.9 %collective-permute-start.1 = (bf16[16,2176]{1,0:T(8,128)(2,1)}, bf16[16,2176]{1,0:T(8,128)(2,1)S(1)}, u32[]{:S(2)}, u32[]{:S(2)}) collective-permute-start(bf16[16,2176]{1,0:T(8,128)(2,1)} %get-tuple-element.41), channel_id=1, source_target_pairs={{0,4},{2,6},{4,0},{6,2},{8,12},{10,14},{12,8},{14,10},{1,5},{3,7},... | collective-permute-start | bytes 208904 | tf_op jit(solution)/shard_map/ppermute | solution.py:156
  11.6 15.1 %collective-permute-start.6 = (bf16[16,2176]{1,0:T(8,128)(2,1)}, bf16[16,2176]{1,0:T(8,128)(2,1)S(1)}, u32[]{:S(2)}, u32[]{:S(2)}) collective-permute-start(bf16[16,2176]{1,0:T(8,128)(2,1)} %get-tuple-element.42), channel_id=1, source_target_pairs={{0,14},{2,12},{4,10},{6,8},{8,6},{10,4},{12,2},{14,0},{1,15},{3,13... | collective-permute-start | bytes 208904 | tf_op jit(solution)/shard_map/ppermute | solution.py:156
  15.0 11.8 %collective-permute-start.2 = (bf16[16,2176]{1,0:T(8,128)(2,1)}, bf16[16,2176]{1,0:T(8,128)(2,1)S(1)}, u32[]{:S(2)}, u32[]{:S(2)}) collective-permute-start(bf16[16,2176]{1,0:T(8,128)(2,1)} %get-tuple-element.42), channel_id=1, source_target_pairs={{0,6},{2,4},{4,2},{6,0},{8,14},{10,12},{12,10},{14,8},{1,7},{3,5},... | collective-permute-start | bytes 208904 | tf_op jit(solution)/shard_map/ppermute | solution.py:156
  15.4 11.4 %collective-permute-start.3 = (bf16[16,2176]{1,0:T(8,128)(2,1)}, bf16[16,2176]{1,0:T(8,128)(2,1)S(1)}, u32[]{:S(2)}, u32[]{:S(2)}) collective-permute-start(bf16[16,2176]{1,0:T(8,128)(2,1)} %get-tuple-element.43.refs_2_), channel_id=1, source_target_pairs={{0,8},{2,10},{4,12},{6,14},{8,0},{10,2},{12,4},{14,6},{1,9},{3,11}... | collective-permute-start | bytes 208904 | tf_op jit(solution)/shard_map/ppermute | solution.py:156
  16.9 3.1 %copy-start = (bf16[4,224,4096]{2,1,0:T(8,128)(2,1)S(1)}, bf16[4,224,4096]{2,1,0:T(8,128)(2,1)}, u32[]{:S(2)}) copy-start(bf16[4,224,4096]{2,1,0:T(8,128)(2,1)} %x_ref.3) | copy-start | bytes 22020100
  20.0 2.2 %copy-start.5 = (bf16[4096,512]{1,0:T(8,128)(2,1)S(1)}, bf16[4096,512]{1,0:T(8,128)(2,1)}, u32[]{:S(2)}) copy-start(bf16[4096,512]{1,0:T(8,128)(2,1)} %weight_ref.1) | copy-start | bytes 12582916
  22.2 4.6 %copy-start.2 = (bf16[16,2176]{1,0:T(8,128)(2,1)S(1)}, bf16[16,2176]{1,0:T(8,128)(2,1)}, u32[]{:S(2)}) copy-start(bf16[16,2176]{1,0:T(8,128)(2,1)} %get-tuple-element.43.refs_2_) | copy-start | bytes 208900
  22.2 24.4 %copy-start.1 = (bf16[4,224,4096]{2,1,0:T(8,128)(2,1)S(1)}, bf16[4,224,4096]{2,1,0:T(8,128)(2,1)}, u32[]{:S(2)}) copy-start(bf16[4,224,4096]{2,1,0:T(8,128)(2,1)} %x_ref.3) | copy-start | bytes 22020100
  27.6 23.3 %collective-permute-start.16 = (f32[4,224,256]{2,1,0:T(8,128)S(1)}, f32[4,224,256]{2,1,0:T(8,128)S(1)}, u32[]{:S(2)}, u32[]{:S(2)}) collective-permute-start(f32[4,224,256]{2,1,0:T(8,128)S(1)} %get-tuple-element.74), channel_id=1, source_target_pairs={{0,1},{1,0},{2,3},{3,2},{4,5},{5,4},{6,7},{7,6},{8,9},{9,8},{10,11... | collective-permute-start | bytes 2752520 | tf_op jit(solution)/shard_map/ppermute | solution.py:195
  27.7 6.1 %collective-permute-start.8 = (bf16[2,16,2176]{2,1,0:T(8,128)(2,1)S(1)}, bf16[2,16,2176]{2,1,0:T(8,128)(2,1)S(1)}, u32[]{:S(2)}, u32[]{:S(2)}) collective-permute-start(bf16[2,16,2176]{2,1,0:T(8,128)(2,1)S(1)} %get-tuple-element.64), channel_id=1, source_target_pairs={{0,2},{2,0},{4,6},{6,4},{8,10},{10,8},{12,14},{14,12},{16,18},{18,... | collective-permute-start | bytes 417800 | tf_op jit(solution)/shard_map/ppermute | solution.py:203
  29.3 7.0 %collective-permute-start.9 = (bf16[2,16,2176]{2,1,0:T(8,128)(2,1)S(1)}, bf16[2,16,2176]{2,1,0:T(8,128)(2,1)S(1)}, u32[]{:S(2)}, u32[]{:S(2)}) collective-permute-start(bf16[2,16,2176]{2,1,0:T(8,128)(2,1)S(1)} %get-tuple-element.65), channel_id=1, source_target_pairs={{0,4},{2,6},{4,0},{6,2},{8,12},{10,14},{12,8},{14,10},{16,20},{18,... | collective-permute-start | bytes 417800 | tf_op jit(solution)/shard_map/ppermute | solution.py:203
  29.9 8.6 %collective-permute-start.10 = (bf16[2,16,2176]{2,1,0:T(8,128)(2,1)S(1)}, bf16[2,16,2176]{2,1,0:T(8,128)(2,1)S(1)}, u32[]{:S(2)}, u32[]{:S(2)}) collective-permute-start(bf16[2,16,2176]{2,1,0:T(8,128)(2,1)S(1)} %get-tuple-element.66), channel_id=1, source_target_pairs={{0,6},{2,4},{4,2},{6,0},{8,14},{10,12},{12,10},{14,8},{16,22},{18,... | collective-permute-start | bytes 417800 | tf_op jit(solution)/shard_map/ppermute | solution.py:203
  31.2 10.3 %collective-permute-start.11 = (bf16[2,16,2176]{2,1,0:T(8,128)(2,1)S(1)}, bf16[2,16,2176]{2,1,0:T(8,128)(2,1)S(1)}, u32[]{:S(2)}, u32[]{:S(2)}) collective-permute-start(bf16[2,16,2176]{2,1,0:T(8,128)(2,1)S(1)} %get-tuple-element.67), channel_id=1, source_target_pairs={{0,16},{2,18},{4,20},{6,22},{8,24},{10,26},{12,28},{14,30},{16,0},... | collective-permute-start | bytes 417800 | tf_op jit(solution)/shard_map/ppermute | solution.py:203
  33.8 12.9 %collective-permute-start.12 = (bf16[2,16,2176]{2,1,0:T(8,128)(2,1)S(1)}, bf16[2,16,2176]{2,1,0:T(8,128)(2,1)S(1)}, u32[]{:S(2)}, u32[]{:S(2)}) collective-permute-start(bf16[2,16,2176]{2,1,0:T(8,128)(2,1)S(1)} %get-tuple-element.68), channel_id=1, source_target_pairs={{0,18},{2,16},{4,22},{6,20},{8,26},{10,24},{12,30},{14,28},{16,2},... | collective-permute-start | bytes 417800 | tf_op jit(solution)/shard_map/ppermute | solution.py:203
  36.2 10.4 %collective-permute-start.13 = (bf16[2,16,2176]{2,1,0:T(8,128)(2,1)S(1)}, bf16[2,16,2176]{2,1,0:T(8,128)(2,1)S(1)}, u32[]{:S(2)}, u32[]{:S(2)}) collective-permute-start(bf16[2,16,2176]{2,1,0:T(8,128)(2,1)S(1)} %get-tuple-element.69), channel_id=1, source_target_pairs={{0,20},{2,22},{4,16},{6,18},{8,28},{10,30},{12,24},{14,26},{16,4},... | collective-permute-start | bytes 417800 | tf_op jit(solution)/shard_map/ppermute | solution.py:203
  38.5 8.1 %collective-permute-start.14 = (bf16[2,16,2176]{2,1,0:T(8,128)(2,1)S(1)}, bf16[2,16,2176]{2,1,0:T(8,128)(2,1)S(1)}, u32[]{:S(2)}, u32[]{:S(2)}) collective-permute-start(bf16[2,16,2176]{2,1,0:T(8,128)(2,1)S(1)} %get-tuple-element.70), channel_id=1, source_target_pairs={{0,22},{2,20},{4,18},{6,16},{8,30},{10,28},{12,26},{14,24},{16,6},... | collective-permute-start | bytes 417800 | tf_op jit(solution)/shard_map/ppermute | solution.py:203
  49.3 1.6 %collective-permute-start.15 = (f32[4,112,128]{2,1,0:T(8,128)S(1)}, f32[4,112,128]{2,1,0:T(8,128)S(1)}, u32[]{:S(2)}, u32[]{:S(2)}) collective-permute-start(f32[4,112,128]{2,1,0:T(8,128)S(1)} %get-tuple-element.71.mine_ref), channel_id=1, source_target_pairs={{0,1},{1,0},{2,3},{3,2},{4,5},{5,4},{6,7},{7,6},{8,9},{9,8},{10,11... | collective-permute-start | bytes 688136 | tf_op jit(solution)/shard_map/ppermute | solution.py:223

commit v3 on v2

--- a/solution.py
+++ b/solution.py
@@ -16,21 +16,33 @@
 VMEM = pl.BlockSpec(memory_space=pltpu.VMEM)
 
 
-def pack_kernel(near, halves, down_ref, up_ref, *outs):
+def pack_kernel(near, halves, down_ref, up_ref, *refs):
+    outs, sem = refs[:-1], refs[-1]
     member_base = lax.axis_index("rep") * near
     low = lax.rem(lax.axis_index("grp"), near)
     tp_index = lax.axis_index("tp")
     wide = down_ref.shape[1] // halves
     up_own = up_ref.shape[1] // lax.axis_size("tp")
     up_wide = up_own // halves
-    for flip in range(near):
-        member = member_base + (low ^ flip)
+    copies = []
+    for at, out in enumerate(outs):
+        member = member_base + (low ^ at % near)
         rows = pl.ds(pl.multiple_of(member // halves * PIECE_ROWS, PIECE_ROWS), PIECE_ROWS)
         half = lax.rem(member, halves)
-        outs[flip][:, :wide] = down_ref[rows, pl.ds(pl.multiple_of(half * wide, 128), wide)]
-        outs[flip][:, wide:] = up_ref[
-            rows, pl.ds(pl.multiple_of(tp_index * up_own + half * up_wide, 128), up_wide)
+        down_at = pl.ds(pl.multiple_of(half * wide, 128), wide)
+        up_at = pl.ds(pl.multiple_of(tp_index * up_own + half * up_wide, 128), up_wide)
+        copies += [
+            pltpu.make_async_copy(
+                down_ref.at[rows, down_at], out.at[:, pl.ds(0, wide)], sem.at[2 * at]
+            ),
+            pltpu.make_async_copy(
+                up_ref.at[rows, up_at], out.at[:, pl.ds(wide, up_wide)], sem.at[2 * at + 1]
+            ),
         ]
+    for copy in copies:
+        copy.start()
+    for copy in copies:
+        copy.wait()
 
 
 def select_kernel(near, rep_count, part_count, home_ref, *refs):
@@ -45,34 +57,45 @@
     else:
         stack = refs[near * rep_count]
         for part in range(part_count):
-            stack[part] = held[part][...]
+            stack[part_count - 1 - part] = held[part][...]
     for flip in range(near * rep_count):
         other = group_index ^ (flip % near)
         for slot in range(slot_count):
-            adapter = jnp.clip(wanted[flip // near][other, slot], 0, pool_size - 1)
+            adapter = jnp.clip(wanted[flip // near][slot, other], 0, pool_size - 1)
             place = jnp.clip(home_ref[adapter], 0, pool_size - 1) ^ group_index
             outs[flip][slot] = stack[place]
 
 
 def base_kernel(x_ref, weight_ref, mine_ref, theirs_ref):
-    share = mine_ref.shape[2]
+    rows, share = mine_ref.shape
+    x = x_ref[...].reshape(rows, x_ref.shape[2])
+    product = jnp.dot(x, weight_ref[...], preferred_element_type=jnp.float32)
+    first, second = product[:, :share], product[:, share:]
     tp_index = lax.axis_index("tp")
-    for step in range(x_ref.shape[0]):
-        product = jnp.dot(x_ref[step], weight_ref[...], preferred_element_type=jnp.float32)
-
-        @pl.when(tp_index == 0)
+    fresh = pl.program_id(0) == 0
+
+    def store(mine, theirs):
+        @pl.when(fresh)
         def _():
-            mine_ref[step] = product[:, :share]
-            theirs_ref[step] = product[:, share:]
-
-        @pl.when(tp_index == 1)
+            mine_ref[...] = mine
+            theirs_ref[...] = theirs
+
+        @pl.when(jnp.logical_not(fresh))
         def _():
-            mine_ref[step] = product[:, share:]
-            theirs_ref[step] = product[:, :share]
+            mine_ref[...] += mine
+            theirs_ref[...] += theirs
+
+    @pl.when(tp_index == 0)
+    def _():
+        store(first, second)
+
+    @pl.when(tp_index == 1)
+    def _():
+        store(second, first)
 
 
 def shrink_kernel(member_count, halves, rank, count_ref, x_ref, *refs):
-    pieces, refs = refs[:member_count], refs[member_count:]
+    pieces, refs = refs[:member_count][::-1], refs[member_count:]
     shrunk_ref, up_ref, down = refs
     slot_count = pieces[0].shape[0]
     wide = down.shape[1] // halves
@@ -119,9 +142,9 @@
                 [jnp.where(slot_of == slot, term, zero) for term in (top, mid, low)], axis=1
             )
             expanded = jnp.dot(terms, up_thrice, preferred_element_type=jnp.float32)
-            at = pl.ds(slot * rows, rows)
-            total = base_ref[step, at, :] + base_other_ref[step, at, :]
-            done[step, at, :] = (total + adapter_scale_factor * expanded).astype(done.dtype)
+            at = pl.ds((step * slot_count + slot) * rows, rows)
+            total = base_ref[at, :] + base_other_ref[at, :]
+            done[step, pl.ds(slot * rows, rows), :] = (total + adapter_scale_factor * expanded).astype(done.dtype)
         pltpu.make_async_copy(done.at[step], out_ref.at[step], sem.at[step]).start()
     for step in range(mine_ref.shape[0]):
         pltpu.make_async_copy(done.at[step], out_ref.at[step], sem.at[step]).wait()
@@ -142,32 +165,43 @@
     bf16, f32 = jnp.bfloat16, jnp.float32
 
     down = jnp.swapaxes(pool_down[0], 0, 1)
+    distinct = group_count if group_count <= MEMBERS else near
     pieces = pl.pallas_call(
         functools.partial(pack_kernel, near, halves),
-        out_shape=[jax.ShapeDtypeStruct((PIECE_ROWS, piece_width), bf16)] * near,
-        in_specs=[VMEM, VMEM],
-        out_specs=[VMEM] * near,
+        out_shape=[jax.ShapeDtypeStruct((PIECE_ROWS, piece_width), bf16)] * distinct,
+        in_specs=[ANY, ANY],
+        out_specs=[VMEM] * distinct,
+        scratch_shapes=[pltpu.SemaphoreType.DMA((2 * distinct,))],
+        compiler_params=pltpu.CompilerParams(vmem_limit_bytes=56 << 20),
         name="pack",
     )(down, pool_up[0])
 
     held = [pieces[0]] + [None] * (group_count - 1)
     for flip in range(group_count - 1, 0, -1):
         pairs = [(g, g ^ flip) for g in range(group_count)]
-        held[flip] = lax.ppermute(pieces[flip % near], "grp", pairs)
-    wanted = [block_adapter]
+        held[flip] = lax.ppermute(pieces[flip % distinct], "grp", pairs)
+    asked = jnp.swapaxes(block_adapter, 0, 1)
+    wanted = [asked]
     for flip in range(1, rep_count):
         pairs = [(r, r ^ flip) for r in range(rep_count)]
-        wanted.append(lax.ppermute(block_adapter, "rep", pairs))
-
+        wanted.append(lax.ppermute(asked, "rep", pairs))
+
+    chunk_count = 4
+    chunk = half_width // chunk_count
+    rows = step_count * row_count
     mine, theirs = pl.pallas_call(
         base_kernel,
-        out_shape=[jax.ShapeDtypeStruct((step_count, row_count, share), f32)] * 2,
-        in_specs=[VMEM, VMEM],
-        out_specs=[VMEM, VMEM],
-        compiler_params=pltpu.CompilerParams(vmem_limit_bytes=24 << 20),
+        grid=(chunk_count,),
+        out_shape=[jax.ShapeDtypeStruct((rows, share), f32)] * 2,
+        in_specs=[
+            pl.BlockSpec((step_count, row_count, chunk), lambda k: (0, 0, k)),
+            pl.BlockSpec((chunk, col_count), lambda k: (k, 0)),
+        ],
+        out_specs=[pl.BlockSpec((rows, share), lambda k: (0, 0))] * 2,
+        compiler_params=pltpu.CompilerParams(vmem_limit_bytes=52 << 20),
         cost_estimate=pl.CostEstimate(
-            flops=2 * step_count * row_count * half_width * col_count,
-            bytes_accessed=2 * step_count * row_count * (half_width + 4 * share),
+            flops=2 * rows * half_width * col_count,
+            bytes_accessed=2 * rows * (half_width + 4 * share),
             transcendentals=0,
         ),
         name="base",
@@ -177,7 +211,7 @@
     )
 
     if group_count <= MEMBERS:
-        parts = held
+        parts = held[::-1]
         stack = [pltpu.VMEM((group_count, PIECE_ROWS, piece_width), bf16)]
     else:
         parts, stack = [jnp.stack(held)], []
@@ -219,7 +253,7 @@
             transcendentals=0,
         ),
         name="shrink",
-    )(block_count, hidden, *got)
+    )(block_count, hidden, *got[::-1])
     shrunk_other = lax.ppermute(shrunk, "tp", swap)
 
     return pl.pallas_call(

time: 52.2 us -> 53.7 us (1.029)
  waiting for transfers between devices: 9.32 us -> 16.4 us
  local copies, waits for them, and re-layouts: 6.04 us -> 0.03 us
  Pallas kernels: 10.8 us -> 14.1 us
  starting transfers between devices: 25.7 us -> 22.8 us
    ppermute x7, waiting for transfers between devices: 7.29 us -> 15 us  [local(): got[flip] = lax.ppermute(sends[flip], ('rep', 'grp'), pairs)]
    unnamed x13 -> x12, local copies, waits for them, and re-layouts: 6.04 us -> 0.03 us
    ppermute x7, starting transfers between devices: 11.7 us -> 6.91 us  [local(): got[flip] = lax.ppermute(sends[flip], ('rep', 'grp'), pairs)]
    pallas_call x1, Pallas kernels: 4.5 us -> 7.56 us  [local(): pl.pallas_call(base_kernel, grid=(chunk_count,), out_shape=[jax.ShapeDtyp...]
    ppermute x8, starting transfers between devices: 13.9 us -> 15.7 us  [the longest x7 14.2 us: local(): held[flip] = lax.ppermute(pieces[flip % distinct], 'grp', pairs)]
  transfers between devices with their start and end apart: 17 -> 17, of which waited for: 5 -> 6; matrix products, arithmetic and copies ran while one was open for 1% -> 0% of each run, Pallas kernels for 14% -> 19%
where the time goes in v3:
time: 53.7 us; the launch traced here: 53.5 us
  starting transfers between devices  22.8 us (42%)
  waiting for transfers between devices  16.4 us (31%)
  Pallas kernels  14.1 us (26%)
    ppermute x7, waiting for transfers between devices, local(): got[flip] = lax.ppermute(sends[flip], ('rep', 'grp'), pairs)  15 us
    ppermute x7, starting transfers between devices, local(): held[flip] = lax.ppermute(pieces[flip % distinct], 'grp', pairs)  14.2 us
    pallas_call x1, Pallas kernels, local(): pl.pallas_call(base_kernel, grid=(chunk_count,), out_shape=[jax.ShapeDtyp...  7.56 us
    ppermute x7, starting transfers between devices, local(): got[flip] = lax.ppermute(sends[flip], ('rep', 'grp'), pairs)  6.91 us
    pallas_call x1, Pallas kernels, local(): pl.pallas_call(functools.partial(shrink_kernel, MEMBERS, halves, rank), o...  2.64 us
    pallas_call x1, Pallas kernels, local(): pl.pallas_call(functools.partial(pack_kernel, near, halves), out_shape=[j...  2.08 us
    ppermute x1, starting transfers between devices, local(): wanted.append(lax.ppermute(asked, 'rep', pairs))  1.49 us
    ppermute x1, waiting for transfers between devices, local(): shrunk_other = lax.ppermute(shrunk, 'tp', swap)  1.48 us
  transfers between devices with their start and end apart: 17, of which 6 were waited for; matrix products, arithmetic and copies ran while one was open for 0% of the time, Pallas kernels for 19%

profile of v3, /device:TPU:0, one launch (start us, length us, event | category | flops | bytes accessed | tf_op | source)
XLA Modules:
  0.0 53.5 jit_solution(15382215749998966540)
XLA Ops:
  0.0 2.1 %pack.1 = (bf16[16,2176]{1,0:T(8,128)(2,1)}, bf16[16,2176]{1,0:T(8,128)(2,1)}, bf16[16,2176]{1,0:T(8,128)(2,1)}, bf16[16,2176]{1,0:T(8,128)(2,1)}, bf16[16,2176]...) custom-call(bf16[64,4096]{1,0:T(8,128)(2,1)} %bitcast.9, ...), custom_call_target="tpu_custom_call" | custom-call | tf_op jit(solution)/shard_map/pack/pallas_call | solution.py:169
  2.1 3.1 %collective-permute-start = (bf16[16,2176]{1,0:T(8,128)(2,1)}, bf16[16,2176]{1,0:T(8,128)(2,1)S(1)}, u32[]{:S(2)}, u32[]{:S(2)}) collective-permute-start(bf16[16,2176]{1,0:T(8,128)(2,1)} %get-tuple-element.44), channel_id=1, source_target_pairs={{0,2},{2,0},{4,6},{6,4},{8,10},{10,8},{12,14},{14,12},{1,3},{3,1},... | collective-permute-start | bytes 208904 | tf_op jit(solution)/shard_map/ppermute | solution.py:182
  5.2 1.6 %collective-permute-start.1 = (bf16[16,2176]{1,0:T(8,128)(2,1)}, bf16[16,2176]{1,0:T(8,128)(2,1)S(1)}, u32[]{:S(2)}, u32[]{:S(2)}) collective-permute-start(bf16[16,2176]{1,0:T(8,128)(2,1)} %get-tuple-element.45), channel_id=1, source_target_pairs={{0,4},{2,6},{4,0},{6,2},{8,12},{10,14},{12,8},{14,10},{1,5},{3,7},... | collective-permute-start | bytes 208904 | tf_op jit(solution)/shard_map/ppermute | solution.py:182
  6.8 1.5 %collective-permute-start.7 = (s32[2,8]{1,0:T(2,128)}, s32[2,8]{1,0:T(2,128)S(1)}, u32[]{:S(2)}, u32[]{:S(2)}) collective-permute-start(s32[2,8]{1,0:T(2,128)} %bitcast.7), channel_id=1, source_target_pairs={{0,16},{16,0},{1,17},{17,1},{2,18},{18,2},{3,19},{19,3},{4,20},{20... | collective-permute-start | bytes 200 | tf_op jit(solution)/shard_map/ppermute | solution.py:187
  8.3 0.4 collective-permute-start.2
  8.6 2.6 %collective-permute-start.3 = (bf16[16,2176]{1,0:T(8,128)(2,1)}, bf16[16,2176]{1,0:T(8,128)(2,1)S(1)}, u32[]{:S(2)}, u32[]{:S(2)}) collective-permute-start(bf16[16,2176]{1,0:T(8,128)(2,1)} %get-tuple-element.47), channel_id=1, source_target_pairs={{0,8},{2,10},{4,12},{6,14},{8,0},{10,2},{12,4},{14,6},{1,9},{3,11}... | collective-permute-start | bytes 208904 | tf_op jit(solution)/shard_map/ppermute | solution.py:182
  11.2 1.8 %collective-permute-start.4 = (bf16[16,2176]{1,0:T(8,128)(2,1)}, bf16[16,2176]{1,0:T(8,128)(2,1)S(1)}, u32[]{:S(2)}, u32[]{:S(2)}) collective-permute-start(bf16[16,2176]{1,0:T(8,128)(2,1)} %get-tuple-element.48), channel_id=1, source_target_pairs={{0,10},{2,8},{4,14},{6,12},{8,2},{10,0},{12,6},{14,4},{1,11},{3,9}... | collective-permute-start | bytes 208904 | tf_op jit(solution)/shard_map/ppermute | solution.py:182
  13.1 3.1 %collective-permute-start.5 = (bf16[16,2176]{1,0:T(8,128)(2,1)}, bf16[16,2176]{1,0:T(8,128)(2,1)S(1)}, u32[]{:S(2)}, u32[]{:S(2)}) collective-permute-start(bf16[16,2176]{1,0:T(8,128)(2,1)} %get-tuple-element.49), channel_id=1, source_target_pairs={{0,12},{2,14},{4,8},{6,10},{8,4},{10,6},{12,0},{14,2},{1,13},{3,15... | collective-permute-start | bytes 208904 | tf_op jit(solution)/shard_map/ppermute | solution.py:182
  16.1 1.7 %collective-permute-start.6 = (bf16[16,2176]{1,0:T(8,128)(2,1)}, bf16[16,2176]{1,0:T(8,128)(2,1)S(1)}, u32[]{:S(2)}, u32[]{:S(2)}) collective-permute-start(bf16[16,2176]{1,0:T(8,128)(2,1)} %get-tuple-element.50), channel_id=1, source_target_pairs={{0,14},{2,12},{4,10},{6,8},{8,6},{10,4},{12,2},{14,0},{1,15},{3,13... | collective-permute-start | bytes 208904 | tf_op jit(solution)/shard_map/ppermute | solution.py:182
  17.9 7.6 %base.1 = (f32[896,256]{1,0:T(8,128)S(1)}, f32[896,256]{1,0:T(8,128)S(1)}) custom-call(bf16[4,224,4096]{2,1,0:T(8,128)(2,1)} %x_ref.3, bf16[4096,512]{1,0:T(8,128)(2,1)} %weight_ref.1), custom_call_target="tpu_custom_call" | custom-call | flops 3758096384 | bytes 9175040 | tf_op jit(solution)/shard_map/base/pallas_call | solution.py:192
  25.5 0.7 %select.1 = (bf16[2,16,2176]{2,1,0:T(8,128)(2,1)S(1)}, bf16[2,16,2176]{2,1,0:T(8,128)(2,1)S(1)}, bf16[2,16,2176]{2,1,0:T(8,128)(2,1)S(1)}, bf16[2,16,2176]{2,1,0...) custom-call(s32[8]{0:T(128)S(1)} %copy-done.2, ...), custom_call_target="tpu_custom_call" | custom-call | tf_op jit(solution)/shard_map/select/pallas_call | solution.py:218
  26.5 2.8 %collective-permute-start.9 = (bf16[2,16,2176]{2,1,0:T(8,128)(2,1)S(1)}, bf16[2,16,2176]{2,1,0:T(8,128)(2,1)S(1)}, u32[]{:S(2)}, u32[]{:S(2)}) collective-permute-start(bf16[2,16,2176]{2,1,0:T(8,128)(2,1)S(1)} %get-tuple-element.72), channel_id=1, source_target_pairs={{0,20},{2,22},{4,16},{6,18},{8,28},{10,30},{12,24},{14,26},{16,4},... | collective-permute-start | bytes 417800 | tf_op jit(solution)/shard_map/ppermute | solution.py:237
  29.2 2.4 %collective-permute-start.10 = (bf16[2,16,2176]{2,1,0:T(8,128)(2,1)S(1)}, bf16[2,16,2176]{2,1,0:T(8,128)(2,1)S(1)}, u32[]{:S(2)}, u32[]{:S(2)}) collective-permute-start(bf16[2,16,2176]{2,1,0:T(8,128)(2,1)S(1)} %get-tuple-element.73), channel_id=1, source_target_pairs={{0,18},{2,16},{4,22},{6,20},{8,26},{10,24},{12,30},{14,28},{16,2},... | collective-permute-start | bytes 417800 | tf_op jit(solution)/shard_map/ppermute | solution.py:237
  31.7 0.5 %collective-permute-start.11 = (bf16[2,16,2176]{2,1,0:T(8,128)(2,1)S(1)}, bf16[2,16,2176]{2,1,0:T(8,128)(2,1)S(1)}, u32[]{:S(2)}, u32[]{:S(2)}) collective-permute-start(bf16[2,16,2176]{2,1,0:T(8,128)(2,1)S(1)} %get-tuple-element.74), channel_id=1, source_target_pairs={{0,16},{2,18},{4,20},{6,22},{8,24},{10,26},{12,28},{14,30},{16,0},... | collective-permute-start | bytes 417800 | tf_op jit(solution)/shard_map/ppermute | solution.py:237
  32.2 2.5 %collective-permute-done.8.refs_0_ = bf16[2,16,2176]{2,1,0:T(8,128)(2,1)S(1)} collective-permute-done((bf16[2,16,2176]{2,1,0:T(8,128)(2,1)S(1)}, bf16[2,16,2176]{2,1,0:T(8,128)(2,1)S(1)}, u32[]{:S(2)}, u32[]{:S(2)}) %collective-permute-start.8) | collective-permute-done | bytes 139296 | tf_op jit(solution)/shard_map/ppermute | solution.py:237
  34.8 1.5 %collective-permute-done.9.refs_1_ = bf16[2,16,2176]{2,1,0:T(8,128)(2,1)S(1)} collective-permute-done((bf16[2,16,2176]{2,1,0:T(8,128)(2,1)S(1)}, bf16[2,16,2176]{2,1,0:T(8,128)(2,1)S(1)}, u32[]{:S(2)}, u32[]{:S(2)}) %collective-permute-start.9) | collective-permute-done | bytes 139296 | tf_op jit(solution)/shard_map/ppermute | solution.py:237
  36.3 0.4 collective-permute-start.13
  36.7 6.3 %collective-permute-done.10.refs_2_ = bf16[2,16,2176]{2,1,0:T(8,128)(2,1)S(1)} collective-permute-done((bf16[2,16,2176]{2,1,0:T(8,128)(2,1)S(1)}, bf16[2,16,2176]{2,1,0:T(8,128)(2,1)S(1)}, u32[]{:S(2)}, u32[]{:S(2)}) %collective-permute-start.10) | collective-permute-done | bytes 139296 | tf_op jit(solution)/shard_map/ppermute | solution.py:237
  43.0 0.5 collective-permute-start.14
  43.5 0.4 collective-permute-done.11.refs_3_
  43.9 4.3 %collective-permute-done.14.refs_6_ = bf16[2,16,2176]{2,1,0:T(8,128)(2,1)S(1)} collective-permute-done((bf16[2,16,2176]{2,1,0:T(8,128)(2,1)S(1)}, bf16[2,16,2176]{2,1,0:T(8,128)(2,1)S(1)}, u32[]{:S(2)}, u32[]{:S(2)}) %collective-permute-start.14) | collective-permute-done | bytes 139296 | tf_op jit(solution)/shard_map/ppermute | solution.py:237
  48.2 2.6 %shrink.1 = (f32[4,112,128]{2,1,0:T(8,128)S(1)}, bf16[128,256]{1,0:T(8,128)(2,1)S(1)}) custom-call(s32[8]{0:T(128)S(1)} %copy-done.3, bf16[4,224,4096]{2,1,0:T(8,128)(2,1)S(1)} %bitcast.6, bf16[2,16,2176]{2,1,0:T(8,128)(2,1)S(1)} %collective-permute-done.8.refs_0_, bf16[2,16,2176]{2,1,0:T(8,128)(2,1)S(1)} %collective-permute-done.9.refs_1_, ...), custom_call_target="tpu_custom_call" | custom-call | flops 939524096 | bytes 7340032 | tf_op jit(solution)/shard_map/shrink/pallas_call | solution.py:240
  50.9 1.5 %collective-permute-done.15.theirs_ref = f32[4,112,128]{2,1,0:T(8,128)S(1)} collective-permute-done((f32[4,112,128]{2,1,0:T(8,128)S(1)}, f32[4,112,128]{2,1,0:T(8,128)S(1)}, u32[]{:S(2)}, u32[]{:S(2)}) %collective-permute-start.15) | collective-permute-done | bytes 229408 | tf_op jit(solution)/shard_map/ppermute | solution.py:257
  52.4 1.1 %expand.1 = bf16[4,224,256]{2,1,0:T(8,128)(2,1)} custom-call(f32[4,112,128]{2,1,0:T(8,128)S(1)} %get-tuple-element.79.mine_ref, f32[4,112,128]{2,1,0:T(8,128)S(1)} %collective-permute-done.15.theirs_ref, bf16[128,256]{1,0:T(8,128)(2,1)S(1)} %get-tuple-element.80.up_ref, f32[896,256]{1,0:T(8,128)S(1)} %get-tuple-element.81.base_ref, ...), custom_call_target="tpu_custom_call" | custom-call | tf_op jit(solution)/shard_map/expand/pallas_call | solution.py:259
  (28 shorter events, 0.5 us)
Async XLA Ops:
  0.0 25.5 %copy-start.1 = (s32[8,2]{0,1:T(2,128)S(1)}, s32[8,2]{0,1:T(2,128)}, u32[]{:S(2)}) copy-start(s32[8,2]{0,1:T(2,128)} %param.12) | copy-start | bytes 196
  0.0 25.5 %copy-start.2 = (s32[8]{0:T(128)S(1)}, s32[8]{0:T(128)}, u32[]{:S(2)}) copy-start(s32[8]{0:T(128)} %home_ref.1) | copy-start | bytes 100
  2.1 23.4 %copy-start = (bf16[16,2176]{1,0:T(8,128)(2,1)S(1)}, bf16[16,2176]{1,0:T(8,128)(2,1)}, u32[]{:S(2)}) copy-start(bf16[16,2176]{1,0:T(8,128)(2,1)} %get-tuple-element.62.refs_9_) | copy-start | bytes 208900
  2.1 46.1 %slice-start = ((s8[7340032]{0:T(1024)(128)(4,1)}), s8[4194304]{0:T(1024)(128)(4,1)S(1)}, s32[]{:S(2)}) async-start(s8[7340032]{0:T(1024)(128)(4,1)} %bitcast.5), calls=%async_computation | async-start | bytes 8388608
  2.1 46.1 %copy-start.3 = (s32[8]{0:T(128)S(1)}, s32[8]{0:T(128)}, u32[]{:S(2)}) copy-start(s32[8]{0:T(128)} %count_ref.1) | copy-start | bytes 100
  2.1 10.9 %collective-permute-start = (bf16[16,2176]{1,0:T(8,128)(2,1)}, bf16[16,2176]{1,0:T(8,128)(2,1)S(1)}, u32[]{:S(2)}, u32[]{:S(2)}) collective-permute-start(bf16[16,2176]{1,0:T(8,128)(2,1)} %get-tuple-element.44), channel_id=1, source_target_pairs={{0,2},{2,0},{4,6},{6,4},{8,10},{10,8},{12,14},{14,12},{1,3},{3,1},... | collective-permute-start | bytes 208904 | tf_op jit(solution)/shard_map/ppermute | solution.py:182
  5.2 11.0 %collective-permute-start.1 = (bf16[16,2176]{1,0:T(8,128)(2,1)}, bf16[16,2176]{1,0:T(8,128)(2,1)S(1)}, u32[]{:S(2)}, u32[]{:S(2)}) collective-permute-start(bf16[16,2176]{1,0:T(8,128)(2,1)} %get-tuple-element.45), channel_id=1, source_target_pairs={{0,4},{2,6},{4,0},{6,2},{8,12},{10,14},{12,8},{14,10},{1,5},{3,7},... | collective-permute-start | bytes 208904 | tf_op jit(solution)/shard_map/ppermute | solution.py:182
  6.8 4.5 %collective-permute-start.7 = (s32[2,8]{1,0:T(2,128)}, s32[2,8]{1,0:T(2,128)S(1)}, u32[]{:S(2)}, u32[]{:S(2)}) collective-permute-start(s32[2,8]{1,0:T(2,128)} %bitcast.7), channel_id=1, source_target_pairs={{0,16},{16,0},{1,17},{17,1},{2,18},{18,2},{3,19},{19,3},{4,20},{20... | collective-permute-start | bytes 200 | tf_op jit(solution)/shard_map/ppermute | solution.py:187
  8.3 17.2 %collective-permute-start.2 = (bf16[16,2176]{1,0:T(8,128)(2,1)}, bf16[16,2176]{1,0:T(8,128)(2,1)S(1)}, u32[]{:S(2)}, u32[]{:S(2)}) collective-permute-start(bf16[16,2176]{1,0:T(8,128)(2,1)} %get-tuple-element.46), channel_id=1, source_target_pairs={{0,6},{2,4},{4,2},{6,0},{8,14},{10,12},{12,10},{14,8},{1,7},{3,5},... | collective-permute-start | bytes 208904 | tf_op jit(solution)/shard_map/ppermute | solution.py:182
  8.6 16.8 %collective-permute-start.3 = (bf16[16,2176]{1,0:T(8,128)(2,1)}, bf16[16,2176]{1,0:T(8,128)(2,1)S(1)}, u32[]{:S(2)}, u32[]{:S(2)}) collective-permute-start(bf16[16,2176]{1,0:T(8,128)(2,1)} %get-tuple-element.47), channel_id=1, source_target_pairs={{0,8},{2,10},{4,12},{6,14},{8,0},{10,2},{12,4},{14,6},{1,9},{3,11}... | collective-permute-start | bytes 208904 | tf_op jit(solution)/shard_map/ppermute | solution.py:182
  11.2 14.2 %collective-permute-start.4 = (bf16[16,2176]{1,0:T(8,128)(2,1)}, bf16[16,2176]{1,0:T(8,128)(2,1)S(1)}, u32[]{:S(2)}, u32[]{:S(2)}) collective-permute-start(bf16[16,2176]{1,0:T(8,128)(2,1)} %get-tuple-element.48), channel_id=1, source_target_pairs={{0,10},{2,8},{4,14},{6,12},{8,2},{10,0},{12,6},{14,4},{1,11},{3,9}... | collective-permute-start | bytes 208904 | tf_op jit(solution)/shard_map/ppermute | solution.py:182
  13.1 12.4 %collective-permute-start.5 = (bf16[16,2176]{1,0:T(8,128)(2,1)}, bf16[16,2176]{1,0:T(8,128)(2,1)S(1)}, u32[]{:S(2)}, u32[]{:S(2)}) collective-permute-start(bf16[16,2176]{1,0:T(8,128)(2,1)} %get-tuple-element.49), channel_id=1, source_target_pairs={{0,12},{2,14},{4,8},{6,10},{8,4},{10,6},{12,0},{14,2},{1,13},{3,15... | collective-permute-start | bytes 208904 | tf_op jit(solution)/shard_map/ppermute | solution.py:182
  16.1 32.0 %slice-start.1 = ((s8[7340032]{0:T(1024)(128)(4,1)}), s8[3145728]{0:T(1024)(128)(4,1)S(1)}, s32[]{:S(2)}) async-start(s8[7340032]{0:T(1024)(128)(4,1)} %bitcast.5), calls=%async_computation.1 | async-start | bytes 6291456
  16.1 9.3 %collective-permute-start.6 = (bf16[16,2176]{1,0:T(8,128)(2,1)}, bf16[16,2176]{1,0:T(8,128)(2,1)S(1)}, u32[]{:S(2)}, u32[]{:S(2)}) collective-permute-start(bf16[16,2176]{1,0:T(8,128)(2,1)} %get-tuple-element.50), channel_id=1, source_target_pairs={{0,14},{2,12},{4,10},{6,8},{8,6},{10,4},{12,2},{14,0},{1,15},{3,13... | collective-permute-start | bytes 208904 | tf_op jit(solution)/shard_map/ppermute | solution.py:182
  26.2 26.2 %collective-permute-start.16 = (f32[896,256]{1,0:T(8,128)S(1)}, f32[896,256]{1,0:T(8,128)S(1)}, u32[]{:S(2)}, u32[]{:S(2)}) collective-permute-start(f32[896,256]{1,0:T(8,128)S(1)} %get-tuple-element.82), channel_id=1, source_target_pairs={{0,1},{1,0},{2,3},{3,2},{4,5},{5,4},{6,7},{7,6},{8,9},{9,8},{10,11... | collective-permute-start | bytes 2752520 | tf_op jit(solution)/shard_map/ppermute | solution.py:229
  26.3 8.4 %collective-permute-start.8 = (bf16[2,16,2176]{2,1,0:T(8,128)(2,1)S(1)}, bf16[2,16,2176]{2,1,0:T(8,128)(2,1)S(1)}, u32[]{:S(2)}, u32[]{:S(2)}) collective-permute-start(bf16[2,16,2176]{2,1,0:T(8,128)(2,1)S(1)} %get-tuple-element.71), channel_id=1, source_target_pairs={{0,22},{2,20},{4,18},{6,16},{8,30},{10,28},{12,26},{14,24},{16,6},... | collective-permute-start | bytes 417800 | tf_op jit(solution)/shard_map/ppermute | solution.py:237
  26.5 9.8 %collective-permute-start.9 = (bf16[2,16,2176]{2,1,0:T(8,128)(2,1)S(1)}, bf16[2,16,2176]{2,1,0:T(8,128)(2,1)S(1)}, u32[]{:S(2)}, u32[]{:S(2)}) collective-permute-start(bf16[2,16,2176]{2,1,0:T(8,128)(2,1)S(1)} %get-tuple-element.72), channel_id=1, source_target_pairs={{0,20},{2,22},{4,16},{6,18},{8,28},{10,30},{12,24},{14,26},{16,4},... | collective-permute-start | bytes 417800 | tf_op jit(solution)/shard_map/ppermute | solution.py:237
  29.2 13.7 %collective-permute-start.10 = (bf16[2,16,2176]{2,1,0:T(8,128)(2,1)S(1)}, bf16[2,16,2176]{2,1,0:T(8,128)(2,1)S(1)}, u32[]{:S(2)}, u32[]{:S(2)}) collective-permute-start(bf16[2,16,2176]{2,1,0:T(8,128)(2,1)S(1)} %get-tuple-element.73), channel_id=1, source_target_pairs={{0,18},{2,16},{4,22},{6,20},{8,26},{10,24},{12,30},{14,28},{16,2},... | collective-permute-start | bytes 417800 | tf_op jit(solution)/shard_map/ppermute | solution.py:237
  31.7 12.2 %collective-permute-start.11 = (bf16[2,16,2176]{2,1,0:T(8,128)(2,1)S(1)}, bf16[2,16,2176]{2,1,0:T(8,128)(2,1)S(1)}, u32[]{:S(2)}, u32[]{:S(2)}) collective-permute-start(bf16[2,16,2176]{2,1,0:T(8,128)(2,1)S(1)} %get-tuple-element.74), channel_id=1, source_target_pairs={{0,16},{2,18},{4,20},{6,22},{8,24},{10,26},{12,28},{14,30},{16,0},... | collective-permute-start | bytes 417800 | tf_op jit(solution)/shard_map/ppermute | solution.py:237
  34.7 9.2 %collective-permute-start.12 = (bf16[2,16,2176]{2,1,0:T(8,128)(2,1)S(1)}, bf16[2,16,2176]{2,1,0:T(8,128)(2,1)S(1)}, u32[]{:S(2)}, u32[]{:S(2)}) collective-permute-start(bf16[2,16,2176]{2,1,0:T(8,128)(2,1)S(1)} %get-tuple-element.75), channel_id=1, source_target_pairs={{0,6},{2,4},{4,2},{6,0},{8,14},{10,12},{12,10},{14,8},{16,22},{18,... | collective-permute-start | bytes 417800 | tf_op jit(solution)/shard_map/ppermute | solution.py:237
  36.3 7.6 %collective-permute-start.13 = (bf16[2,16,2176]{2,1,0:T(8,128)(2,1)S(1)}, bf16[2,16,2176]{2,1,0:T(8,128)(2,1)S(1)}, u32[]{:S(2)}, u32[]{:S(2)}) collective-permute-start(bf16[2,16,2176]{2,1,0:T(8,128)(2,1)S(1)} %get-tuple-element.76), channel_id=1, source_target_pairs={{0,4},{2,6},{4,0},{6,2},{8,12},{10,14},{12,8},{14,10},{16,20},{18,... | collective-permute-start | bytes 417800 | tf_op jit(solution)/shard_map/ppermute | solution.py:237
  43.0 5.2 %collective-permute-start.14 = (bf16[2,16,2176]{2,1,0:T(8,128)(2,1)S(1)}, bf16[2,16,2176]{2,1,0:T(8,128)(2,1)S(1)}, u32[]{:S(2)}, u32[]{:S(2)}) collective-permute-start(bf16[2,16,2176]{2,1,0:T(8,128)(2,1)S(1)} %get-tuple-element.77), channel_id=1, source_target_pairs={{0,2},{2,0},{4,6},{6,4},{8,10},{10,8},{12,14},{14,12},{16,18},{18,... | collective-permute-start | bytes 417800 | tf_op jit(solution)/shard_map/ppermute | solution.py:237
  50.8 1.6 %collective-permute-start.15 = (f32[4,112,128]{2,1,0:T(8,128)S(1)}, f32[4,112,128]{2,1,0:T(8,128)S(1)}, u32[]{:S(2)}, u32[]{:S(2)}) collective-permute-start(f32[4,112,128]{2,1,0:T(8,128)S(1)} %get-tuple-element.79.mine_ref), channel_id=1, source_target_pairs={{0,1},{1,0},{2,3},{3,2},{4,5},{5,4},{6,7},{7,6},{8,9},{9,8},{10,11... | collective-permute-start | bytes 688136 | tf_op jit(solution)/shard_map/ppermute | solution.py:257

commit v4 on v3

--- a/solution.py
+++ b/solution.py
@@ -10,33 +10,34 @@
 adapter_scale_factor = 0.5
 MEMBERS = 8
 PIECE_ROWS = 16
+ORDER = (1, 7, 2, 4, 3, 5, 6)
 
 ANY = pl.BlockSpec(memory_space=pl.ANY)
 SMEM = pl.BlockSpec(memory_space=pltpu.SMEM)
 VMEM = pl.BlockSpec(memory_space=pltpu.VMEM)
 
 
-def pack_kernel(near, halves, down_ref, up_ref, *refs):
-    outs, sem = refs[:-1], refs[-1]
+def pack_kernel(near, halves, down_ref, up_ref, out_ref, sem):
     member_base = lax.axis_index("rep") * near
-    low = lax.rem(lax.axis_index("grp"), near)
     tp_index = lax.axis_index("tp")
     wide = down_ref.shape[1] // halves
     up_own = up_ref.shape[1] // lax.axis_size("tp")
     up_wide = up_own // halves
     copies = []
-    for at, out in enumerate(outs):
-        member = member_base + (low ^ at % near)
+    for group in range(out_ref.shape[0]):
+        member = member_base + group % near
         rows = pl.ds(pl.multiple_of(member // halves * PIECE_ROWS, PIECE_ROWS), PIECE_ROWS)
         half = lax.rem(member, halves)
         down_at = pl.ds(pl.multiple_of(half * wide, 128), wide)
         up_at = pl.ds(pl.multiple_of(tp_index * up_own + half * up_wide, 128), up_wide)
         copies += [
             pltpu.make_async_copy(
-                down_ref.at[rows, down_at], out.at[:, pl.ds(0, wide)], sem.at[2 * at]
+                down_ref.at[rows, down_at], out_ref.at[group, :, pl.ds(0, wide)], sem.at[2 * group]
             ),
             pltpu.make_async_copy(
-                up_ref.at[rows, up_at], out.at[:, pl.ds(wide, up_wide)], sem.at[2 * at + 1]
+                up_ref.at[rows, up_at],
+                out_ref.at[group, :, pl.ds(wide, up_wide)],
+                sem.at[2 * group + 1],
             ),
         ]
     for copy in copies:
@@ -45,25 +46,22 @@
         copy.wait()
 
 
-def select_kernel(near, rep_count, part_count, home_ref, *refs):
-    wanted, refs = refs[:rep_count], refs[rep_count:]
-    held, refs = refs[:part_count], refs[part_count:]
-    outs = refs[: near * rep_count]
+def select_kernel(near, rep_count, home_ref, *refs):
+    wanted, held_ref, outs = refs[:rep_count], refs[rep_count], refs[rep_count + 1 :]
     group_index = lax.axis_index("grp")
-    slot_count = outs[0].shape[0]
     pool_size = home_ref.shape[0]
-    if part_count == 1:
-        stack = held[0]
-    else:
-        stack = refs[near * rep_count]
-        for part in range(part_count):
-            stack[part_count - 1 - part] = held[part][...]
-    for flip in range(near * rep_count):
+    for flip, out in zip((0,) + ORDER, outs):
         other = group_index ^ (flip % near)
-        for slot in range(slot_count):
+        for slot in range(out.shape[0]):
             adapter = jnp.clip(wanted[flip // near][slot, other], 0, pool_size - 1)
-            place = jnp.clip(home_ref[adapter], 0, pool_size - 1) ^ group_index
-            outs[flip][slot] = stack[place]
+            place = jnp.clip(home_ref[adapter], 0, pool_size - 1)
+            out[slot] = held_ref[place]
+
+
+def stage_kernel(x_ref, out_ref, sem):
+    copy = pltpu.make_async_copy(x_ref, out_ref, sem)
+    copy.start()
+    copy.wait()
 
 
 def base_kernel(x_ref, weight_ref, mine_ref, theirs_ref):
@@ -94,19 +92,18 @@
         store(second, first)
 
 
-def shrink_kernel(member_count, halves, rank, count_ref, x_ref, *refs):
-    pieces, refs = refs[:member_count][::-1], refs[member_count:]
-    shrunk_ref, up_ref, down = refs
+def shrink_kernel(halves, rank, count_ref, x_ref, *refs):
+    pieces, (shrunk_ref, up_ref, down) = refs[:-3], refs[-3:]
     slot_count = pieces[0].shape[0]
     wide = down.shape[1] // halves
     up_wide = up_ref.shape[1] // halves
     group_index = lax.axis_index("grp")
-    for flip in range(member_count):
+    for flip, piece in zip((0,) + ORDER, pieces):
         half = lax.rem(group_index ^ flip, halves)
         for slot in range(slot_count):
             rows = pl.ds(slot * rank + flip // halves * PIECE_ROWS, PIECE_ROWS)
-            down[rows, pl.ds(pl.multiple_of(half * wide, 128), wide)] = pieces[flip][slot, :, :wide]
-            up_ref[rows, pl.ds(pl.multiple_of(half * up_wide, 128), up_wide)] = pieces[flip][
+            down[rows, pl.ds(pl.multiple_of(half * wide, 128), wide)] = piece[slot, :, :wide]
+            up_ref[rows, pl.ds(pl.multiple_of(half * up_wide, 128), up_wide)] = piece[
                 slot, :, wide:
             ]
     rows = shrunk_ref.shape[1]
@@ -165,27 +162,34 @@
     bf16, f32 = jnp.bfloat16, jnp.float32
 
     down = jnp.swapaxes(pool_down[0], 0, 1)
-    distinct = group_count if group_count <= MEMBERS else near
-    pieces = pl.pallas_call(
+    packed = pl.pallas_call(
         functools.partial(pack_kernel, near, halves),
-        out_shape=[jax.ShapeDtypeStruct((PIECE_ROWS, piece_width), bf16)] * distinct,
+        out_shape=jax.ShapeDtypeStruct((group_count, PIECE_ROWS, piece_width), bf16),
         in_specs=[ANY, ANY],
-        out_specs=[VMEM] * distinct,
-        scratch_shapes=[pltpu.SemaphoreType.DMA((2 * distinct,))],
+        out_specs=VMEM,
+        scratch_shapes=[pltpu.SemaphoreType.DMA((2 * group_count,))],
         compiler_params=pltpu.CompilerParams(vmem_limit_bytes=56 << 20),
         name="pack",
     )(down, pool_up[0])
-
-    held = [pieces[0]] + [None] * (group_count - 1)
-    for flip in range(group_count - 1, 0, -1):
-        pairs = [(g, g ^ flip) for g in range(group_count)]
-        held[flip] = lax.ppermute(pieces[flip % distinct], "grp", pairs)
+    held = lax.all_to_all(packed, "grp", 0, 0, tiled=True)
     asked = jnp.swapaxes(block_adapter, 0, 1)
     wanted = [asked]
     for flip in range(1, rep_count):
         pairs = [(r, r ^ flip) for r in range(rep_count)]
         wanted.append(lax.ppermute(asked, "rep", pairs))
 
+    near_hidden = pl.pallas_call(
+        stage_kernel,
+        out_shape=pltpu.VMEM(hidden.shape, bf16),
+        in_specs=[ANY],
+        out_specs=VMEM,
+        scratch_shapes=[pltpu.SemaphoreType.DMA(())],
+        compiler_params=pltpu.CompilerParams(vmem_limit_bytes=40 << 20),
+        cost_estimate=pl.CostEstimate(
+            flops=0, bytes_accessed=4 * hidden.size, transcendentals=0
+        ),
+        name="stage",
+    )(hidden)
     chunk_count = 4
     chunk = half_width // chunk_count
     rows = step_count * row_count
@@ -198,47 +202,40 @@
             pl.BlockSpec((chunk, col_count), lambda k: (k, 0)),
         ],
         out_specs=[pl.BlockSpec((rows, share), lambda k: (0, 0))] * 2,
-        compiler_params=pltpu.CompilerParams(vmem_limit_bytes=52 << 20),
+        compiler_params=pltpu.CompilerParams(vmem_limit_bytes=40 << 20),
         cost_estimate=pl.CostEstimate(
             flops=2 * rows * half_width * col_count,
             bytes_accessed=2 * rows * (half_width + 4 * share),
             transcendentals=0,
         ),
         name="base",
-    )(hidden, base_weight)
-    held[1:], wanted[1:], mine, theirs = lax.optimization_barrier(
-        (held[1:], wanted[1:], mine, theirs)
+    )(near_hidden, base_weight)
+    swap = [(0, 1), (1, 0)]
+    base_other = lax.ppermute(theirs, "tp", swap)
+    held, wanted[1:], mine, base_other = lax.optimization_barrier(
+        (held, wanted[1:], mine, base_other)
     )
 
-    if group_count <= MEMBERS:
-        parts = held[::-1]
-        stack = [pltpu.VMEM((group_count, PIECE_ROWS, piece_width), bf16)]
-    else:
-        parts, stack = [jnp.stack(held)], []
     sends = pl.pallas_call(
-        functools.partial(select_kernel, near, rep_count, len(parts)),
+        functools.partial(select_kernel, near, rep_count),
         out_shape=[jax.ShapeDtypeStruct((slot_count, PIECE_ROWS, piece_width), bf16)] * MEMBERS,
-        in_specs=[SMEM] * (1 + rep_count) + [VMEM] * len(parts),
+        in_specs=[SMEM] * (1 + rep_count) + [VMEM],
         out_specs=[VMEM] * MEMBERS,
-        scratch_shapes=stack,
-        compiler_params=pltpu.CompilerParams(vmem_limit_bytes=24 << 20),
+        compiler_params=pltpu.CompilerParams(vmem_limit_bytes=12 << 20),
         name="select",
-    )(adapter_home, *wanted, *parts)
-    swap = [(0, 1), (1, 0)]
-    theirs, sends = lax.optimization_barrier((theirs, sends))
-    base_other = lax.ppermute(theirs, "tp", swap)
-    got = [sends[0]] + [None] * (MEMBERS - 1)
-    for flip in range(MEMBERS - 1, 0, -1):
+    )(adapter_home, *wanted, held)
+    got = []
+    for flip, send in zip(ORDER, sends[1:]):
         pairs = [
             (r * group_count + g, (r ^ flip // near) * group_count + (g ^ flip % near))
             for r in range(rep_count)
             for g in range(group_count)
         ]
-        got[flip] = lax.ppermute(sends[flip], ("rep", "grp"), pairs)
+        got.append(lax.ppermute(send, ("rep", "grp"), pairs))
 
     both = slot_count * rank
     shrunk, up = pl.pallas_call(
-        functools.partial(shrink_kernel, MEMBERS, halves, rank),
+        functools.partial(shrink_kernel, halves, rank),
         out_shape=[
             jax.ShapeDtypeStruct((step_count, block_rows, both), f32),
             jax.ShapeDtypeStruct((both, share), bf16),
@@ -246,14 +243,14 @@
         in_specs=[SMEM] + [VMEM] * (1 + MEMBERS),
         out_specs=[VMEM, VMEM],
         scratch_shapes=[pltpu.VMEM((both, half_width), bf16)],
-        compiler_params=pltpu.CompilerParams(vmem_limit_bytes=24 << 20),
+        compiler_params=pltpu.CompilerParams(vmem_limit_bytes=12 << 20),
         cost_estimate=pl.CostEstimate(
-            flops=2 * step_count * row_count * half_width * both,
-            bytes_accessed=2 * step_count * row_count * half_width,
+            flops=2 * rows * half_width * both,
+            bytes_accessed=2 * rows * half_width,
             transcendentals=0,
         ),
         name="shrink",
-    )(block_count, hidden, *got[::-1])
+    )(block_count, near_hidden, sends[0], *got)
     shrunk_other = lax.ppermute(shrunk, "tp", swap)
 
     return pl.pallas_call(
@@ -265,7 +262,7 @@
             pltpu.VMEM((step_count, row_count, share), bf16),
             pltpu.SemaphoreType.DMA((step_count,)),
         ],
-        compiler_params=pltpu.CompilerParams(vmem_limit_bytes=24 << 20),
+        compiler_params=pltpu.CompilerParams(vmem_limit_bytes=12 << 20),
         name="expand",
     )(shrunk, shrunk_other, up, mine, base_other)
 

time: 53.7 us -> 53.1 us (0.989)
  waiting for transfers between devices: 16.4 us -> 8.53 us
  local copies, waits for them, and re-layouts: 0.03 us -> 7.07 us
  Pallas kernels: 14.1 us -> 15.4 us
  starting transfers between devices: 22.8 us -> 21.7 us
    ppermute x14 -> x7, waiting for transfers between devices: 15 us -> 4.97 us  [local(): got.append(lax.ppermute(send, ('rep', 'grp'), pairs))]
    ppermute x14 -> x7, starting transfers between devices: 21.1 us -> 12.9 us  [local(): got.append(lax.ppermute(send, ('rep', 'grp'), pairs))]
    all_to_all x0 -> x1, starting transfers between devices: none -> 7.29 us  [local(): held = lax.all_to_all(packed, 'grp', 0, 0, tiled=True)]
    unnamed x12, local copies, waits for them, and re-layouts: 0.03 us -> 7.07 us
    pallas_call x3 -> x4, Pallas kernels: 5.42 us -> 8.68 us  [the longest x1 3.24 us: local(): pl.pallas_call(stage_kernel, out_shape=pltpu.VMEM(hidden.shape, bf16), in...]
    ppermute x1, waiting for transfers between devices: 0.01 us -> 2.08 us  [local(): wanted.append(lax.ppermute(asked, 'rep', pairs))]
    pallas_call x1, Pallas kernels: 7.56 us -> 5.65 us  [local(): pl.pallas_call(base_kernel, grid=(chunk_count,), out_shape=[jax.ShapeDtyp...]
  transfers between devices with their start and end apart: 17 -> 11, of which waited for: 6 -> 4; matrix products, arithmetic and copies ran while one was open for 0% -> 0% of each run, Pallas kernels for 19% -> 17%
where the time goes in v4:
time: 53.1 us; the launch traced here: 52.9 us
  starting transfers between devices  21.7 us (41%)
  Pallas kernels  15.4 us (29%)
  waiting for transfers between devices  8.53 us (16%)
  local copies, waits for them, and re-layouts  7.07 us (13%)
    ppermute x7, starting transfers between devices, local(): got.append(lax.ppermute(send, ('rep', 'grp'), pairs))  12.9 us
    all_to_all x1, starting transfers between devices, local(): held = lax.all_to_all(packed, 'grp', 0, 0, tiled=True)  7.29 us
    unnamed x12, local copies, waits for them, and re-layouts  7.07 us
    pallas_call x1, Pallas kernels, local(): pl.pallas_call(base_kernel, grid=(chunk_count,), out_shape=[jax.ShapeDtyp...  5.65 us
    ppermute x7, waiting for transfers between devices, local(): got.append(lax.ppermute(send, ('rep', 'grp'), pairs))  4.97 us
    pallas_call x1, Pallas kernels, local(): pl.pallas_call(stage_kernel, out_shape=pltpu.VMEM(hidden.shape, bf16), in...  3.24 us
    pallas_call x1, Pallas kernels, local(): pl.pallas_call(functools.partial(shrink_kernel, halves, rank), out_shape=...  2.67 us
    pallas_call x1, Pallas kernels, local(): pl.pallas_call(functools.partial(pack_kernel, near, halves), out_shape=ja...  2.09 us
  transfers between devices with their start and end apart: 11, of which 4 were waited for; matrix products, arithmetic and copies ran while one was open for 0% of the time, Pallas kernels for 17%

profile of v4, /device:TPU:0, one launch (start us, length us, event | category | flops | bytes accessed | tf_op | source)
XLA Modules:
  0.0 52.9 jit_solution(6352326110721934787)
XLA Ops:
  0.0 2.1 %pack.1 = bf16[8,16,2176]{2,1,0:T(8,128)(2,1)} custom-call(bf16[64,4096]{1,0:T(8,128)(2,1)} %bitcast.7, bf16[64,512]{1,0:T(8,128)(2,1)} %bitcast.8), custom_call_target="tpu_custom_call" | custom-call | tf_op jit(solution)/shard_map/pack/pallas_call | solution.py:165
  2.1 7.3 %all-to-all-start = ((bf16[8,16,2176]{2,1,0:T(8,128)(2,1)}), bf16[8,16,2176]{2,1,0:T(8,128)(2,1)S(1)}, u32[]{:S(2)}, u32[]{:S(2)}) async-start(bf16[8,16,2176]{2,1,0:T(8,128)(2,1)} %pack.1), calls=%async_computation | async-start | bytes 1114112 | tf_op jit(solution)/shard_map/all_to_all | solution.py:174
  9.4 3.2 %stage.1.x_ref = bf16[4,224,4096]{2,1,0:T(8,128)(2,1)S(1)} custom-call(bf16[4,224,4096]{2,1,0:T(8,128)(2,1)} %x_ref.1), custom_call_target="tpu_custom_call" | custom-call | bytes 14680064 | tf_op jit(solution)/shard_map/stage/pallas_call | solution.py:181
  12.6 1.0 %copy-done.5 = bf16[4096,512]{1,0:T(8,128)(2,1)S(1)} copy-done((bf16[4096,512]{1,0:T(8,128)(2,1)S(1)}, bf16[4096,512]{1,0:T(8,128)(2,1)}, u32[]{:S(2)}) %copy-start.5) | copy-done | bytes 4194328
  13.7 5.7 %base.1 = (f32[896,256]{1,0:T(8,128)S(1)}, f32[896,256]{1,0:T(8,128)S(1)}) custom-call(bf16[4,224,4096]{2,1,0:T(8,128)(2,1)S(1)} %stage.1.x_ref, bf16[4096,512]{1,0:T(8,128)(2,1)S(1)} %copy-done.5), custom_call_target="tpu_custom_call" | custom-call | flops 3758096384 | bytes 9175040 | tf_op jit(solution)/shard_map/base/pallas_call | solution.py:196
  19.3 2.9 %copy-done = bf16[4,224,4096]{2,1,0:T(8,128)(2,1)} copy-done((bf16[4,224,4096]{2,1,0:T(8,128)(2,1)}, bf16[4,224,4096]{2,1,0:T(8,128)(2,1)S(1)}, u32[]{:S(2)}) %copy-start) | copy-done | bytes 7340056
  22.3 1.5 %collective-permute-start = (s32[2,8]{1,0:T(2,128)S(1)}, s32[2,8]{1,0:T(2,128)S(1)}, u32[]{:S(2)}, u32[]{:S(2)}) collective-permute-start(s32[2,8]{1,0:T(2,128)S(1)} %bitcast.5), channel_id=1, source_target_pairs={{0,16},{16,0},{1,17},{17,1},{2,18},{18,2},{3,19},{19,3},{4,20},{20... | collective-permute-start | bytes 200 | tf_op jit(solution)/shard_map/ppermute | solution.py:179
  23.8 2.1 %collective-permute-done.refs_1_ = s32[2,8]{1,0:T(2,128)S(1)} collective-permute-done((s32[2,8]{1,0:T(2,128)S(1)}, s32[2,8]{1,0:T(2,128)S(1)}, u32[]{:S(2)}, u32[]{:S(2)}) %collective-permute-start) | collective-permute-done | bytes 96 | tf_op jit(solution)/shard_map/ppermute | solution.py:179
  25.9 0.0 collective-permute-done.1.base_other_ref
  25.9 0.7 %select.1 = (bf16[2,16,2176]{2,1,0:T(8,128)(2,1)S(1)}, bf16[2,16,2176]{2,1,0:T(8,128)(2,1)S(1)}, bf16[2,16,2176]{2,1,0:T(8,128)(2,1)S(1)}, bf16[2,16,2176]{2,1,0...) custom-call(s32[8]{0:T(128)S(1)} %copy-done.3, ...), custom_call_target="tpu_custom_call" | custom-call | tf_op jit(solution)/shard_map/select/pallas_call | solution.py:219
  26.6 2.1 %collective-permute-start.2 = (bf16[2,16,2176]{2,1,0:T(8,128)(2,1)S(1)}, bf16[2,16,2176]{2,1,0:T(8,128)(2,1)S(1)}, u32[]{:S(2)}, u32[]{:S(2)}) collective-permute-start(bf16[2,16,2176]{2,1,0:T(8,128)(2,1)S(1)} %get-tuple-element.26), channel_id=1, source_target_pairs={{0,2},{2,0},{4,6},{6,4},{8,10},{10,8},{12,14},{14,12},{16,18},{18,... | collective-permute-start | bytes 417800 | tf_op jit(solution)/shard_map/ppermute | solution.py:234
  28.7 2.4 %collective-permute-start.3 = (bf16[2,16,2176]{2,1,0:T(8,128)(2,1)S(1)}, bf16[2,16,2176]{2,1,0:T(8,128)(2,1)S(1)}, u32[]{:S(2)}, u32[]{:S(2)}) collective-permute-start(bf16[2,16,2176]{2,1,0:T(8,128)(2,1)S(1)} %get-tuple-element.27), channel_id=1, source_target_pairs={{0,22},{2,20},{4,18},{6,16},{8,30},{10,28},{12,26},{14,24},{16,6},... | collective-permute-start | bytes 417800 | tf_op jit(solution)/shard_map/ppermute | solution.py:234
  31.0 0.1 collective-permute-start.4
  31.1 0.5 %collective-permute-start.5 = (bf16[2,16,2176]{2,1,0:T(8,128)(2,1)S(1)}, bf16[2,16,2176]{2,1,0:T(8,128)(2,1)S(1)}, u32[]{:S(2)}, u32[]{:S(2)}) collective-permute-start(bf16[2,16,2176]{2,1,0:T(8,128)(2,1)S(1)} %get-tuple-element.29), channel_id=1, source_target_pairs={{0,16},{2,18},{4,20},{6,22},{8,24},{10,26},{12,28},{14,30},{16,0},... | collective-permute-start | bytes 417800 | tf_op jit(solution)/shard_map/ppermute | solution.py:234
  31.7 2.8 %collective-permute-start.6 = (bf16[2,16,2176]{2,1,0:T(8,128)(2,1)S(1)}, bf16[2,16,2176]{2,1,0:T(8,128)(2,1)S(1)}, u32[]{:S(2)}, u32[]{:S(2)}) collective-permute-start(bf16[2,16,2176]{2,1,0:T(8,128)(2,1)S(1)} %get-tuple-element.30), channel_id=1, source_target_pairs={{0,6},{2,4},{4,2},{6,0},{8,14},{10,12},{12,10},{14,8},{16,22},{18,... | collective-permute-start | bytes 417800 | tf_op jit(solution)/shard_map/ppermute | solution.py:234
  34.5 4.0 %collective-permute-start.7 = (bf16[2,16,2176]{2,1,0:T(8,128)(2,1)S(1)}, bf16[2,16,2176]{2,1,0:T(8,128)(2,1)S(1)}, u32[]{:S(2)}, u32[]{:S(2)}) collective-permute-start(bf16[2,16,2176]{2,1,0:T(8,128)(2,1)S(1)} %get-tuple-element.31), channel_id=1, source_target_pairs={{0,18},{2,16},{4,22},{6,20},{8,26},{10,24},{12,30},{14,28},{16,2},... | collective-permute-start | bytes 417800 | tf_op jit(solution)/shard_map/ppermute | solution.py:234
  38.5 1.0 %collective-permute-start.8 = (bf16[2,16,2176]{2,1,0:T(8,128)(2,1)S(1)}, bf16[2,16,2176]{2,1,0:T(8,128)(2,1)S(1)}, u32[]{:S(2)}, u32[]{:S(2)}) collective-permute-start(bf16[2,16,2176]{2,1,0:T(8,128)(2,1)S(1)} %get-tuple-element.32), channel_id=1, source_target_pairs={{0,20},{2,22},{4,16},{6,18},{8,28},{10,30},{12,24},{14,26},{16,4},... | collective-permute-start | bytes 417800 | tf_op jit(solution)/shard_map/ppermute | solution.py:234
  39.5 3.6 %collective-permute-done.6.refs_5_ = bf16[2,16,2176]{2,1,0:T(8,128)(2,1)S(1)} collective-permute-done((bf16[2,16,2176]{2,1,0:T(8,128)(2,1)S(1)}, bf16[2,16,2176]{2,1,0:T(8,128)(2,1)S(1)}, u32[]{:S(2)}, u32[]{:S(2)}) %collective-permute-start.6) | collective-permute-done | bytes 139296 | tf_op jit(solution)/shard_map/ppermute | solution.py:234
  43.1 1.4 %collective-permute-done.8.refs_7_ = bf16[2,16,2176]{2,1,0:T(8,128)(2,1)S(1)} collective-permute-done((bf16[2,16,2176]{2,1,0:T(8,128)(2,1)S(1)}, bf16[2,16,2176]{2,1,0:T(8,128)(2,1)S(1)}, u32[]{:S(2)}, u32[]{:S(2)}) %collective-permute-start.8) | collective-permute-done | bytes 139296 | tf_op jit(solution)/shard_map/ppermute | solution.py:234
  44.4 3.1 %copy-done.1 = bf16[4,224,4096]{2,1,0:T(8,128)(2,1)S(1)} copy-done((bf16[4,224,4096]{2,1,0:T(8,128)(2,1)S(1)}, bf16[4,224,4096]{2,1,0:T(8,128)(2,1)}, u32[]{:S(2)}) %copy-start.1) | copy-done | bytes 7340056
  47.5 2.7 %shrink.1 = (f32[4,112,128]{2,1,0:T(8,128)S(1)}, bf16[128,256]{1,0:T(8,128)(2,1)S(1)}) custom-call(s32[8]{0:T(128)S(1)} %copy-done.4, bf16[4,224,4096]{2,1,0:T(8,128)(2,1)S(1)} %copy-done.1, bf16[2,16,2176]{2,1,0:T(8,128)(2,1)S(1)} %get-tuple-element.25.refs_0_, bf16[2,16,2176]{2,1,0:T(8,128)(2,1)S(1)} %collective-permute-done.2.refs_1_, ...), custom_call_target="tpu_custom_call" | custom-call | flops 939524096 | bytes 7340032 | tf_op jit(solution)/shard_map/shrink/pallas_call | solution.py:237
  50.2 0.1 collective-permute-start.9
  50.3 1.5 %collective-permute-done.9.theirs_ref = f32[4,112,128]{2,1,0:T(8,128)S(1)} collective-permute-done((f32[4,112,128]{2,1,0:T(8,128)S(1)}, f32[4,112,128]{2,1,0:T(8,128)S(1)}, u32[]{:S(2)}, u32[]{:S(2)}) %collective-permute-start.9) | collective-permute-done | bytes 229408 | tf_op jit(solution)/shard_map/ppermute | solution.py:254
  51.7 1.1 %expand.1 = bf16[4,224,256]{2,1,0:T(8,128)(2,1)} custom-call(f32[4,112,128]{2,1,0:T(8,128)S(1)} %get-tuple-element.33.mine_ref, f32[4,112,128]{2,1,0:T(8,128)S(1)} %collective-permute-done.9.theirs_ref, bf16[128,256]{1,0:T(8,128)(2,1)S(1)} %get-tuple-element.34.up_ref, f32[896,256]{1,0:T(8,128)S(1)} %get-tuple-element.35.base_ref, ...), custom_call_target="tpu_custom_call" | custom-call | tf_op jit(solution)/shard_map/expand/pallas_call | solution.py:256
  (16 shorter events, 0.0 us)
Async XLA Ops:
  2.1 23.8 %all-to-all-start = ((bf16[8,16,2176]{2,1,0:T(8,128)(2,1)}), bf16[8,16,2176]{2,1,0:T(8,128)(2,1)S(1)}, u32[]{:S(2)}, u32[]{:S(2)}) async-start(bf16[8,16,2176]{2,1,0:T(8,128)(2,1)} %pack.1), calls=%async_computation | async-start | bytes 1114112 | tf_op jit(solution)/shard_map/all_to_all | solution.py:174
  9.4 4.3 %copy-start.5 = (bf16[4096,512]{1,0:T(8,128)(2,1)S(1)}, bf16[4096,512]{1,0:T(8,128)(2,1)}, u32[]{:S(2)}) copy-start(bf16[4096,512]{1,0:T(8,128)(2,1)} %weight_ref.1) | copy-start | bytes 12582916
  13.7 8.6 %copy-start.2 = (s32[8,2]{0,1:T(2,128)S(1)}, s32[8,2]{0,1:T(2,128)}, u32[]{:S(2)}) copy-start(s32[8,2]{0,1:T(2,128)} %param.12) | copy-start | bytes 196
  13.7 12.2 %copy-start.3 = (s32[8]{0:T(128)S(1)}, s32[8]{0:T(128)}, u32[]{:S(2)}) copy-start(s32[8]{0:T(128)} %home_ref.1) | copy-start | bytes 100
  13.7 30.7 %copy-start.4 = (s32[8]{0:T(128)S(1)}, s32[8]{0:T(128)}, u32[]{:S(2)}) copy-start(s32[8]{0:T(128)} %count_ref.1) | copy-start | bytes 100
  19.3 3.0 %copy-start = (bf16[4,224,4096]{2,1,0:T(8,128)(2,1)}, bf16[4,224,4096]{2,1,0:T(8,128)(2,1)S(1)}, u32[]{:S(2)}) copy-start(bf16[4,224,4096]{2,1,0:T(8,128)(2,1)S(1)} %stage.1.x_ref) | copy-start | bytes 22020100
  22.3 3.6 %collective-permute-start.1 = (f32[896,256]{1,0:T(8,128)S(1)}, f32[896,256]{1,0:T(8,128)S(1)}, u32[]{:S(2)}, u32[]{:S(2)}) collective-permute-start(f32[896,256]{1,0:T(8,128)S(1)} %get-tuple-element.22), channel_id=1, source_target_pairs={{0,1},{1,0},{2,3},{3,2},{4,5},{5,4},{6,7},{7,6},{8,9},{9,8},{10,11... | collective-permute-start | bytes 2752520 | tf_op jit(solution)/shard_map/ppermute | solution.py:214
  22.3 3.6 %collective-permute-start = (s32[2,8]{1,0:T(2,128)S(1)}, s32[2,8]{1,0:T(2,128)S(1)}, u32[]{:S(2)}, u32[]{:S(2)}) collective-permute-start(s32[2,8]{1,0:T(2,128)S(1)} %bitcast.5), channel_id=1, source_target_pairs={{0,16},{16,0},{1,17},{17,1},{2,18},{18,2},{3,19},{19,3},{4,20},{20... | collective-permute-start | bytes 200 | tf_op jit(solution)/shard_map/ppermute | solution.py:179
  26.6 7.9 %collective-permute-start.2 = (bf16[2,16,2176]{2,1,0:T(8,128)(2,1)S(1)}, bf16[2,16,2176]{2,1,0:T(8,128)(2,1)S(1)}, u32[]{:S(2)}, u32[]{:S(2)}) collective-permute-start(bf16[2,16,2176]{2,1,0:T(8,128)(2,1)S(1)} %get-tuple-element.26), channel_id=1, source_target_pairs={{0,2},{2,0},{4,6},{6,4},{8,10},{10,8},{12,14},{14,12},{16,18},{18,... | collective-permute-start | bytes 417800 | tf_op jit(solution)/shard_map/ppermute | solution.py:234
  28.7 9.8 %collective-permute-start.3 = (bf16[2,16,2176]{2,1,0:T(8,128)(2,1)S(1)}, bf16[2,16,2176]{2,1,0:T(8,128)(2,1)S(1)}, u32[]{:S(2)}, u32[]{:S(2)}) collective-permute-start(bf16[2,16,2176]{2,1,0:T(8,128)(2,1)S(1)} %get-tuple-element.27), channel_id=1, source_target_pairs={{0,22},{2,20},{4,18},{6,16},{8,30},{10,28},{12,26},{14,24},{16,6},... | collective-permute-start | bytes 417800 | tf_op jit(solution)/shard_map/ppermute | solution.py:234
  31.0 8.4 %collective-permute-start.4 = (bf16[2,16,2176]{2,1,0:T(8,128)(2,1)S(1)}, bf16[2,16,2176]{2,1,0:T(8,128)(2,1)S(1)}, u32[]{:S(2)}, u32[]{:S(2)}) collective-permute-start(bf16[2,16,2176]{2,1,0:T(8,128)(2,1)S(1)} %get-tuple-element.28), channel_id=1, source_target_pairs={{0,4},{2,6},{4,0},{6,2},{8,12},{10,14},{12,8},{14,10},{16,20},{18,... | collective-permute-start | bytes 417800 | tf_op jit(solution)/shard_map/ppermute | solution.py:234
  31.1 8.3 %collective-permute-start.5 = (bf16[2,16,2176]{2,1,0:T(8,128)(2,1)S(1)}, bf16[2,16,2176]{2,1,0:T(8,128)(2,1)S(1)}, u32[]{:S(2)}, u32[]{:S(2)}) collective-permute-start(bf16[2,16,2176]{2,1,0:T(8,128)(2,1)S(1)} %get-tuple-element.29), channel_id=1, source_target_pairs={{0,16},{2,18},{4,20},{6,22},{8,24},{10,26},{12,28},{14,30},{16,0},... | collective-permute-start | bytes 417800 | tf_op jit(solution)/shard_map/ppermute | solution.py:234
  31.7 11.4 %collective-permute-start.6 = (bf16[2,16,2176]{2,1,0:T(8,128)(2,1)S(1)}, bf16[2,16,2176]{2,1,0:T(8,128)(2,1)S(1)}, u32[]{:S(2)}, u32[]{:S(2)}) collective-permute-start(bf16[2,16,2176]{2,1,0:T(8,128)(2,1)S(1)} %get-tuple-element.30), channel_id=1, source_target_pairs={{0,6},{2,4},{4,2},{6,0},{8,14},{10,12},{12,10},{14,8},{16,22},{18,... | collective-permute-start | bytes 417800 | tf_op jit(solution)/shard_map/ppermute | solution.py:234
  34.5 8.5 %collective-permute-start.7 = (bf16[2,16,2176]{2,1,0:T(8,128)(2,1)S(1)}, bf16[2,16,2176]{2,1,0:T(8,128)(2,1)S(1)}, u32[]{:S(2)}, u32[]{:S(2)}) collective-permute-start(bf16[2,16,2176]{2,1,0:T(8,128)(2,1)S(1)} %get-tuple-element.31), channel_id=1, source_target_pairs={{0,18},{2,16},{4,22},{6,20},{8,26},{10,24},{12,30},{14,28},{16,2},... | collective-permute-start | bytes 417800 | tf_op jit(solution)/shard_map/ppermute | solution.py:234
  38.5 6.0 %collective-permute-start.8 = (bf16[2,16,2176]{2,1,0:T(8,128)(2,1)S(1)}, bf16[2,16,2176]{2,1,0:T(8,128)(2,1)S(1)}, u32[]{:S(2)}, u32[]{:S(2)}) collective-permute-start(bf16[2,16,2176]{2,1,0:T(8,128)(2,1)S(1)} %get-tuple-element.32), channel_id=1, source_target_pairs={{0,20},{2,22},{4,16},{6,18},{8,28},{10,30},{12,24},{14,26},{16,4},... | collective-permute-start | bytes 417800 | tf_op jit(solution)/shard_map/ppermute | solution.py:234
  44.4 3.1 %copy-start.1 = (bf16[4,224,4096]{2,1,0:T(8,128)(2,1)S(1)}, bf16[4,224,4096]{2,1,0:T(8,128)(2,1)}, u32[]{:S(2)}) copy-start(bf16[4,224,4096]{2,1,0:T(8,128)(2,1)} %copy-done) | copy-start | bytes 22020100
  50.2 1.6 %collective-permute-start.9 = (f32[4,112,128]{2,1,0:T(8,128)S(1)}, f32[4,112,128]{2,1,0:T(8,128)S(1)}, u32[]{:S(2)}, u32[]{:S(2)}) collective-permute-start(f32[4,112,128]{2,1,0:T(8,128)S(1)} %get-tuple-element.33.mine_ref), channel_id=1, source_target_pairs={{0,1},{1,0},{2,3},{3,2},{4,5},{5,4},{6,7},{7,6},{8,9},{9,8},{10,11... | collective-permute-start | bytes 688136 | tf_op jit(solution)/shard_map/ppermute | solution.py:254

commit v5 on v4

--- a/solution.py
+++ b/solution.py
@@ -164,7 +164,7 @@
     down = jnp.swapaxes(pool_down[0], 0, 1)
     packed = pl.pallas_call(
         functools.partial(pack_kernel, near, halves),
-        out_shape=jax.ShapeDtypeStruct((group_count, PIECE_ROWS, piece_width), bf16),
+        out_shape=pltpu.VMEM((group_count, PIECE_ROWS, piece_width), bf16),
         in_specs=[ANY, ANY],
         out_specs=VMEM,
         scratch_shapes=[pltpu.SemaphoreType.DMA((2 * group_count,))],
@@ -178,18 +178,6 @@
         pairs = [(r, r ^ flip) for r in range(rep_count)]
         wanted.append(lax.ppermute(asked, "rep", pairs))
 
-    near_hidden = pl.pallas_call(
-        stage_kernel,
-        out_shape=pltpu.VMEM(hidden.shape, bf16),
-        in_specs=[ANY],
-        out_specs=VMEM,
-        scratch_shapes=[pltpu.SemaphoreType.DMA(())],
-        compiler_params=pltpu.CompilerParams(vmem_limit_bytes=40 << 20),
-        cost_estimate=pl.CostEstimate(
-            flops=0, bytes_accessed=4 * hidden.size, transcendentals=0
-        ),
-        name="stage",
-    )(hidden)
     chunk_count = 4
     chunk = half_width // chunk_count
     rows = step_count * row_count
@@ -202,14 +190,14 @@
             pl.BlockSpec((chunk, col_count), lambda k: (k, 0)),
         ],
         out_specs=[pl.BlockSpec((rows, share), lambda k: (0, 0))] * 2,
-        compiler_params=pltpu.CompilerParams(vmem_limit_bytes=40 << 20),
+        compiler_params=pltpu.CompilerParams(vmem_limit_bytes=52 << 20),
         cost_estimate=pl.CostEstimate(
             flops=2 * rows * half_width * col_count,
             bytes_accessed=2 * rows * (half_width + 4 * share),
             transcendentals=0,
         ),
         name="base",
-    )(near_hidden, base_weight)
+    )(hidden, base_weight)
     swap = [(0, 1), (1, 0)]
     base_other = lax.ppermute(theirs, "tp", swap)
     held, wanted[1:], mine, base_other = lax.optimization_barrier(
@@ -232,6 +220,20 @@
             for g in range(group_count)
         ]
         got.append(lax.ppermute(send, ("rep", "grp"), pairs))
+
+    late, own = lax.optimization_barrier((hidden, sends[0]))
+    near_hidden = pl.pallas_call(
+        stage_kernel,
+        out_shape=pltpu.VMEM(hidden.shape, bf16),
+        in_specs=[ANY],
+        out_specs=VMEM,
+        scratch_shapes=[pltpu.SemaphoreType.DMA(())],
+        compiler_params=pltpu.CompilerParams(vmem_limit_bytes=48 << 20),
+        cost_estimate=pl.CostEstimate(
+            flops=0, bytes_accessed=4 * hidden.size, transcendentals=0
+        ),
+        name="stage",
+    )(late)
 
     both = slot_count * rank
     shrunk, up = pl.pallas_call(
@@ -250,7 +252,7 @@
             transcendentals=0,
         ),
         name="shrink",
-    )(block_count, near_hidden, sends[0], *got)
+    )(block_count, near_hidden, own, *got)
     shrunk_other = lax.ppermute(shrunk, "tp", swap)
 
     return pl.pallas_call(

time: 53.1 us -> 50.1 us (0.944)
  local copies, waits for them, and re-layouts: 7.07 us -> 0.02 us
  waiting for transfers between devices: 8.53 us -> 11 us
  Pallas kernels: 15.4 us -> 17.2 us
    unnamed x12 -> x6, local copies, waits for them, and re-layouts: 7.07 us -> 0.02 us
    all_to_all x1, waiting for transfers between devices: 0.01 us -> 3.89 us  [local(): held = lax.all_to_all(packed, 'grp', 0, 0, tiled=True)]
    pallas_call x1, Pallas kernels: 5.65 us -> 7.56 us  [local(): pl.pallas_call(base_kernel, grid=(chunk_count,), out_shape=[jax.ShapeDtyp...]
    ppermute x7, waiting for transfers between devices: 4.97 us -> 3.51 us  [local(): got.append(lax.ppermute(send, ('rep', 'grp'), pairs))]
  transfers between devices with their start and end apart: 11 -> 11, of which waited for: 4 -> 6; matrix products, arithmetic and copies ran while one was open for 0% -> 0% of each run, Pallas kernels for 17% -> 21%
where the time goes in v5:
time: 50.1 us; the launch traced here: 49.7 us
  starting transfers between devices  21.5 us (43%)
  Pallas kernels  17.2 us (34%)
  waiting for transfers between devices  11 us (22%)
    ppermute x7, starting transfers between devices, local(): got.append(lax.ppermute(send, ('rep', 'grp'), pairs))  12.5 us
    pallas_call x1, Pallas kernels, local(): pl.pallas_call(base_kernel, grid=(chunk_count,), out_shape=[jax.ShapeDtyp...  7.56 us
    all_to_all x1, starting transfers between devices, local(): held = lax.all_to_all(packed, 'grp', 0, 0, tiled=True)  7.29 us
    all_to_all x1, waiting for transfers between devices, local(): held = lax.all_to_all(packed, 'grp', 0, 0, tiled=True)  3.89 us
    ppermute x7, waiting for transfers between devices, local(): got.append(lax.ppermute(send, ('rep', 'grp'), pairs))  3.51 us
    pallas_call x1, Pallas kernels, local(): pl.pallas_call(stage_kernel, out_shape=pltpu.VMEM(hidden.shape, bf16), in...  3.1 us
    pallas_call x1, Pallas kernels, local(): pl.pallas_call(functools.partial(shrink_kernel, halves, rank), out_shape=...  2.65 us
    pallas_call x1, Pallas kernels, local(): pl.pallas_call(functools.partial(pack_kernel, near, halves), out_shape=pl...  2.09 us
  transfers between devices with their start and end apart: 11, of which 6 were waited for; matrix products, arithmetic and copies ran while one was open for 0% of the time, Pallas kernels for 21%

profile of v5, /device:TPU:0, one launch (start us, length us, event | category | flops | bytes accessed | tf_op | source)
XLA Modules:
  0.0 49.7 jit_solution(18234228765696665693)
XLA Ops:
  0.0 2.1 %pack.1 = bf16[8,16,2176]{2,1,0:T(8,128)(2,1)} custom-call(bf16[64,4096]{1,0:T(8,128)(2,1)} %bitcast.7, bf16[64,512]{1,0:T(8,128)(2,1)} %bitcast.8), custom_call_target="tpu_custom_call" | custom-call | tf_op jit(solution)/shard_map/pack/pallas_call | solution.py:165
  2.1 0.0 copy-start
  2.1 0.0 copy-start.1
  2.1 7.3 %all-to-all-start = ((bf16[8,16,2176]{2,1,0:T(8,128)(2,1)}), bf16[8,16,2176]{2,1,0:T(8,128)(2,1)S(1)}, u32[]{:S(2)}, u32[]{:S(2)}) async-start(bf16[8,16,2176]{2,1,0:T(8,128)(2,1)} %pack.1), calls=%async_computation | async-start | bytes 1114112 | tf_op jit(solution)/shard_map/all_to_all | solution.py:174
  9.4 7.6 %base.1 = (f32[896,256]{1,0:T(8,128)S(1)}, f32[896,256]{1,0:T(8,128)S(1)}) custom-call(bf16[4,224,4096]{2,1,0:T(8,128)(2,1)} %x_ref.2, bf16[4096,512]{1,0:T(8,128)(2,1)} %weight_ref.1), custom_call_target="tpu_custom_call" | custom-call | flops 3758096384 | bytes 9175040 | tf_op jit(solution)/shard_map/base/pallas_call | solution.py:184
  17.0 0.1 collective-permute-start.1
  17.1 1.6 %collective-permute-start = (s32[2,8]{1,0:T(2,128)S(1)}, s32[2,8]{1,0:T(2,128)S(1)}, u32[]{:S(2)}, u32[]{:S(2)}) collective-permute-start(s32[2,8]{1,0:T(2,128)S(1)} %bitcast.5), channel_id=1, source_target_pairs={{0,16},{16,0},{1,17},{17,1},{2,18},{18,2},{3,19},{19,3},{4,20},{20... | collective-permute-start | bytes 200 | tf_op jit(solution)/shard_map/ppermute | solution.py:179
  18.6 2.1 %collective-permute-done.refs_1_ = s32[2,8]{1,0:T(2,128)S(1)} collective-permute-done((s32[2,8]{1,0:T(2,128)S(1)}, s32[2,8]{1,0:T(2,128)S(1)}, u32[]{:S(2)}, u32[]{:S(2)}) %collective-permute-start) | collective-permute-done | bytes 96 | tf_op jit(solution)/shard_map/ppermute | solution.py:179
  20.7 3.9 %all-to-all-done.refs_2_ = bf16[8,16,2176]{2,1,0:T(8,128)(2,1)S(1)} async-done(((bf16[8,16,2176]{2,1,0:T(8,128)(2,1)}), bf16[8,16,2176]{2,1,0:T(8,128)(2,1)S(1)}, u32[]{:S(2)}, u32[]{:S(2)}) %all-to-all-start) | async-done | bytes 557088 | tf_op jit(solution)/shard_map/all_to_all | solution.py:174
  24.6 0.7 %select.1 = (bf16[2,16,2176]{2,1,0:T(8,128)(2,1)S(1)}, bf16[2,16,2176]{2,1,0:T(8,128)(2,1)S(1)}, bf16[2,16,2176]{2,1,0:T(8,128)(2,1)S(1)}, bf16[2,16,2176]{2,1,0...) custom-call(s32[8]{0:T(128)S(1)} %copy-done.1, ...), custom_call_target="tpu_custom_call" | custom-call | tf_op jit(solution)/shard_map/select/pallas_call | solution.py:207
  25.3 1.5 %collective-permute-start.2 = (bf16[2,16,2176]{2,1,0:T(8,128)(2,1)S(1)}, bf16[2,16,2176]{2,1,0:T(8,128)(2,1)S(1)}, u32[]{:S(2)}, u32[]{:S(2)}) collective-permute-start(bf16[2,16,2176]{2,1,0:T(8,128)(2,1)S(1)} %get-tuple-element.30), channel_id=1, source_target_pairs={{0,2},{2,0},{4,6},{6,4},{8,10},{10,8},{12,14},{14,12},{16,18},{18,... | collective-permute-start | bytes 417800 | tf_op jit(solution)/shard_map/ppermute | solution.py:222
  26.8 1.6 %collective-permute-start.3 = (bf16[2,16,2176]{2,1,0:T(8,128)(2,1)S(1)}, bf16[2,16,2176]{2,1,0:T(8,128)(2,1)S(1)}, u32[]{:S(2)}, u32[]{:S(2)}) collective-permute-start(bf16[2,16,2176]{2,1,0:T(8,128)(2,1)S(1)} %get-tuple-element.31), channel_id=1, source_target_pairs={{0,22},{2,20},{4,18},{6,16},{8,30},{10,28},{12,26},{14,24},{16,6},... | collective-permute-start | bytes 417800 | tf_op jit(solution)/shard_map/ppermute | solution.py:222
  28.5 1.3 %collective-permute-start.4 = (bf16[2,16,2176]{2,1,0:T(8,128)(2,1)S(1)}, bf16[2,16,2176]{2,1,0:T(8,128)(2,1)S(1)}, u32[]{:S(2)}, u32[]{:S(2)}) collective-permute-start(bf16[2,16,2176]{2,1,0:T(8,128)(2,1)S(1)} %get-tuple-element.32), channel_id=1, source_target_pairs={{0,4},{2,6},{4,0},{6,2},{8,12},{10,14},{12,8},{14,10},{16,20},{18,... | collective-permute-start | bytes 417800 | tf_op jit(solution)/shard_map/ppermute | solution.py:222
  29.8 0.5 %collective-permute-start.5 = (bf16[2,16,2176]{2,1,0:T(8,128)(2,1)S(1)}, bf16[2,16,2176]{2,1,0:T(8,128)(2,1)S(1)}, u32[]{:S(2)}, u32[]{:S(2)}) collective-permute-start(bf16[2,16,2176]{2,1,0:T(8,128)(2,1)S(1)} %get-tuple-element.33), channel_id=1, source_target_pairs={{0,16},{2,18},{4,20},{6,22},{8,24},{10,26},{12,28},{14,30},{16,0},... | collective-permute-start | bytes 417800 | tf_op jit(solution)/shard_map/ppermute | solution.py:222
  30.3 0.9 %collective-permute-start.6 = (bf16[2,16,2176]{2,1,0:T(8,128)(2,1)S(1)}, bf16[2,16,2176]{2,1,0:T(8,128)(2,1)S(1)}, u32[]{:S(2)}, u32[]{:S(2)}) collective-permute-start(bf16[2,16,2176]{2,1,0:T(8,128)(2,1)S(1)} %get-tuple-element.34), channel_id=1, source_target_pairs={{0,6},{2,4},{4,2},{6,0},{8,14},{10,12},{12,10},{14,8},{16,22},{18,... | collective-permute-start | bytes 417800 | tf_op jit(solution)/shard_map/ppermute | solution.py:222
  31.2 0.7 %collective-permute-done.2.refs_1_ = bf16[2,16,2176]{2,1,0:T(8,128)(2,1)S(1)} collective-permute-done((bf16[2,16,2176]{2,1,0:T(8,128)(2,1)S(1)}, bf16[2,16,2176]{2,1,0:T(8,128)(2,1)S(1)}, u32[]{:S(2)}, u32[]{:S(2)}) %collective-permute-start.2) | collective-permute-done | bytes 139296 | tf_op jit(solution)/shard_map/ppermute | solution.py:222
  31.9 6.5 %collective-permute-start.7 = (bf16[2,16,2176]{2,1,0:T(8,128)(2,1)S(1)}, bf16[2,16,2176]{2,1,0:T(8,128)(2,1)S(1)}, u32[]{:S(2)}, u32[]{:S(2)}) collective-permute-start(bf16[2,16,2176]{2,1,0:T(8,128)(2,1)S(1)} %get-tuple-element.35), channel_id=1, source_target_pairs={{0,18},{2,16},{4,22},{6,20},{8,26},{10,24},{12,30},{14,28},{16,2},... | collective-permute-start | bytes 417800 | tf_op jit(solution)/shard_map/ppermute | solution.py:222
  38.5 3.1 %stage.1.x_ref = bf16[4,224,4096]{2,1,0:T(8,128)(2,1)S(1)} custom-call(bf16[4,224,4096]{2,1,0:T(8,128)(2,1)} %x_ref.2), custom_call_target="tpu_custom_call" | custom-call | bytes 14680064 | tf_op jit(solution)/shard_map/stage/pallas_call | solution.py:225
  41.6 0.4 collective-permute-done.7.refs_6_
  42.0 2.4 %collective-permute-done.8.refs_7_ = bf16[2,16,2176]{2,1,0:T(8,128)(2,1)S(1)} collective-permute-done((bf16[2,16,2176]{2,1,0:T(8,128)(2,1)S(1)}, bf16[2,16,2176]{2,1,0:T(8,128)(2,1)S(1)}, u32[]{:S(2)}, u32[]{:S(2)}) %collective-permute-start.8) | collective-permute-done | bytes 139296 | tf_op jit(solution)/shard_map/ppermute | solution.py:222
  44.4 2.7 %shrink.1 = (f32[4,112,128]{2,1,0:T(8,128)S(1)}, bf16[128,256]{1,0:T(8,128)(2,1)S(1)}) custom-call(s32[8]{0:T(128)S(1)} %copy-done.2, bf16[4,224,4096]{2,1,0:T(8,128)(2,1)S(1)} %stage.1.x_ref, bf16[2,16,2176]{2,1,0:T(8,128)(2,1)S(1)} %get-tuple-element.29.refs_0_, bf16[2,16,2176]{2,1,0:T(8,128)(2,1)S(1)} %collective-permute-done.2.refs_1_, ...), custom_call_target="tpu_custom_call" | custom-call | flops 939524096 | bytes 7340032 | tf_op jit(solution)/shard_map/shrink/pallas_call | solution.py:239
  47.1 0.1 collective-permute-start.9
  47.1 1.5 %collective-permute-done.9.theirs_ref = f32[4,112,128]{2,1,0:T(8,128)S(1)} collective-permute-done((f32[4,112,128]{2,1,0:T(8,128)S(1)}, f32[4,112,128]{2,1,0:T(8,128)S(1)}, u32[]{:S(2)}, u32[]{:S(2)}) %collective-permute-start.9) | collective-permute-done | bytes 229408 | tf_op jit(solution)/shard_map/ppermute | solution.py:256
  48.6 1.1 %expand.1 = bf16[4,224,256]{2,1,0:T(8,128)(2,1)} custom-call(f32[4,112,128]{2,1,0:T(8,128)S(1)} %get-tuple-element.37.mine_ref, f32[4,112,128]{2,1,0:T(8,128)S(1)} %collective-permute-done.9.theirs_ref, bf16[128,256]{1,0:T(8,128)(2,1)S(1)} %get-tuple-element.38.up_ref, f32[896,256]{1,0:T(8,128)S(1)} %get-tuple-element.39.base_ref, ...), custom_call_target="tpu_custom_call" | custom-call | tf_op jit(solution)/shard_map/expand/pallas_call | solution.py:258
  (10 shorter events, 0.0 us)
Async XLA Ops:
  2.1 15.0 %copy-start = (s32[8,2]{0,1:T(2,128)S(1)}, s32[8,2]{0,1:T(2,128)}, u32[]{:S(2)}) copy-start(s32[8,2]{0,1:T(2,128)} %param.12) | copy-start | bytes 196
  2.1 22.5 %copy-start.1 = (s32[8]{0:T(128)S(1)}, s32[8]{0:T(128)}, u32[]{:S(2)}) copy-start(s32[8]{0:T(128)} %home_ref.1) | copy-start | bytes 100
  2.1 22.5 %all-to-all-start = ((bf16[8,16,2176]{2,1,0:T(8,128)(2,1)}), bf16[8,16,2176]{2,1,0:T(8,128)(2,1)S(1)}, u32[]{:S(2)}, u32[]{:S(2)}) async-start(bf16[8,16,2176]{2,1,0:T(8,128)(2,1)} %pack.1), calls=%async_computation | async-start | bytes 1114112 | tf_op jit(solution)/shard_map/all_to_all | solution.py:174
  17.0 3.7 %collective-permute-start.1 = (f32[896,256]{1,0:T(8,128)S(1)}, f32[896,256]{1,0:T(8,128)S(1)}, u32[]{:S(2)}, u32[]{:S(2)}) collective-permute-start(f32[896,256]{1,0:T(8,128)S(1)} %get-tuple-element.24), channel_id=1, source_target_pairs={{0,1},{1,0},{2,3},{3,2},{4,5},{5,4},{6,7},{7,6},{8,9},{9,8},{10,11... | collective-permute-start | bytes 2752520 | tf_op jit(solution)/shard_map/ppermute | solution.py:202
  17.1 3.6 %collective-permute-start = (s32[2,8]{1,0:T(2,128)S(1)}, s32[2,8]{1,0:T(2,128)S(1)}, u32[]{:S(2)}, u32[]{:S(2)}) collective-permute-start(s32[2,8]{1,0:T(2,128)S(1)} %bitcast.5), channel_id=1, source_target_pairs={{0,16},{16,0},{1,17},{17,1},{2,18},{18,2},{3,19},{19,3},{4,20},{20... | collective-permute-start | bytes 200 | tf_op jit(solution)/shard_map/ppermute | solution.py:179
  25.3 6.6 %collective-permute-start.2 = (bf16[2,16,2176]{2,1,0:T(8,128)(2,1)S(1)}, bf16[2,16,2176]{2,1,0:T(8,128)(2,1)S(1)}, u32[]{:S(2)}, u32[]{:S(2)}) collective-permute-start(bf16[2,16,2176]{2,1,0:T(8,128)(2,1)S(1)} %get-tuple-element.30), channel_id=1, source_target_pairs={{0,2},{2,0},{4,6},{6,4},{8,10},{10,8},{12,14},{14,12},{16,18},{18,... | collective-permute-start | bytes 417800 | tf_op jit(solution)/shard_map/ppermute | solution.py:222
  26.8 11.6 %collective-permute-start.3 = (bf16[2,16,2176]{2,1,0:T(8,128)(2,1)S(1)}, bf16[2,16,2176]{2,1,0:T(8,128)(2,1)S(1)}, u32[]{:S(2)}, u32[]{:S(2)}) collective-permute-start(bf16[2,16,2176]{2,1,0:T(8,128)(2,1)S(1)} %get-tuple-element.31), channel_id=1, source_target_pairs={{0,22},{2,20},{4,18},{6,16},{8,30},{10,28},{12,26},{14,24},{16,6},... | collective-permute-start | bytes 417800 | tf_op jit(solution)/shard_map/ppermute | solution.py:222
  28.5 13.1 %collective-permute-start.4 = (bf16[2,16,2176]{2,1,0:T(8,128)(2,1)S(1)}, bf16[2,16,2176]{2,1,0:T(8,128)(2,1)S(1)}, u32[]{:S(2)}, u32[]{:S(2)}) collective-permute-start(bf16[2,16,2176]{2,1,0:T(8,128)(2,1)S(1)} %get-tuple-element.32), channel_id=1, source_target_pairs={{0,4},{2,6},{4,0},{6,2},{8,12},{10,14},{12,8},{14,10},{16,20},{18,... | collective-permute-start | bytes 417800 | tf_op jit(solution)/shard_map/ppermute | solution.py:222
  29.8 11.8 %collective-permute-start.5 = (bf16[2,16,2176]{2,1,0:T(8,128)(2,1)S(1)}, bf16[2,16,2176]{2,1,0:T(8,128)(2,1)S(1)}, u32[]{:S(2)}, u32[]{:S(2)}) collective-permute-start(bf16[2,16,2176]{2,1,0:T(8,128)(2,1)S(1)} %get-tuple-element.33), channel_id=1, source_target_pairs={{0,16},{2,18},{4,20},{6,22},{8,24},{10,26},{12,28},{14,30},{16,0},... | collective-permute-start | bytes 417800 | tf_op jit(solution)/shard_map/ppermute | solution.py:222
  30.3 11.3 %collective-permute-start.6 = (bf16[2,16,2176]{2,1,0:T(8,128)(2,1)S(1)}, bf16[2,16,2176]{2,1,0:T(8,128)(2,1)S(1)}, u32[]{:S(2)}, u32[]{:S(2)}) collective-permute-start(bf16[2,16,2176]{2,1,0:T(8,128)(2,1)S(1)} %get-tuple-element.34), channel_id=1, source_target_pairs={{0,6},{2,4},{4,2},{6,0},{8,14},{10,12},{12,10},{14,8},{16,22},{18,... | collective-permute-start | bytes 417800 | tf_op jit(solution)/shard_map/ppermute | solution.py:222
  31.9 10.1 %collective-permute-start.7 = (bf16[2,16,2176]{2,1,0:T(8,128)(2,1)S(1)}, bf16[2,16,2176]{2,1,0:T(8,128)(2,1)S(1)}, u32[]{:S(2)}, u32[]{:S(2)}) collective-permute-start(bf16[2,16,2176]{2,1,0:T(8,128)(2,1)S(1)} %get-tuple-element.35), channel_id=1, source_target_pairs={{0,18},{2,16},{4,22},{6,20},{8,26},{10,24},{12,30},{14,28},{16,2},... | collective-permute-start | bytes 417800 | tf_op jit(solution)/shard_map/ppermute | solution.py:222
  38.4 6.0 %collective-permute-start.8 = (bf16[2,16,2176]{2,1,0:T(8,128)(2,1)S(1)}, bf16[2,16,2176]{2,1,0:T(8,128)(2,1)S(1)}, u32[]{:S(2)}, u32[]{:S(2)}) collective-permute-start(bf16[2,16,2176]{2,1,0:T(8,128)(2,1)S(1)} %get-tuple-element.36), channel_id=1, source_target_pairs={{0,20},{2,22},{4,16},{6,18},{8,28},{10,30},{12,24},{14,26},{16,4},... | collective-permute-start | bytes 417800 | tf_op jit(solution)/shard_map/ppermute | solution.py:222
  38.4 6.0 %copy-start.2 = (s32[8]{0:T(128)S(1)}, s32[8]{0:T(128)}, u32[]{:S(2)}) copy-start(s32[8]{0:T(128)} %count_ref.1) | copy-start | bytes 100
  47.1 1.6 %collective-permute-start.9 = (f32[4,112,128]{2,1,0:T(8,128)S(1)}, f32[4,112,128]{2,1,0:T(8,128)S(1)}, u32[]{:S(2)}, u32[]{:S(2)}) collective-permute-start(f32[4,112,128]{2,1,0:T(8,128)S(1)} %get-tuple-element.37.mine_ref), channel_id=1, source_target_pairs={{0,1},{1,0},{2,3},{3,2},{4,5},{5,4},{6,7},{7,6},{8,9},{9,8},{10,11... | collective-permute-start | bytes 688136 | tf_op jit(solution)/shard_map/ppermute | solution.py:256

commit v6 on v5

--- a/solution.py
+++ b/solution.py
@@ -10,52 +10,53 @@
 adapter_scale_factor = 0.5
 MEMBERS = 8
 PIECE_ROWS = 16
-ORDER = (1, 7, 2, 4, 3, 5, 6)
 
 ANY = pl.BlockSpec(memory_space=pl.ANY)
 SMEM = pl.BlockSpec(memory_space=pltpu.SMEM)
 VMEM = pl.BlockSpec(memory_space=pltpu.VMEM)
 
 
-def pack_kernel(near, halves, down_ref, up_ref, out_ref, sem):
-    member_base = lax.axis_index("rep") * near
-    tp_index = lax.axis_index("tp")
-    wide = down_ref.shape[1] // halves
-    up_own = up_ref.shape[1] // lax.axis_size("tp")
-    up_wide = up_own // halves
-    copies = []
-    for group in range(out_ref.shape[0]):
-        member = member_base + group % near
-        rows = pl.ds(pl.multiple_of(member // halves * PIECE_ROWS, PIECE_ROWS), PIECE_ROWS)
-        half = lax.rem(member, halves)
-        down_at = pl.ds(pl.multiple_of(half * wide, 128), wide)
-        up_at = pl.ds(pl.multiple_of(tp_index * up_own + half * up_wide, 128), up_wide)
-        copies += [
-            pltpu.make_async_copy(
-                down_ref.at[rows, down_at], out_ref.at[group, :, pl.ds(0, wide)], sem.at[2 * group]
-            ),
-            pltpu.make_async_copy(
-                up_ref.at[rows, up_at],
-                out_ref.at[group, :, pl.ds(wide, up_wide)],
-                sem.at[2 * group + 1],
-            ),
-        ]
+def pack_kernel(near, halves, down_ref, up_ref, out_ref, down, up, sem):
+    tall, up_own = up.shape
+    rows = pl.ds(pl.multiple_of(lax.axis_index("rep") * tall, tall), tall)
+    columns = pl.ds(pl.multiple_of(lax.axis_index("tp") * up_own, 128), up_own)
+    copies = [
+        pltpu.make_async_copy(down_ref.at[rows], down, sem.at[0]),
+        pltpu.make_async_copy(up_ref.at[rows, columns], up, sem.at[1]),
+    ]
     for copy in copies:
         copy.start()
     for copy in copies:
         copy.wait()
-
-
-def select_kernel(near, rep_count, home_ref, *refs):
-    wanted, held_ref, outs = refs[:rep_count], refs[rep_count], refs[rep_count + 1 :]
+    wide, up_wide = down.shape[1] // halves, up_own // halves
+    for group in range(out_ref.shape[0]):
+        place, half = group % near // halves, group % halves
+        rows = slice(place * PIECE_ROWS, (place + 1) * PIECE_ROWS)
+        out_ref[group, :, :wide] = down[rows, half * wide : (half + 1) * wide]
+        out_ref[group, :, wide:] = up[rows, half * up_wide : (half + 1) * up_wide]
+
+
+def select_kernel(near, halves, crossing, rep_count, home_ref, *refs):
+    wanted, held_ref, (plane_ref, *outs) = refs[:rep_count], refs[rep_count], refs[rep_count + 1 :]
     group_index = lax.axis_index("grp")
+    rep_index = lax.axis_index("rep")
     pool_size = home_ref.shape[0]
-    for flip, out in zip((0,) + ORDER, outs):
-        other = group_index ^ (flip % near)
-        for slot in range(out.shape[0]):
-            adapter = jnp.clip(wanted[flip // near][slot, other], 0, pool_size - 1)
+
+    def fill(out_ref, flip, other):
+        for slot in range(out_ref.shape[0]):
+            adapter = jnp.clip(wanted[flip][slot, other], 0, pool_size - 1)
             place = jnp.clip(home_ref[adapter], 0, pool_size - 1)
-            out[slot] = held_ref[place]
+            out_ref[slot] = held_ref[place]
+
+    for flip, out_ref in zip(crossing, outs):
+        fill(out_ref, flip // near, group_index ^ (flip % near))
+    for flip in range(rep_count):
+        for half in range(halves):
+            fill(
+                plane_ref.at[(rep_index ^ flip) * halves + half],
+                flip,
+                group_index // halves * halves + half,
+            )
 
 
 def stage_kernel(x_ref, out_ref, sem):
@@ -92,20 +93,28 @@
         store(second, first)
 
 
-def shrink_kernel(halves, rank, count_ref, x_ref, *refs):
+def shrink_kernel(near, halves, crossing, rank, count_ref, x_ref, plane_ref, *refs):
     pieces, (shrunk_ref, up_ref, down) = refs[:-3], refs[-3:]
-    slot_count = pieces[0].shape[0]
+    slot_count = plane_ref.shape[1]
     wide = down.shape[1] // halves
     up_wide = up_ref.shape[1] // halves
     group_index = lax.axis_index("grp")
-    for flip, piece in zip((0,) + ORDER, pieces):
-        half = lax.rem(group_index ^ flip, halves)
+    low = lax.rem(group_index, near)
+    me = lax.axis_index("rep") * near + low
+
+    def put(member, half, piece_ref):
         for slot in range(slot_count):
-            rows = pl.ds(slot * rank + flip // halves * PIECE_ROWS, PIECE_ROWS)
-            down[rows, pl.ds(pl.multiple_of(half * wide, 128), wide)] = piece[slot, :, :wide]
-            up_ref[rows, pl.ds(pl.multiple_of(half * up_wide, 128), up_wide)] = piece[
+            row = slot * rank + member // halves * PIECE_ROWS
+            rows = pl.ds(pl.multiple_of(row, PIECE_ROWS), PIECE_ROWS)
+            down[rows, pl.ds(pl.multiple_of(half * wide, 128), wide)] = piece_ref[slot, :, :wide]
+            up_ref[rows, pl.ds(pl.multiple_of(half * up_wide, 128), up_wide)] = piece_ref[
                 slot, :, wide:
             ]
+
+    for flip, piece_ref in zip(crossing, pieces):
+        put(me ^ flip, lax.rem(me ^ flip, halves), piece_ref)
+    for at in range(plane_ref.shape[0]):
+        put(at // halves * near + low // halves * halves, at % halves, plane_ref.at[at])
     rows = shrunk_ref.shape[1]
     slot_of = lax.broadcasted_iota(jnp.int32, shrunk_ref.shape[1:], 1) // rank
     live_count = count_ref[group_index]
@@ -167,7 +176,11 @@
         out_shape=pltpu.VMEM((group_count, PIECE_ROWS, piece_width), bf16),
         in_specs=[ANY, ANY],
         out_specs=VMEM,
-        scratch_shapes=[pltpu.SemaphoreType.DMA((2 * group_count,))],
+        scratch_shapes=[
+            pltpu.VMEM((rank // rep_count, half_width), bf16),
+            pltpu.VMEM((rank // rep_count, share), bf16),
+            pltpu.SemaphoreType.DMA((2,)),
+        ],
         compiler_params=pltpu.CompilerParams(vmem_limit_bytes=56 << 20),
         name="pack",
     )(down, pool_up[0])
@@ -204,24 +217,35 @@
         (held, wanted[1:], mine, base_other)
     )
 
-    sends = pl.pallas_call(
-        functools.partial(select_kernel, near, rep_count),
-        out_shape=[jax.ShapeDtypeStruct((slot_count, PIECE_ROWS, piece_width), bf16)] * MEMBERS,
+    crossing = [flip for flip in range(MEMBERS - 1, 0, -1) if flip % near >= halves]
+    plane_size = rep_count * halves
+    piece_shape = (slot_count, PIECE_ROWS, piece_width)
+    plane, *sends = pl.pallas_call(
+        functools.partial(select_kernel, near, halves, crossing, rep_count),
+        out_shape=[jax.ShapeDtypeStruct((plane_size, *piece_shape), bf16)]
+        + [jax.ShapeDtypeStruct(piece_shape, bf16)] * len(crossing),
         in_specs=[SMEM] * (1 + rep_count) + [VMEM],
-        out_specs=[VMEM] * MEMBERS,
+        out_specs=[VMEM] * (1 + len(crossing)),
         compiler_params=pltpu.CompilerParams(vmem_limit_bytes=12 << 20),
         name="select",
     )(adapter_home, *wanted, held)
     got = []
-    for flip, send in zip(ORDER, sends[1:]):
+    for flip, send in zip(crossing, sends):
         pairs = [
             (r * group_count + g, (r ^ flip // near) * group_count + (g ^ flip % near))
             for r in range(rep_count)
             for g in range(group_count)
         ]
         got.append(lax.ppermute(send, ("rep", "grp"), pairs))
-
-    late, own = lax.optimization_barrier((hidden, sends[0]))
+    groups = [
+        [r * group_count + g for r in range(rep_count) for g in range(first, first + halves)]
+        for first in range(0, group_count, halves)
+    ]
+    got_plane = lax.all_to_all(
+        plane, ("rep", "grp"), 0, 0, axis_index_groups=groups, tiled=True
+    )
+
+    late, got_plane = lax.optimization_barrier((hidden, got_plane))
     near_hidden = pl.pallas_call(
         stage_kernel,
         out_shape=pltpu.VMEM(hidden.shape, bf16),
@@ -237,12 +261,12 @@
 
     both = slot_count * rank
     shrunk, up = pl.pallas_call(
-        functools.partial(shrink_kernel, halves, rank),
+        functools.partial(shrink_kernel, near, halves, crossing, rank),
         out_shape=[
             jax.ShapeDtypeStruct((step_count, block_rows, both), f32),
             jax.ShapeDtypeStruct((both, share), bf16),
         ],
-        in_specs=[SMEM] + [VMEM] * (1 + MEMBERS),
+        in_specs=[SMEM] + [VMEM] * (2 + len(crossing)),
         out_specs=[VMEM, VMEM],
         scratch_shapes=[pltpu.VMEM((both, half_width), bf16)],
         compiler_params=pltpu.CompilerParams(vmem_limit_bytes=12 << 20),
@@ -252,7 +276,7 @@
             transcendentals=0,
         ),
         name="shrink",
-    )(block_count, near_hidden, own, *got)
+    )(block_count, near_hidden, got_plane, *got)
     shrunk_other = lax.ppermute(shrunk, "tp", swap)
 
     return pl.pallas_call(

time: 50.1 us -> 52 us (1.038)
  waiting for transfers between devices: 11 us -> 15.2 us
  starting transfers between devices: 21.5 us -> 18.5 us
  Pallas kernels: 17.2 us -> 17.8 us
    all_to_all x0 -> x1, waiting for transfers between devices: none -> 7.71 us  [local(): lax.all_to_all(plane, ('rep', 'grp'), 0, 0, axis_index_groups=groups, til...]
    ppermute x7 -> x4, starting transfers between devices: 12.5 us -> 5.85 us  [local(): got.append(lax.ppermute(send, ('rep', 'grp'), pairs))]
    all_to_all x0 -> x1, starting transfers between devices: none -> 3.66 us  [local(): lax.all_to_all(plane, ('rep', 'grp'), 0, 0, axis_index_groups=groups, til...]
    ppermute x7 -> x4, waiting for transfers between devices: 3.51 us -> 0.01 us  [local(): got.append(lax.ppermute(send, ('rep', 'grp'), pairs))]
    pallas_call x2, Pallas kernels: 3.32 us -> 4.2 us  [the longest x1 2.71 us: local(): pl.pallas_call(functools.partial(shrink_kernel, near, halves, crossing, r...]
  transfers between devices with their start and end apart: 11 -> 9, of which waited for: 6 -> 4; matrix products, arithmetic and copies ran while one was open for 0% -> 0% of each run, Pallas kernels for 21% -> 21%
where the time goes in v6:
time: 52 us; the launch traced here: 51.6 us
  starting transfers between devices  18.5 us (36%)
  Pallas kernels  17.8 us (34%)
  waiting for transfers between devices  15.2 us (29%)
    all_to_all x1, waiting for transfers between devices, local(): lax.all_to_all(plane, ('rep', 'grp'), 0, 0, axis_index_groups=groups, til...  7.71 us
    pallas_call x1, Pallas kernels, local(): pl.pallas_call(base_kernel, grid=(chunk_count,), out_shape=[jax.ShapeDtyp...  7.56 us
    all_to_all x1, starting transfers between devices, local(): held = lax.all_to_all(packed, 'grp', 0, 0, tiled=True)  7.29 us
    ppermute x4, starting transfers between devices, local(): got.append(lax.ppermute(send, ('rep', 'grp'), pairs))  5.85 us
    all_to_all x1, waiting for transfers between devices, local(): held = lax.all_to_all(packed, 'grp', 0, 0, tiled=True)  3.89 us
    all_to_all x1, starting transfers between devices, local(): lax.all_to_all(plane, ('rep', 'grp'), 0, 0, axis_index_groups=groups, til...  3.66 us
    pallas_call x1, Pallas kernels, local(): pl.pallas_call(stage_kernel, out_shape=pltpu.VMEM(hidden.shape, bf16), in...  3.09 us
    pallas_call x1, Pallas kernels, local(): pl.pallas_call(functools.partial(shrink_kernel, near, halves, crossing, r...  2.71 us
  transfers between devices with their start and end apart: 9, of which 4 were waited for; matrix products, arithmetic and copies ran while one was open for 0% of the time, Pallas kernels for 21%

profile of v6, /device:TPU:0, one launch (start us, length us, event | category | flops | bytes accessed | tf_op | source)
XLA Modules:
  0.0 51.6 jit_solution(9863299063581420352)
XLA Ops:
  0.0 1.8 %pack.1 = bf16[8,16,2176]{2,1,0:T(8,128)(2,1)} custom-call(bf16[64,4096]{1,0:T(8,128)(2,1)} %bitcast.7, bf16[64,512]{1,0:T(8,128)(2,1)} %bitcast.8), custom_call_target="tpu_custom_call" | custom-call | tf_op jit(solution)/shard_map/pack/pallas_call | solution.py:174
  1.8 0.0 copy-start
  1.8 0.0 copy-start.1
  1.9 7.3 %all-to-all-start = ((bf16[8,16,2176]{2,1,0:T(8,128)(2,1)}), bf16[8,16,2176]{2,1,0:T(8,128)(2,1)S(1)}, u32[]{:S(2)}, u32[]{:S(2)}) async-start(bf16[8,16,2176]{2,1,0:T(8,128)(2,1)} %pack.1), calls=%async_computation | async-start | bytes 1114112 | tf_op jit(solution)/shard_map/all_to_all | solution.py:187
  9.1 7.6 %base.1 = (f32[896,256]{1,0:T(8,128)S(1)}, f32[896,256]{1,0:T(8,128)S(1)}) custom-call(bf16[4,224,4096]{2,1,0:T(8,128)(2,1)} %x_ref.2, bf16[4096,512]{1,0:T(8,128)(2,1)} %weight_ref.1), custom_call_target="tpu_custom_call" | custom-call | flops 3758096384 | bytes 9175040 | tf_op jit(solution)/shard_map/base/pallas_call | solution.py:197
  16.7 0.1 collective-permute-start.1
  16.8 1.6 %collective-permute-start = (s32[2,8]{1,0:T(2,128)S(1)}, s32[2,8]{1,0:T(2,128)S(1)}, u32[]{:S(2)}, u32[]{:S(2)}) collective-permute-start(s32[2,8]{1,0:T(2,128)S(1)} %bitcast.5), channel_id=1, source_target_pairs={{0,16},{16,0},{1,17},{17,1},{2,18},{18,2},{3,19},{19,3},{4,20},{20... | collective-permute-start | bytes 200 | tf_op jit(solution)/shard_map/ppermute | solution.py:192
  18.4 2.1 %collective-permute-done.refs_1_ = s32[2,8]{1,0:T(2,128)S(1)} collective-permute-done((s32[2,8]{1,0:T(2,128)S(1)}, s32[2,8]{1,0:T(2,128)S(1)}, u32[]{:S(2)}, u32[]{:S(2)}) %collective-permute-start) | collective-permute-done | bytes 96 | tf_op jit(solution)/shard_map/ppermute | solution.py:192
  20.4 0.0 collective-permute-done.1.base_other_ref
  20.4 3.9 %all-to-all-done.refs_2_ = bf16[8,16,2176]{2,1,0:T(8,128)(2,1)S(1)} async-done(((bf16[8,16,2176]{2,1,0:T(8,128)(2,1)}), bf16[8,16,2176]{2,1,0:T(8,128)(2,1)S(1)}, u32[]{:S(2)}, u32[]{:S(2)}) %all-to-all-start) | async-done | bytes 557088 | tf_op jit(solution)/shard_map/all_to_all | solution.py:187
  24.3 1.5 %select.1 = (bf16[4,2,16,2176]{3,2,1,0:T(8,128)(2,1)}, bf16[2,16,2176]{2,1,0:T(8,128)(2,1)S(1)}, bf16[2,16,2176]{2,1,0:T(8,128)(2,1)S(1)}, bf16[2,16,2176]{2,1,0:T(8,128)(2,1)S(1)}, bf16[2,16,2176]{2,1,0:T(8,128)(2,1)S(1)}) custom-call(s32[8]{0:T(128)S(1)} %copy-done.1, s32[2,8]{1,0:T(2,128)S(1)} %bitcast.6, s32[2,8]{1,0:T(2,128)S(1)} %collective-permute-done.refs_1_, ...), custom_call_target="tpu_custom_call" | custom-call | tf_op jit(solution)/shard_map/select/pallas_call | solution.py:223
  25.8 3.7 %all-to-all-start.1 = ((bf16[4,2,16,2176]{3,2,1,0:T(8,128)(2,1)}), bf16[4,2,16,2176]{3,2,1,0:T(8,128)(2,1)S(1)}, u32[]{:S(2)}, u32[]{:S(2)}) async-start(bf16[4,2,16,2176]{3,2,1,0:T(8,128)(2,1)} %get-tuple-element.24), calls=%async_computation.1 | async-start | bytes 1114112 | tf_op jit(solution)/shard_map/all_to_all | solution.py:244
  29.5 2.9 %collective-permute-start.2 = (bf16[2,16,2176]{2,1,0:T(8,128)(2,1)S(1)}, bf16[2,16,2176]{2,1,0:T(8,128)(2,1)S(1)}, u32[]{:S(2)}, u32[]{:S(2)}) collective-permute-start(bf16[2,16,2176]{2,1,0:T(8,128)(2,1)S(1)} %get-tuple-element.27), channel_id=1, source_target_pairs={{0,22},{2,20},{4,18},{6,16},{8,30},{10,28},{12,26},{14,24},{16,6},... | collective-permute-start | bytes 417800 | tf_op jit(solution)/shard_map/ppermute | solution.py:239
  32.4 1.5 %collective-permute-start.3 = (bf16[2,16,2176]{2,1,0:T(8,128)(2,1)S(1)}, bf16[2,16,2176]{2,1,0:T(8,128)(2,1)S(1)}, u32[]{:S(2)}, u32[]{:S(2)}) collective-permute-start(bf16[2,16,2176]{2,1,0:T(8,128)(2,1)S(1)} %get-tuple-element.28), channel_id=1, source_target_pairs={{0,20},{2,22},{4,16},{6,18},{8,28},{10,30},{12,24},{14,26},{16,4},... | collective-permute-start | bytes 417800 | tf_op jit(solution)/shard_map/ppermute | solution.py:239
  33.9 0.0 collective-permute-start.4
  33.9 1.4 %collective-permute-start.5 = (bf16[2,16,2176]{2,1,0:T(8,128)(2,1)S(1)}, bf16[2,16,2176]{2,1,0:T(8,128)(2,1)S(1)}, u32[]{:S(2)}, u32[]{:S(2)}) collective-permute-start(bf16[2,16,2176]{2,1,0:T(8,128)(2,1)S(1)} %get-tuple-element.30), channel_id=1, source_target_pairs={{0,4},{2,6},{4,0},{6,2},{8,12},{10,14},{12,8},{14,10},{16,20},{18,... | collective-permute-start | bytes 417800 | tf_op jit(solution)/shard_map/ppermute | solution.py:239
  35.3 7.7 %all-to-all-done.1.plane_ref = bf16[4,2,16,2176]{3,2,1,0:T(8,128)(2,1)S(1)} async-done(((bf16[4,2,16,2176]{3,2,1,0:T(8,128)(2,1)}), bf16[4,2,16,2176]{3,2,1,0:T(8,128)(2,1)S(1)}, u32[]{:S(2)}, u32[]{:S(2)}) %all-to-all-start.1) | async-done | bytes 557088 | tf_op jit(solution)/shard_map/all_to_all | solution.py:244
  43.1 3.1 %stage.1.x_ref = bf16[4,224,4096]{2,1,0:T(8,128)(2,1)S(1)} custom-call(bf16[4,224,4096]{2,1,0:T(8,128)(2,1)} %x_ref.2), custom_call_target="tpu_custom_call" | custom-call | bytes 14680064 | tf_op jit(solution)/shard_map/stage/pallas_call | solution.py:249
  46.2 0.0 collective-permute-done.2.refs_0_
  46.2 0.0 collective-permute-done.4.refs_2_
  46.2 2.7 %shrink.1 = (f32[4,112,128]{2,1,0:T(8,128)S(1)}, bf16[128,256]{1,0:T(8,128)(2,1)S(1)}) custom-call(s32[8]{0:T(128)S(1)} %copy-done.2, bf16[4,224,4096]{2,1,0:T(8,128)(2,1)S(1)} %stage.1.x_ref, bf16[4,2,16,2176]{3,2,1,0:T(8,128)(2,1)S(1)} %all-to-all-done.1.plane_ref, bf16[2,16,2176]{2,1,0:T(8,128)(2,1)S(1)} %collective-permute-done.2.refs_0_, ...), custom_call_target="tpu_custom_call" | custom-call | flops 939524096 | bytes 7340032 | tf_op jit(solution)/shard_map/shrink/pallas_call | solution.py:263
  48.9 0.1 collective-permute-start.6
  49.0 1.5 %collective-permute-done.6.theirs_ref = f32[4,112,128]{2,1,0:T(8,128)S(1)} collective-permute-done((f32[4,112,128]{2,1,0:T(8,128)S(1)}, f32[4,112,128]{2,1,0:T(8,128)S(1)}, u32[]{:S(2)}, u32[]{:S(2)}) %collective-permute-start.6) | collective-permute-done | bytes 229408 | tf_op jit(solution)/shard_map/ppermute | solution.py:280
  50.5 1.1 %expand.1 = bf16[4,224,256]{2,1,0:T(8,128)(2,1)} custom-call(f32[4,112,128]{2,1,0:T(8,128)S(1)} %get-tuple-element.31.mine_ref, f32[4,112,128]{2,1,0:T(8,128)S(1)} %collective-permute-done.6.theirs_ref, bf16[128,256]{1,0:T(8,128)(2,1)S(1)} %get-tuple-element.32.up_ref, f32[896,256]{1,0:T(8,128)S(1)} %get-tuple-element.33.base_ref, ...), custom_call_target="tpu_custom_call" | custom-call | tf_op jit(solution)/shard_map/expand/pallas_call | solution.py:282
  (6 shorter events, 0.0 us)
Async XLA Ops:
  1.8 15.0 %copy-start = (s32[8,2]{0,1:T(2,128)S(1)}, s32[8,2]{0,1:T(2,128)}, u32[]{:S(2)}) copy-start(s32[8,2]{0,1:T(2,128)} %param.12) | copy-start | bytes 196
  1.8 22.5 %copy-start.1 = (s32[8]{0:T(128)S(1)}, s32[8]{0:T(128)}, u32[]{:S(2)}) copy-start(s32[8]{0:T(128)} %home_ref.1) | copy-start | bytes 100
  1.9 22.5 %all-to-all-start = ((bf16[8,16,2176]{2,1,0:T(8,128)(2,1)}), bf16[8,16,2176]{2,1,0:T(8,128)(2,1)S(1)}, u32[]{:S(2)}, u32[]{:S(2)}) async-start(bf16[8,16,2176]{2,1,0:T(8,128)(2,1)} %pack.1), calls=%async_computation | async-start | bytes 1114112 | tf_op jit(solution)/shard_map/all_to_all | solution.py:187
  16.7 3.7 %collective-permute-start.1 = (f32[896,256]{1,0:T(8,128)S(1)}, f32[896,256]{1,0:T(8,128)S(1)}, u32[]{:S(2)}, u32[]{:S(2)}) collective-permute-start(f32[896,256]{1,0:T(8,128)S(1)} %get-tuple-element.21), channel_id=1, source_target_pairs={{0,1},{1,0},{2,3},{3,2},{4,5},{5,4},{6,7},{7,6},{8,9},{9,8},{10,11... | collective-permute-start | bytes 2752520 | tf_op jit(solution)/shard_map/ppermute | solution.py:215
  16.8 3.6 %collective-permute-start = (s32[2,8]{1,0:T(2,128)S(1)}, s32[2,8]{1,0:T(2,128)S(1)}, u32[]{:S(2)}, u32[]{:S(2)}) collective-permute-start(s32[2,8]{1,0:T(2,128)S(1)} %bitcast.5), channel_id=1, source_target_pairs={{0,16},{16,0},{1,17},{17,1},{2,18},{18,2},{3,19},{19,3},{4,20},{20... | collective-permute-start | bytes 200 | tf_op jit(solution)/shard_map/ppermute | solution.py:192
  25.8 17.2 %all-to-all-start.1 = ((bf16[4,2,16,2176]{3,2,1,0:T(8,128)(2,1)}), bf16[4,2,16,2176]{3,2,1,0:T(8,128)(2,1)S(1)}, u32[]{:S(2)}, u32[]{:S(2)}) async-start(bf16[4,2,16,2176]{3,2,1,0:T(8,128)(2,1)} %get-tuple-element.24), calls=%async_computation.1 | async-start | bytes 1114112 | tf_op jit(solution)/shard_map/all_to_all | solution.py:244
  29.5 16.7 %collective-permute-start.2 = (bf16[2,16,2176]{2,1,0:T(8,128)(2,1)S(1)}, bf16[2,16,2176]{2,1,0:T(8,128)(2,1)S(1)}, u32[]{:S(2)}, u32[]{:S(2)}) collective-permute-start(bf16[2,16,2176]{2,1,0:T(8,128)(2,1)S(1)} %get-tuple-element.27), channel_id=1, source_target_pairs={{0,22},{2,20},{4,18},{6,16},{8,30},{10,28},{12,26},{14,24},{16,6},... | collective-permute-start | bytes 417800 | tf_op jit(solution)/shard_map/ppermute | solution.py:239
  32.4 13.8 %collective-permute-start.3 = (bf16[2,16,2176]{2,1,0:T(8,128)(2,1)S(1)}, bf16[2,16,2176]{2,1,0:T(8,128)(2,1)S(1)}, u32[]{:S(2)}, u32[]{:S(2)}) collective-permute-start(bf16[2,16,2176]{2,1,0:T(8,128)(2,1)S(1)} %get-tuple-element.28), channel_id=1, source_target_pairs={{0,20},{2,22},{4,16},{6,18},{8,28},{10,30},{12,24},{14,26},{16,4},... | collective-permute-start | bytes 417800 | tf_op jit(solution)/shard_map/ppermute | solution.py:239
  33.9 12.3 %collective-permute-start.4 = (bf16[2,16,2176]{2,1,0:T(8,128)(2,1)S(1)}, bf16[2,16,2176]{2,1,0:T(8,128)(2,1)S(1)}, u32[]{:S(2)}, u32[]{:S(2)}) collective-permute-start(bf16[2,16,2176]{2,1,0:T(8,128)(2,1)S(1)} %get-tuple-element.29), channel_id=1, source_target_pairs={{0,6},{2,4},{4,2},{6,0},{8,14},{10,12},{12,10},{14,8},{16,22},{18,... | collective-permute-start | bytes 417800 | tf_op jit(solution)/shard_map/ppermute | solution.py:239
  33.9 12.3 %copy-start.2 = (s32[8]{0:T(128)S(1)}, s32[8]{0:T(128)}, u32[]{:S(2)}) copy-start(s32[8]{0:T(128)} %count_ref.1) | copy-start | bytes 100
  33.9 12.3 %collective-permute-start.5 = (bf16[2,16,2176]{2,1,0:T(8,128)(2,1)S(1)}, bf16[2,16,2176]{2,1,0:T(8,128)(2,1)S(1)}, u32[]{:S(2)}, u32[]{:S(2)}) collective-permute-start(bf16[2,16,2176]{2,1,0:T(8,128)(2,1)S(1)} %get-tuple-element.30), channel_id=1, source_target_pairs={{0,4},{2,6},{4,0},{6,2},{8,12},{10,14},{12,8},{14,10},{16,20},{18,... | collective-permute-start | bytes 417800 | tf_op jit(solution)/shard_map/ppermute | solution.py:239
  48.9 1.6 %collective-permute-start.6 = (f32[4,112,128]{2,1,0:T(8,128)S(1)}, f32[4,112,128]{2,1,0:T(8,128)S(1)}, u32[]{:S(2)}, u32[]{:S(2)}) collective-permute-start(f32[4,112,128]{2,1,0:T(8,128)S(1)} %get-tuple-element.31.mine_ref), channel_id=1, source_target_pairs={{0,1},{1,0},{2,3},{3,2},{4,5},{5,4},{6,7},{7,6},{8,9},{9,8},{10,11... | collective-permute-start | bytes 688136 | tf_op jit(solution)/shard_map/ppermute | solution.py:280

commit v7 on v5

--- a/solution.py
+++ b/solution.py
@@ -10,40 +10,31 @@
 adapter_scale_factor = 0.5
 MEMBERS = 8
 PIECE_ROWS = 16
-ORDER = (1, 7, 2, 4, 3, 5, 6)
+ORDER = (4, 2, 1, 7, 6, 5, 3)
 
 ANY = pl.BlockSpec(memory_space=pl.ANY)
 SMEM = pl.BlockSpec(memory_space=pltpu.SMEM)
 VMEM = pl.BlockSpec(memory_space=pltpu.VMEM)
 
 
-def pack_kernel(near, halves, down_ref, up_ref, out_ref, sem):
-    member_base = lax.axis_index("rep") * near
-    tp_index = lax.axis_index("tp")
-    wide = down_ref.shape[1] // halves
-    up_own = up_ref.shape[1] // lax.axis_size("tp")
-    up_wide = up_own // halves
-    copies = []
-    for group in range(out_ref.shape[0]):
-        member = member_base + group % near
-        rows = pl.ds(pl.multiple_of(member // halves * PIECE_ROWS, PIECE_ROWS), PIECE_ROWS)
-        half = lax.rem(member, halves)
-        down_at = pl.ds(pl.multiple_of(half * wide, 128), wide)
-        up_at = pl.ds(pl.multiple_of(tp_index * up_own + half * up_wide, 128), up_wide)
-        copies += [
-            pltpu.make_async_copy(
-                down_ref.at[rows, down_at], out_ref.at[group, :, pl.ds(0, wide)], sem.at[2 * group]
-            ),
-            pltpu.make_async_copy(
-                up_ref.at[rows, up_at],
-                out_ref.at[group, :, pl.ds(wide, up_wide)],
-                sem.at[2 * group + 1],
-            ),
-        ]
+def pack_kernel(near, halves, down_ref, up_ref, out_ref, down, up, sem):
+    tall, up_own = up.shape
+    rows = pl.ds(pl.multiple_of(lax.axis_index("rep") * tall, tall), tall)
+    columns = pl.ds(pl.multiple_of(lax.axis_index("tp") * up_own, 128), up_own)
+    copies = [
+        pltpu.make_async_copy(down_ref.at[rows], down, sem.at[0]),
+        pltpu.make_async_copy(up_ref.at[rows, columns], up, sem.at[1]),
+    ]
     for copy in copies:
         copy.start()
     for copy in copies:
         copy.wait()
+    wide, up_wide = down.shape[1] // halves, up_own // halves
+    for group in range(out_ref.shape[0]):
+        place, half = group % near // halves, group % halves
+        rows = slice(place * PIECE_ROWS, (place + 1) * PIECE_ROWS)
+        out_ref[group, :, :wide] = down[rows, half * wide : (half + 1) * wide]
+        out_ref[group, :, wide:] = up[rows, half * up_wide : (half + 1) * up_wide]
 
 
 def select_kernel(near, rep_count, home_ref, *refs):
@@ -167,7 +158,11 @@
         out_shape=pltpu.VMEM((group_count, PIECE_ROWS, piece_width), bf16),
         in_specs=[ANY, ANY],
         out_specs=VMEM,
-        scratch_shapes=[pltpu.SemaphoreType.DMA((2 * group_count,))],
+        scratch_shapes=[
+            pltpu.VMEM((rank // rep_count, half_width), bf16),
+            pltpu.VMEM((rank // rep_count, share), bf16),
+            pltpu.SemaphoreType.DMA((2,)),
+        ],
         compiler_params=pltpu.CompilerParams(vmem_limit_bytes=56 << 20),
         name="pack",
     )(down, pool_up[0])

time: 50.1 us -> 47.3 us (0.944)
  starting transfers between devices: 21.5 us -> 18.9 us
    ppermute x7, starting transfers between devices: 12.5 us -> 9.92 us  [local(): got.append(lax.ppermute(send, ('rep', 'grp'), pairs))]
  transfers between devices with their start and end apart: 11 -> 11, of which waited for: 6 -> 6; matrix products, arithmetic and copies ran while one was open for 0% -> 0% of each run, Pallas kernels for 21% -> 23%
where the time goes in v7:
time: 47.3 us; the launch traced here: 47 us
  starting transfers between devices  18.9 us (40%)
  Pallas kernels  16.9 us (36%)
  waiting for transfers between devices  11 us (23%)
    ppermute x7, starting transfers between devices, local(): got.append(lax.ppermute(send, ('rep', 'grp'), pairs))  9.92 us
    pallas_call x1, Pallas kernels, local(): pl.pallas_call(base_kernel, grid=(chunk_count,), out_shape=[jax.ShapeDtyp...  7.56 us
    all_to_all x1, starting transfers between devices, local(): held = lax.all_to_all(packed, 'grp', 0, 0, tiled=True)  7.29 us
    all_to_all x1, waiting for transfers between devices, local(): held = lax.all_to_all(packed, 'grp', 0, 0, tiled=True)  3.89 us
    ppermute x7, waiting for transfers between devices, local(): got.append(lax.ppermute(send, ('rep', 'grp'), pairs))  3.58 us
    pallas_call x1, Pallas kernels, local(): pl.pallas_call(stage_kernel, out_shape=pltpu.VMEM(hidden.shape, bf16), in...  3.1 us
    pallas_call x1, Pallas kernels, local(): pl.pallas_call(functools.partial(shrink_kernel, halves, rank), out_shape=...  2.65 us
    ppermute x1, waiting for transfers between devices, local(): wanted.append(lax.ppermute(asked, 'rep', pairs))  2.08 us
  transfers between devices with their start and end apart: 11, of which 6 were waited for; matrix products, arithmetic and copies ran while one was open for 0% of the time, Pallas kernels for 23%

profile of v7, /device:TPU:0, one launch (start us, length us, event | category | flops | bytes accessed | tf_op | source)
XLA Modules:
  0.0 47.0 jit_solution(4566860889359158117)
XLA Ops:
  0.0 1.8 %pack.1 = bf16[8,16,2176]{2,1,0:T(8,128)(2,1)} custom-call(bf16[64,4096]{1,0:T(8,128)(2,1)} %bitcast.7, bf16[64,512]{1,0:T(8,128)(2,1)} %bitcast.8), custom_call_target="tpu_custom_call" | custom-call | tf_op jit(solution)/shard_map/pack/pallas_call | solution.py:156
  1.8 0.0 copy-start
  1.8 0.0 copy-start.1
  1.8 7.3 %all-to-all-start = ((bf16[8,16,2176]{2,1,0:T(8,128)(2,1)}), bf16[8,16,2176]{2,1,0:T(8,128)(2,1)S(1)}, u32[]{:S(2)}, u32[]{:S(2)}) async-start(bf16[8,16,2176]{2,1,0:T(8,128)(2,1)} %pack.1), calls=%async_computation | async-start | bytes 1114112 | tf_op jit(solution)/shard_map/all_to_all | solution.py:169
  9.1 7.6 %base.1 = (f32[896,256]{1,0:T(8,128)S(1)}, f32[896,256]{1,0:T(8,128)S(1)}) custom-call(bf16[4,224,4096]{2,1,0:T(8,128)(2,1)} %x_ref.2, bf16[4096,512]{1,0:T(8,128)(2,1)} %weight_ref.1), custom_call_target="tpu_custom_call" | custom-call | flops 3758096384 | bytes 9175040 | tf_op jit(solution)/shard_map/base/pallas_call | solution.py:179
  16.7 0.1 collective-permute-start.1
  16.8 1.6 %collective-permute-start = (s32[2,8]{1,0:T(2,128)S(1)}, s32[2,8]{1,0:T(2,128)S(1)}, u32[]{:S(2)}, u32[]{:S(2)}) collective-permute-start(s32[2,8]{1,0:T(2,128)S(1)} %bitcast.5), channel_id=1, source_target_pairs={{0,16},{16,0},{1,17},{17,1},{2,18},{18,2},{3,19},{19,3},{4,20},{20... | collective-permute-start | bytes 200 | tf_op jit(solution)/shard_map/ppermute | solution.py:174
  18.4 2.1 %collective-permute-done.refs_1_ = s32[2,8]{1,0:T(2,128)S(1)} collective-permute-done((s32[2,8]{1,0:T(2,128)S(1)}, s32[2,8]{1,0:T(2,128)S(1)}, u32[]{:S(2)}, u32[]{:S(2)}) %collective-permute-start) | collective-permute-done | bytes 96 | tf_op jit(solution)/shard_map/ppermute | solution.py:174
  20.4 3.9 %all-to-all-done.refs_2_ = bf16[8,16,2176]{2,1,0:T(8,128)(2,1)S(1)} async-done(((bf16[8,16,2176]{2,1,0:T(8,128)(2,1)}), bf16[8,16,2176]{2,1,0:T(8,128)(2,1)S(1)}, u32[]{:S(2)}, u32[]{:S(2)}) %all-to-all-start) | async-done | bytes 557088 | tf_op jit(solution)/shard_map/all_to_all | solution.py:169
  24.3 0.7 %select.1 = (bf16[2,16,2176]{2,1,0:T(8,128)(2,1)S(1)}, bf16[2,16,2176]{2,1,0:T(8,128)(2,1)S(1)}, bf16[2,16,2176]{2,1,0:T(8,128)(2,1)S(1)}, bf16[2,16,2176]{2,1,0...) custom-call(s32[8]{0:T(128)S(1)} %copy-done.1, ...), custom_call_target="tpu_custom_call" | custom-call | tf_op jit(solution)/shard_map/select/pallas_call | solution.py:202
  25.0 1.6 %collective-permute-start.2 = (bf16[2,16,2176]{2,1,0:T(8,128)(2,1)S(1)}, bf16[2,16,2176]{2,1,0:T(8,128)(2,1)S(1)}, u32[]{:S(2)}, u32[]{:S(2)}) collective-permute-start(bf16[2,16,2176]{2,1,0:T(8,128)(2,1)S(1)} %get-tuple-element.30), channel_id=1, source_target_pairs={{0,16},{2,18},{4,20},{6,22},{8,24},{10,26},{12,28},{14,30},{16,0},... | collective-permute-start | bytes 417800 | tf_op jit(solution)/shard_map/ppermute | solution.py:217
  26.6 0.7 %collective-permute-start.3 = (bf16[2,16,2176]{2,1,0:T(8,128)(2,1)S(1)}, bf16[2,16,2176]{2,1,0:T(8,128)(2,1)S(1)}, u32[]{:S(2)}, u32[]{:S(2)}) collective-permute-start(bf16[2,16,2176]{2,1,0:T(8,128)(2,1)S(1)} %get-tuple-element.31), channel_id=1, source_target_pairs={{0,4},{2,6},{4,0},{6,2},{8,12},{10,14},{12,8},{14,10},{16,20},{18,... | collective-permute-start | bytes 417800 | tf_op jit(solution)/shard_map/ppermute | solution.py:217
  27.3 0.7 %collective-permute-start.4 = (bf16[2,16,2176]{2,1,0:T(8,128)(2,1)S(1)}, bf16[2,16,2176]{2,1,0:T(8,128)(2,1)S(1)}, u32[]{:S(2)}, u32[]{:S(2)}) collective-permute-start(bf16[2,16,2176]{2,1,0:T(8,128)(2,1)S(1)} %get-tuple-element.32), channel_id=1, source_target_pairs={{0,2},{2,0},{4,6},{6,4},{8,10},{10,8},{12,14},{14,12},{16,18},{18,... | collective-permute-start | bytes 417800 | tf_op jit(solution)/shard_map/ppermute | solution.py:217
  28.0 2.0 %collective-permute-start.5 = (bf16[2,16,2176]{2,1,0:T(8,128)(2,1)S(1)}, bf16[2,16,2176]{2,1,0:T(8,128)(2,1)S(1)}, u32[]{:S(2)}, u32[]{:S(2)}) collective-permute-start(bf16[2,16,2176]{2,1,0:T(8,128)(2,1)S(1)} %get-tuple-element.33), channel_id=1, source_target_pairs={{0,22},{2,20},{4,18},{6,16},{8,30},{10,28},{12,26},{14,24},{16,6},... | collective-permute-start | bytes 417800 | tf_op jit(solution)/shard_map/ppermute | solution.py:217
  30.0 1.6 %collective-permute-start.6 = (bf16[2,16,2176]{2,1,0:T(8,128)(2,1)S(1)}, bf16[2,16,2176]{2,1,0:T(8,128)(2,1)S(1)}, u32[]{:S(2)}, u32[]{:S(2)}) collective-permute-start(bf16[2,16,2176]{2,1,0:T(8,128)(2,1)S(1)} %get-tuple-element.34), channel_id=1, source_target_pairs={{0,20},{2,22},{4,16},{6,18},{8,28},{10,30},{12,24},{14,26},{16,4},... | collective-permute-start | bytes 417800 | tf_op jit(solution)/shard_map/ppermute | solution.py:217
  31.7 3.3 %collective-permute-start.7 = (bf16[2,16,2176]{2,1,0:T(8,128)(2,1)S(1)}, bf16[2,16,2176]{2,1,0:T(8,128)(2,1)S(1)}, u32[]{:S(2)}, u32[]{:S(2)}) collective-permute-start(bf16[2,16,2176]{2,1,0:T(8,128)(2,1)S(1)} %get-tuple-element.35), channel_id=1, source_target_pairs={{0,18},{2,16},{4,22},{6,20},{8,26},{10,24},{12,30},{14,28},{16,2},... | collective-permute-start | bytes 417800 | tf_op jit(solution)/shard_map/ppermute | solution.py:217
  34.9 3.1 %stage.1.x_ref = bf16[4,224,4096]{2,1,0:T(8,128)(2,1)S(1)} custom-call(bf16[4,224,4096]{2,1,0:T(8,128)(2,1)} %x_ref.2), custom_call_target="tpu_custom_call" | custom-call | bytes 14680064 | tf_op jit(solution)/shard_map/stage/pallas_call | solution.py:220
  38.1 0.6 %collective-permute-done.6.refs_5_ = bf16[2,16,2176]{2,1,0:T(8,128)(2,1)S(1)} collective-permute-done((bf16[2,16,2176]{2,1,0:T(8,128)(2,1)S(1)}, bf16[2,16,2176]{2,1,0:T(8,128)(2,1)S(1)}, u32[]{:S(2)}, u32[]{:S(2)}) %collective-permute-start.6) | collective-permute-done | bytes 139296 | tf_op jit(solution)/shard_map/ppermute | solution.py:217
  38.7 2.5 %collective-permute-done.7.refs_6_ = bf16[2,16,2176]{2,1,0:T(8,128)(2,1)S(1)} collective-permute-done((bf16[2,16,2176]{2,1,0:T(8,128)(2,1)S(1)}, bf16[2,16,2176]{2,1,0:T(8,128)(2,1)S(1)}, u32[]{:S(2)}, u32[]{:S(2)}) %collective-permute-start.7) | collective-permute-done | bytes 139296 | tf_op jit(solution)/shard_map/ppermute | solution.py:217
  41.2 0.5 collective-permute-done.8.refs_7_
  41.6 2.6 %shrink.1 = (f32[4,112,128]{2,1,0:T(8,128)S(1)}, bf16[128,256]{1,0:T(8,128)(2,1)S(1)}) custom-call(s32[8]{0:T(128)S(1)} %copy-done.2, bf16[4,224,4096]{2,1,0:T(8,128)(2,1)S(1)} %stage.1.x_ref, bf16[2,16,2176]{2,1,0:T(8,128)(2,1)S(1)} %get-tuple-element.29.refs_0_, bf16[2,16,2176]{2,1,0:T(8,128)(2,1)S(1)} %collective-permute-done.2.refs_1_, ...), custom_call_target="tpu_custom_call" | custom-call | flops 939524096 | bytes 7340032 | tf_op jit(solution)/shard_map/shrink/pallas_call | solution.py:234
  44.3 0.1 collective-permute-start.9
  44.4 1.5 %collective-permute-done.9.theirs_ref = f32[4,112,128]{2,1,0:T(8,128)S(1)} collective-permute-done((f32[4,112,128]{2,1,0:T(8,128)S(1)}, f32[4,112,128]{2,1,0:T(8,128)S(1)}, u32[]{:S(2)}, u32[]{:S(2)}) %collective-permute-start.9) | collective-permute-done | bytes 229408 | tf_op jit(solution)/shard_map/ppermute | solution.py:251
  45.9 1.1 %expand.1 = bf16[4,224,256]{2,1,0:T(8,128)(2,1)} custom-call(f32[4,112,128]{2,1,0:T(8,128)S(1)} %get-tuple-element.37.mine_ref, f32[4,112,128]{2,1,0:T(8,128)S(1)} %collective-permute-done.9.theirs_ref, bf16[128,256]{1,0:T(8,128)(2,1)S(1)} %get-tuple-element.38.up_ref, f32[896,256]{1,0:T(8,128)S(1)} %get-tuple-element.39.base_ref, ...), custom_call_target="tpu_custom_call" | custom-call | tf_op jit(solution)/shard_map/expand/pallas_call | solution.py:253
  (10 shorter events, 0.0 us)
Async XLA Ops:
  1.8 15.0 %copy-start = (s32[8,2]{0,1:T(2,128)S(1)}, s32[8,2]{0,1:T(2,128)}, u32[]{:S(2)}) copy-start(s32[8,2]{0,1:T(2,128)} %param.12) | copy-start | bytes 196
  1.8 22.5 %copy-start.1 = (s32[8]{0:T(128)S(1)}, s32[8]{0:T(128)}, u32[]{:S(2)}) copy-start(s32[8]{0:T(128)} %home_ref.1) | copy-start | bytes 100
  1.8 22.5 %all-to-all-start = ((bf16[8,16,2176]{2,1,0:T(8,128)(2,1)}), bf16[8,16,2176]{2,1,0:T(8,128)(2,1)S(1)}, u32[]{:S(2)}, u32[]{:S(2)}) async-start(bf16[8,16,2176]{2,1,0:T(8,128)(2,1)} %pack.1), calls=%async_computation | async-start | bytes 1114112 | tf_op jit(solution)/shard_map/all_to_all | solution.py:169
  16.7 3.7 %collective-permute-start.1 = (f32[896,256]{1,0:T(8,128)S(1)}, f32[896,256]{1,0:T(8,128)S(1)}, u32[]{:S(2)}, u32[]{:S(2)}) collective-permute-start(f32[896,256]{1,0:T(8,128)S(1)} %get-tuple-element.24), channel_id=1, source_target_pairs={{0,1},{1,0},{2,3},{3,2},{4,5},{5,4},{6,7},{7,6},{8,9},{9,8},{10,11... | collective-permute-start | bytes 2752520 | tf_op jit(solution)/shard_map/ppermute | solution.py:197
  16.8 3.6 %collective-permute-start = (s32[2,8]{1,0:T(2,128)S(1)}, s32[2,8]{1,0:T(2,128)S(1)}, u32[]{:S(2)}, u32[]{:S(2)}) collective-permute-start(s32[2,8]{1,0:T(2,128)S(1)} %bitcast.5), channel_id=1, source_target_pairs={{0,16},{16,0},{1,17},{17,1},{2,18},{18,2},{3,19},{19,3},{4,20},{20... | collective-permute-start | bytes 200 | tf_op jit(solution)/shard_map/ppermute | solution.py:174
  25.0 6.7 %collective-permute-start.2 = (bf16[2,16,2176]{2,1,0:T(8,128)(2,1)S(1)}, bf16[2,16,2176]{2,1,0:T(8,128)(2,1)S(1)}, u32[]{:S(2)}, u32[]{:S(2)}) collective-permute-start(bf16[2,16,2176]{2,1,0:T(8,128)(2,1)S(1)} %get-tuple-element.30), channel_id=1, source_target_pairs={{0,16},{2,18},{4,20},{6,22},{8,24},{10,26},{12,28},{14,30},{16,0},... | collective-permute-start | bytes 417800 | tf_op jit(solution)/shard_map/ppermute | solution.py:217
  26.6 8.4 %collective-permute-start.3 = (bf16[2,16,2176]{2,1,0:T(8,128)(2,1)S(1)}, bf16[2,16,2176]{2,1,0:T(8,128)(2,1)S(1)}, u32[]{:S(2)}, u32[]{:S(2)}) collective-permute-start(bf16[2,16,2176]{2,1,0:T(8,128)(2,1)S(1)} %get-tuple-element.31), channel_id=1, source_target_pairs={{0,4},{2,6},{4,0},{6,2},{8,12},{10,14},{12,8},{14,10},{16,20},{18,... | collective-permute-start | bytes 417800 | tf_op jit(solution)/shard_map/ppermute | solution.py:217
  27.3 10.8 %collective-permute-start.4 = (bf16[2,16,2176]{2,1,0:T(8,128)(2,1)S(1)}, bf16[2,16,2176]{2,1,0:T(8,128)(2,1)S(1)}, u32[]{:S(2)}, u32[]{:S(2)}) collective-permute-start(bf16[2,16,2176]{2,1,0:T(8,128)(2,1)S(1)} %get-tuple-element.32), channel_id=1, source_target_pairs={{0,2},{2,0},{4,6},{6,4},{8,10},{10,8},{12,14},{14,12},{16,18},{18,... | collective-permute-start | bytes 417800 | tf_op jit(solution)/shard_map/ppermute | solution.py:217
  28.0 10.0 %collective-permute-start.5 = (bf16[2,16,2176]{2,1,0:T(8,128)(2,1)S(1)}, bf16[2,16,2176]{2,1,0:T(8,128)(2,1)S(1)}, u32[]{:S(2)}, u32[]{:S(2)}) collective-permute-start(bf16[2,16,2176]{2,1,0:T(8,128)(2,1)S(1)} %get-tuple-element.33), channel_id=1, source_target_pairs={{0,22},{2,20},{4,18},{6,16},{8,30},{10,28},{12,26},{14,24},{16,6},... | collective-permute-start | bytes 417800 | tf_op jit(solution)/shard_map/ppermute | solution.py:217
  30.0 8.7 %collective-permute-start.6 = (bf16[2,16,2176]{2,1,0:T(8,128)(2,1)S(1)}, bf16[2,16,2176]{2,1,0:T(8,128)(2,1)S(1)}, u32[]{:S(2)}, u32[]{:S(2)}) collective-permute-start(bf16[2,16,2176]{2,1,0:T(8,128)(2,1)S(1)} %get-tuple-element.34), channel_id=1, source_target_pairs={{0,20},{2,22},{4,16},{6,18},{8,28},{10,30},{12,24},{14,26},{16,4},... | collective-permute-start | bytes 417800 | tf_op jit(solution)/shard_map/ppermute | solution.py:217
  31.7 9.5 %collective-permute-start.7 = (bf16[2,16,2176]{2,1,0:T(8,128)(2,1)S(1)}, bf16[2,16,2176]{2,1,0:T(8,128)(2,1)S(1)}, u32[]{:S(2)}, u32[]{:S(2)}) collective-permute-start(bf16[2,16,2176]{2,1,0:T(8,128)(2,1)S(1)} %get-tuple-element.35), channel_id=1, source_target_pairs={{0,18},{2,16},{4,22},{6,20},{8,26},{10,24},{12,30},{14,28},{16,2},... | collective-permute-start | bytes 417800 | tf_op jit(solution)/shard_map/ppermute | solution.py:217
  34.9 6.7 %collective-permute-start.8 = (bf16[2,16,2176]{2,1,0:T(8,128)(2,1)S(1)}, bf16[2,16,2176]{2,1,0:T(8,128)(2,1)S(1)}, u32[]{:S(2)}, u32[]{:S(2)}) collective-permute-start(bf16[2,16,2176]{2,1,0:T(8,128)(2,1)S(1)} %get-tuple-element.36), channel_id=1, source_target_pairs={{0,6},{2,4},{4,2},{6,0},{8,14},{10,12},{12,10},{14,8},{16,22},{18,... | collective-permute-start | bytes 417800 | tf_op jit(solution)/shard_map/ppermute | solution.py:217
  34.9 6.7 %copy-start.2 = (s32[8]{0:T(128)S(1)}, s32[8]{0:T(128)}, u32[]{:S(2)}) copy-start(s32[8]{0:T(128)} %count_ref.1) | copy-start | bytes 100
  44.3 1.6 %collective-permute-start.9 = (f32[4,112,128]{2,1,0:T(8,128)S(1)}, f32[4,112,128]{2,1,0:T(8,128)S(1)}, u32[]{:S(2)}, u32[]{:S(2)}) collective-permute-start(f32[4,112,128]{2,1,0:T(8,128)S(1)} %get-tuple-element.37.mine_ref), channel_id=1, source_target_pairs={{0,1},{1,0},{2,3},{3,2},{4,5},{5,4},{6,7},{7,6},{8,9},{9,8},{10,11... | collective-permute-start | bytes 688136 | tf_op jit(solution)/shard_map/ppermute | solution.py:251

commit v8 on v7

--- a/solution.py
+++ b/solution.py
@@ -10,7 +10,7 @@
 adapter_scale_factor = 0.5
 MEMBERS = 8
 PIECE_ROWS = 16
-ORDER = (4, 2, 1, 7, 6, 5, 3)
+ORDER = (4, 2, 1, 3, 6, 5, 7)
 
 ANY = pl.BlockSpec(memory_space=pl.ANY)
 SMEM = pl.BlockSpec(memory_space=pltpu.SMEM)
@@ -83,32 +83,44 @@
         store(second, first)
 
 
-def shrink_kernel(halves, rank, count_ref, x_ref, *refs):
-    pieces, (shrunk_ref, up_ref, down) = refs[:-3], refs[-3:]
+def shrink_kernel(halves, rank, flips, count_ref, x_ref, *refs):
+    pieces, refs = refs[: len(flips)], refs[len(flips) :]
     slot_count = pieces[0].shape[0]
-    wide = down.shape[1] // halves
-    up_wide = up_ref.shape[1] // halves
     group_index = lax.axis_index("grp")
-    for flip, piece in zip((0,) + ORDER, pieces):
-        half = lax.rem(group_index ^ flip, halves)
+    half = lax.rem(group_index ^ flips[0], halves)
+    if len(refs) == 3:
+        shrunk_ref, up_ref, down = refs
+        sum_ref = None
+    else:
+        sum_ref, part_ref, shrunk_ref, up_ref, down = refs
+    wide = down.shape[1]
+    up_wide = up_ref.shape[1] if sum_ref is None else part_ref.shape[1]
+    if sum_ref is None:
+        up_at = slice(None)
+    else:
+        up_at = pl.ds(pl.multiple_of(half * up_wide, 128), up_wide)
+        up_ref[:, pl.ds(pl.multiple_of((1 - half) * up_wide, 128), up_wide)] = part_ref[...]
+    for flip, piece in zip(flips, pieces):
         for slot in range(slot_count):
             rows = pl.ds(slot * rank + flip // halves * PIECE_ROWS, PIECE_ROWS)
-            down[rows, pl.ds(pl.multiple_of(half * wide, 128), wide)] = piece[slot, :, :wide]
-            up_ref[rows, pl.ds(pl.multiple_of(half * up_wide, 128), up_wide)] = piece[
-                slot, :, wide:
-            ]
+            down[rows, :] = piece[slot, :, :wide]
+            up_ref[rows, up_at] = piece[slot, :, wide:]
+    columns = pl.ds(pl.multiple_of(half * wide, 128), wide)
     rows = shrunk_ref.shape[1]
     slot_of = lax.broadcasted_iota(jnp.int32, shrunk_ref.shape[1:], 1) // rank
     live_count = count_ref[group_index]
     for step in range(x_ref.shape[0]):
         product = lax.dot_general(
-            x_ref[step], down[...], (((1,), (1,)), ((), ())), preferred_element_type=jnp.float32
+            x_ref[step, :, columns],
+            down[...],
+            (((1,), (1,)), ((), ())),
+            preferred_element_type=jnp.float32,
         )
         packed = jnp.zeros(shrunk_ref.shape[1:], jnp.float32)
         for slot in range(slot_count):
             keep = (slot_of == slot) & (slot < live_count)
             packed = jnp.where(keep, product[slot * rows : (slot + 1) * rows], packed)
-        shrunk_ref[step] = packed
+        shrunk_ref[step] = packed if sum_ref is None else packed + sum_ref[step]
 
 
 def expand_kernel(
@@ -231,23 +243,32 @@
     )(late)
 
     both = slot_count * rank
-    shrunk, up = pl.pallas_call(
-        functools.partial(shrink_kernel, halves, rank),
-        out_shape=[
-            jax.ShapeDtypeStruct((step_count, block_rows, both), f32),
-            jax.ShapeDtypeStruct((both, share), bf16),
-        ],
-        in_specs=[SMEM] + [VMEM] * (1 + MEMBERS),
-        out_specs=[VMEM, VMEM],
-        scratch_shapes=[pltpu.VMEM((both, half_width), bf16)],
-        compiler_params=pltpu.CompilerParams(vmem_limit_bytes=12 << 20),
-        cost_estimate=pl.CostEstimate(
-            flops=2 * rows * half_width * both,
-            bytes_accessed=2 * rows * half_width,
-            transcendentals=0,
-        ),
-        name="shrink",
-    )(block_count, near_hidden, own, *got)
+    got[:5] = lax.optimization_barrier(tuple(got[:5]))
+    arrived = [own, *got]
+    parts = ()
+    for change in range(halves):
+        mine_at = [at for at, flip in enumerate((0,) + ORDER) if flip % halves == change]
+        up_width = share if change else share // halves
+        parts = pl.pallas_call(
+            functools.partial(
+                shrink_kernel, halves, rank, [((0,) + ORDER)[at] for at in mine_at]
+            ),
+            out_shape=[
+                jax.ShapeDtypeStruct((step_count, block_rows, both), f32),
+                jax.ShapeDtypeStruct((both, up_width), bf16),
+            ],
+            in_specs=[SMEM] + [VMEM] * (1 + len(mine_at) + len(parts)),
+            out_specs=[VMEM, VMEM],
+            scratch_shapes=[pltpu.VMEM((both, half_width // halves), bf16)],
+            compiler_params=pltpu.CompilerParams(vmem_limit_bytes=12 << 20),
+            cost_estimate=pl.CostEstimate(
+                flops=2 * rows * half_width * both // halves,
+                bytes_accessed=2 * rows * half_width // halves,
+                transcendentals=0,
+            ),
+            name="shrink",
+        )(block_count, near_hidden, *(arrived[at] for at in mine_at), *parts)
+    shrunk, up = parts
     shrunk_other = lax.ppermute(shrunk, "tp", swap)
 
     return pl.pallas_call(

time: 47.3 us -> 46.2 us (0.977)
  starting transfers between devices: 18.9 us -> 17.8 us
  Pallas kernels: 16.9 us -> 17.6 us
  waiting for transfers between devices: 11 us -> 10.4 us
    ppermute x7, starting transfers between devices: 9.92 us -> 8.82 us  [local(): got.append(lax.ppermute(send, ('rep', 'grp'), pairs))]
    pallas_call x1 -> x2, Pallas kernels: 2.65 us -> 3.32 us  [local(): pl.pallas_call(functools.partial(shrink_kernel, halves, rank, [((0,) + OR...]
    ppermute x7, waiting for transfers between devices: 3.58 us -> 2.94 us  [local(): got.append(lax.ppermute(send, ('rep', 'grp'), pairs))]
  transfers between devices with their start and end apart: 11 -> 11, of which waited for: 6 -> 6; matrix products, arithmetic and copies ran while one was open for 0% -> 0% of each run, Pallas kernels for 23% -> 27%
where the time goes in v8:
time: 46.2 us; the launch traced here: 45.9 us
  starting transfers between devices  17.8 us (39%)
  Pallas kernels  17.6 us (38%)
  waiting for transfers between devices  10.4 us (23%)
    ppermute x7, starting transfers between devices, local(): got.append(lax.ppermute(send, ('rep', 'grp'), pairs))  8.82 us
    pallas_call x1, Pallas kernels, local(): pl.pallas_call(base_kernel, grid=(chunk_count,), out_shape=[jax.ShapeDtyp...  7.56 us
    all_to_all x1, starting transfers between devices, local(): held = lax.all_to_all(packed, 'grp', 0, 0, tiled=True)  7.29 us
    all_to_all x1, waiting for transfers between devices, local(): held = lax.all_to_all(packed, 'grp', 0, 0, tiled=True)  3.89 us
    pallas_call x2, Pallas kernels, local(): pl.pallas_call(functools.partial(shrink_kernel, halves, rank, [((0,) + OR...  3.32 us
    pallas_call x1, Pallas kernels, local(): pl.pallas_call(stage_kernel, out_shape=pltpu.VMEM(hidden.shape, bf16), in...  3.1 us
    ppermute x7, waiting for transfers between devices, local(): got.append(lax.ppermute(send, ('rep', 'grp'), pairs))  2.94 us
    ppermute x1, waiting for transfers between devices, local(): wanted.append(lax.ppermute(asked, 'rep', pairs))  2.08 us
  transfers between devices with their start and end apart: 11, of which 6 were waited for; matrix products, arithmetic and copies ran while one was open for 0% of the time, Pallas kernels for 27%

profile of v8, /device:TPU:0, one launch (start us, length us, event | category | flops | bytes accessed | tf_op | source)
XLA Modules:
  0.0 45.9 jit_solution(5649643641044202246)
XLA Ops:
  0.0 1.8 %pack.1 = bf16[8,16,2176]{2,1,0:T(8,128)(2,1)} custom-call(bf16[64,4096]{1,0:T(8,128)(2,1)} %bitcast.7, bf16[64,512]{1,0:T(8,128)(2,1)} %bitcast.8), custom_call_target="tpu_custom_call" | custom-call | tf_op jit(solution)/shard_map/pack/pallas_call | solution.py:168
  1.8 7.3 %all-to-all-start = ((bf16[8,16,2176]{2,1,0:T(8,128)(2,1)}), bf16[8,16,2176]{2,1,0:T(8,128)(2,1)S(1)}, u32[]{:S(2)}, u32[]{:S(2)}) async-start(bf16[8,16,2176]{2,1,0:T(8,128)(2,1)} %pack.1), calls=%async_computation | async-start | bytes 1114112 | tf_op jit(solution)/shard_map/all_to_all | solution.py:181
  9.1 7.6 %base.1 = (f32[896,256]{1,0:T(8,128)S(1)}, f32[896,256]{1,0:T(8,128)S(1)}) custom-call(bf16[4,224,4096]{2,1,0:T(8,128)(2,1)} %x_ref.2, bf16[4096,512]{1,0:T(8,128)(2,1)} %weight_ref.1), custom_call_target="tpu_custom_call" | custom-call | flops 3758096384 | bytes 9175040 | tf_op jit(solution)/shard_map/base/pallas_call | solution.py:191
  16.7 0.1 collective-permute-start.1
  16.8 1.6 %collective-permute-start = (s32[2,8]{1,0:T(2,128)S(1)}, s32[2,8]{1,0:T(2,128)S(1)}, u32[]{:S(2)}, u32[]{:S(2)}) collective-permute-start(s32[2,8]{1,0:T(2,128)S(1)} %bitcast.5), channel_id=1, source_target_pairs={{0,16},{16,0},{1,17},{17,1},{2,18},{18,2},{3,19},{19,3},{4,20},{20... | collective-permute-start | bytes 200 | tf_op jit(solution)/shard_map/ppermute | solution.py:186
  18.4 2.1 %collective-permute-done.refs_1_ = s32[2,8]{1,0:T(2,128)S(1)} collective-permute-done((s32[2,8]{1,0:T(2,128)S(1)}, s32[2,8]{1,0:T(2,128)S(1)}, u32[]{:S(2)}, u32[]{:S(2)}) %collective-permute-start) | collective-permute-done | bytes 96 | tf_op jit(solution)/shard_map/ppermute | solution.py:186
  20.4 3.9 %all-to-all-done.refs_2_ = bf16[8,16,2176]{2,1,0:T(8,128)(2,1)S(1)} async-done(((bf16[8,16,2176]{2,1,0:T(8,128)(2,1)}), bf16[8,16,2176]{2,1,0:T(8,128)(2,1)S(1)}, u32[]{:S(2)}, u32[]{:S(2)}) %all-to-all-start) | async-done | bytes 557088 | tf_op jit(solution)/shard_map/all_to_all | solution.py:181
  24.3 0.7 %select.1 = (bf16[2,16,2176]{2,1,0:T(8,128)(2,1)S(1)}, bf16[2,16,2176]{2,1,0:T(8,128)(2,1)S(1)}, bf16[2,16,2176]{2,1,0:T(8,128)(2,1)S(1)}, bf16[2,16,2176]{2,1,0...) custom-call(s32[8]{0:T(128)S(1)} %copy-done.2, ...), custom_call_target="tpu_custom_call" | custom-call | tf_op jit(solution)/shard_map/select/pallas_call | solution.py:214
  25.0 1.6 %collective-permute-start.2 = (bf16[2,16,2176]{2,1,0:T(8,128)(2,1)S(1)}, bf16[2,16,2176]{2,1,0:T(8,128)(2,1)S(1)}, u32[]{:S(2)}, u32[]{:S(2)}) collective-permute-start(bf16[2,16,2176]{2,1,0:T(8,128)(2,1)S(1)} %get-tuple-element.36), channel_id=1, source_target_pairs={{0,16},{2,18},{4,20},{6,22},{8,24},{10,26},{12,28},{14,30},{16,0},... | collective-permute-start | bytes 417800 | tf_op jit(solution)/shard_map/ppermute | solution.py:229
  26.6 0.7 %collective-permute-start.3 = (bf16[2,16,2176]{2,1,0:T(8,128)(2,1)S(1)}, bf16[2,16,2176]{2,1,0:T(8,128)(2,1)S(1)}, u32[]{:S(2)}, u32[]{:S(2)}) collective-permute-start(bf16[2,16,2176]{2,1,0:T(8,128)(2,1)S(1)} %get-tuple-element.37), channel_id=1, source_target_pairs={{0,4},{2,6},{4,0},{6,2},{8,12},{10,14},{12,8},{14,10},{16,20},{18,... | collective-permute-start | bytes 417800 | tf_op jit(solution)/shard_map/ppermute | solution.py:229
  27.3 0.7 %collective-permute-start.4 = (bf16[2,16,2176]{2,1,0:T(8,128)(2,1)S(1)}, bf16[2,16,2176]{2,1,0:T(8,128)(2,1)S(1)}, u32[]{:S(2)}, u32[]{:S(2)}) collective-permute-start(bf16[2,16,2176]{2,1,0:T(8,128)(2,1)S(1)} %get-tuple-element.38), channel_id=1, source_target_pairs={{0,2},{2,0},{4,6},{6,4},{8,10},{10,8},{12,14},{14,12},{16,18},{18,... | collective-permute-start | bytes 417800 | tf_op jit(solution)/shard_map/ppermute | solution.py:229
  28.0 2.0 %collective-permute-start.5 = (bf16[2,16,2176]{2,1,0:T(8,128)(2,1)S(1)}, bf16[2,16,2176]{2,1,0:T(8,128)(2,1)S(1)}, u32[]{:S(2)}, u32[]{:S(2)}) collective-permute-start(bf16[2,16,2176]{2,1,0:T(8,128)(2,1)S(1)} %get-tuple-element.39), channel_id=1, source_target_pairs={{0,6},{2,4},{4,2},{6,0},{8,14},{10,12},{12,10},{14,8},{16,22},{18,... | collective-permute-start | bytes 417800 | tf_op jit(solution)/shard_map/ppermute | solution.py:229
  30.1 0.7 %collective-permute-start.6 = (bf16[2,16,2176]{2,1,0:T(8,128)(2,1)S(1)}, bf16[2,16,2176]{2,1,0:T(8,128)(2,1)S(1)}, u32[]{:S(2)}, u32[]{:S(2)}) collective-permute-start(bf16[2,16,2176]{2,1,0:T(8,128)(2,1)S(1)} %get-tuple-element.40), channel_id=1, source_target_pairs={{0,20},{2,22},{4,16},{6,18},{8,28},{10,30},{12,24},{14,26},{16,4},... | collective-permute-start | bytes 417800 | tf_op jit(solution)/shard_map/ppermute | solution.py:229
  30.7 1.8 %collective-permute-start.7 = (bf16[2,16,2176]{2,1,0:T(8,128)(2,1)S(1)}, bf16[2,16,2176]{2,1,0:T(8,128)(2,1)S(1)}, u32[]{:S(2)}, u32[]{:S(2)}) collective-permute-start(bf16[2,16,2176]{2,1,0:T(8,128)(2,1)S(1)} %get-tuple-element.43), channel_id=1, source_target_pairs={{0,18},{2,16},{4,22},{6,20},{8,26},{10,24},{12,30},{14,28},{16,2},... | collective-permute-start | bytes 417800 | tf_op jit(solution)/shard_map/ppermute | solution.py:229
  32.5 0.6 %collective-permute-done.3.refs_2_ = bf16[2,16,2176]{2,1,0:T(8,128)(2,1)S(1)} collective-permute-done((bf16[2,16,2176]{2,1,0:T(8,128)(2,1)S(1)}, bf16[2,16,2176]{2,1,0:T(8,128)(2,1)S(1)}, u32[]{:S(2)}, u32[]{:S(2)}) %collective-permute-start.3) | collective-permute-done | bytes 139296 | tf_op jit(solution)/shard_map/ppermute | solution.py:229
  33.1 1.3 %collective-permute-start.8 = (bf16[2,16,2176]{2,1,0:T(8,128)(2,1)S(1)}, bf16[2,16,2176]{2,1,0:T(8,128)(2,1)S(1)}, u32[]{:S(2)}, u32[]{:S(2)}) collective-permute-start(bf16[2,16,2176]{2,1,0:T(8,128)(2,1)S(1)} %get-tuple-element.44), channel_id=1, source_target_pairs={{0,22},{2,20},{4,18},{6,16},{8,30},{10,28},{12,26},{14,24},{16,6},... | collective-permute-start | bytes 417800 | tf_op jit(solution)/shard_map/ppermute | solution.py:229
  34.4 3.1 %stage.1.x_ref = bf16[4,224,4096]{2,1,0:T(8,128)(2,1)S(1)} custom-call(bf16[4,224,4096]{2,1,0:T(8,128)(2,1)} %x_ref.2), custom_call_target="tpu_custom_call" | custom-call | bytes 14680064 | tf_op jit(solution)/shard_map/stage/pallas_call | solution.py:232
  37.5 0.9 %collective-permute-done.4.refs_0_ = bf16[2,16,2176]{2,1,0:T(8,128)(2,1)S(1)} collective-permute-done((bf16[2,16,2176]{2,1,0:T(8,128)(2,1)S(1)}, bf16[2,16,2176]{2,1,0:T(8,128)(2,1)S(1)}, u32[]{:S(2)}, u32[]{:S(2)}) %collective-permute-start.4) | collective-permute-done | bytes 139296 | tf_op jit(solution)/shard_map/ppermute | solution.py:229
  38.5 1.7 %shrink.2 = (f32[4,112,128]{2,1,0:T(8,128)S(1)}, bf16[128,128]{1,0:T(8,128)(2,1)S(1)}) custom-call(s32[8]{0:T(128)S(1)} %copy-done, bf16[4,224,4096]{2,1,0:T(8,128)(2,1)S(1)} %stage.1.x_ref, bf16[2,16,2176]{2,1,0:T(8,128)(2,1)S(1)} %get-tuple-element.45.refs_0_, bf16[2,16,2176]{2,1,0:T(8,128)(2,1)S(1)} %collective-permute-done.2.refs_1_, ...), custom_call_target="tpu_custom_call" | custom-call | flops 469762048 | bytes 3670016 | tf_op jit(solution)/shard_map/shrink/pallas_call | solution.py:252
  40.1 1.4 %collective-permute-done.7.refs_2_ = bf16[2,16,2176]{2,1,0:T(8,128)(2,1)S(1)} collective-permute-done((bf16[2,16,2176]{2,1,0:T(8,128)(2,1)S(1)}, bf16[2,16,2176]{2,1,0:T(8,128)(2,1)S(1)}, u32[]{:S(2)}, u32[]{:S(2)}) %collective-permute-start.7) | collective-permute-done | bytes 139296 | tf_op jit(solution)/shard_map/ppermute | solution.py:229
  41.6 1.7 %shrink.3 = (f32[4,112,128]{2,1,0:T(8,128)S(1)}, bf16[128,256]{1,0:T(8,128)(2,1)S(1)}) custom-call(s32[8]{0:T(128)S(1)} %copy-done, bf16[4,224,4096]{2,1,0:T(8,128)(2,1)S(1)} %stage.1.x_ref, bf16[2,16,2176]{2,1,0:T(8,128)(2,1)S(1)} %collective-permute-done.4.refs_0_, bf16[2,16,2176]{2,1,0:T(8,128)(2,1)S(1)} %collective-permute-done.5.refs_1_, ...), custom_call_target="tpu_custom_call" | custom-call | flops 469762048 | bytes 3670016 | tf_op jit(solution)/shard_map/shrink/pallas_call | solution.py:252
  43.2 0.1 collective-permute-start.9
  43.3 1.5 %collective-permute-done.9.theirs_ref = f32[4,112,128]{2,1,0:T(8,128)S(1)} collective-permute-done((f32[4,112,128]{2,1,0:T(8,128)S(1)}, f32[4,112,128]{2,1,0:T(8,128)S(1)}, u32[]{:S(2)}, u32[]{:S(2)}) %collective-permute-start.9) | collective-permute-done | bytes 229408 | tf_op jit(solution)/shard_map/ppermute | solution.py:272
  44.8 1.1 %expand.1 = bf16[4,224,256]{2,1,0:T(8,128)(2,1)} custom-call(f32[4,112,128]{2,1,0:T(8,128)S(1)} %get-tuple-element.51.mine_ref, f32[4,112,128]{2,1,0:T(8,128)S(1)} %collective-permute-done.9.theirs_ref, bf16[128,256]{1,0:T(8,128)(2,1)S(1)} %get-tuple-element.52.up_ref, f32[896,256]{1,0:T(8,128)S(1)} %get-tuple-element.53.base_ref, ...), custom_call_target="tpu_custom_call" | custom-call | tf_op jit(solution)/shard_map/expand/pallas_call | solution.py:274
  (11 shorter events, 0.0 us)
Async XLA Ops:
  1.8 15.0 %copy-start.1 = (s32[8,2]{0,1:T(2,128)S(1)}, s32[8,2]{0,1:T(2,128)}, u32[]{:S(2)}) copy-start(s32[8,2]{0,1:T(2,128)} %param.12) | copy-start | bytes 196
  1.8 22.5 %copy-start.2 = (s32[8]{0:T(128)S(1)}, s32[8]{0:T(128)}, u32[]{:S(2)}) copy-start(s32[8]{0:T(128)} %home_ref.1) | copy-start | bytes 100
  1.8 22.5 %all-to-all-start = ((bf16[8,16,2176]{2,1,0:T(8,128)(2,1)}), bf16[8,16,2176]{2,1,0:T(8,128)(2,1)S(1)}, u32[]{:S(2)}, u32[]{:S(2)}) async-start(bf16[8,16,2176]{2,1,0:T(8,128)(2,1)} %pack.1), calls=%async_computation | async-start | bytes 1114112 | tf_op jit(solution)/shard_map/all_to_all | solution.py:181
  16.7 3.7 %collective-permute-start.1 = (f32[896,256]{1,0:T(8,128)S(1)}, f32[896,256]{1,0:T(8,128)S(1)}, u32[]{:S(2)}, u32[]{:S(2)}) collective-permute-start(f32[896,256]{1,0:T(8,128)S(1)} %get-tuple-element.31), channel_id=1, source_target_pairs={{0,1},{1,0},{2,3},{3,2},{4,5},{5,4},{6,7},{7,6},{8,9},{9,8},{10,11... | collective-permute-start | bytes 2752520 | tf_op jit(solution)/shard_map/ppermute | solution.py:209
  16.8 3.6 %collective-permute-start = (s32[2,8]{1,0:T(2,128)S(1)}, s32[2,8]{1,0:T(2,128)S(1)}, u32[]{:S(2)}, u32[]{:S(2)}) collective-permute-start(s32[2,8]{1,0:T(2,128)S(1)} %bitcast.5), channel_id=1, source_target_pairs={{0,16},{16,0},{1,17},{17,1},{2,18},{18,2},{3,19},{19,3},{4,20},{20... | collective-permute-start | bytes 200 | tf_op jit(solution)/shard_map/ppermute | solution.py:186
  25.0 5.7 %collective-permute-start.2 = (bf16[2,16,2176]{2,1,0:T(8,128)(2,1)S(1)}, bf16[2,16,2176]{2,1,0:T(8,128)(2,1)S(1)}, u32[]{:S(2)}, u32[]{:S(2)}) collective-permute-start(bf16[2,16,2176]{2,1,0:T(8,128)(2,1)S(1)} %get-tuple-element.36), channel_id=1, source_target_pairs={{0,16},{2,18},{4,20},{6,22},{8,24},{10,26},{12,28},{14,30},{16,0},... | collective-permute-start | bytes 417800 | tf_op jit(solution)/shard_map/ppermute | solution.py:229
  26.6 6.5 %collective-permute-start.3 = (bf16[2,16,2176]{2,1,0:T(8,128)(2,1)S(1)}, bf16[2,16,2176]{2,1,0:T(8,128)(2,1)S(1)}, u32[]{:S(2)}, u32[]{:S(2)}) collective-permute-start(bf16[2,16,2176]{2,1,0:T(8,128)(2,1)S(1)} %get-tuple-element.37), channel_id=1, source_target_pairs={{0,4},{2,6},{4,0},{6,2},{8,12},{10,14},{12,8},{14,10},{16,20},{18,... | collective-permute-start | bytes 417800 | tf_op jit(solution)/shard_map/ppermute | solution.py:229
  27.3 11.2 %collective-permute-start.4 = (bf16[2,16,2176]{2,1,0:T(8,128)(2,1)S(1)}, bf16[2,16,2176]{2,1,0:T(8,128)(2,1)S(1)}, u32[]{:S(2)}, u32[]{:S(2)}) collective-permute-start(bf16[2,16,2176]{2,1,0:T(8,128)(2,1)S(1)} %get-tuple-element.38), channel_id=1, source_target_pairs={{0,2},{2,0},{4,6},{6,4},{8,10},{10,8},{12,14},{14,12},{16,18},{18,... | collective-permute-start | bytes 417800 | tf_op jit(solution)/shard_map/ppermute | solution.py:229
  28.0 10.4 %collective-permute-start.5 = (bf16[2,16,2176]{2,1,0:T(8,128)(2,1)S(1)}, bf16[2,16,2176]{2,1,0:T(8,128)(2,1)S(1)}, u32[]{:S(2)}, u32[]{:S(2)}) collective-permute-start(bf16[2,16,2176]{2,1,0:T(8,128)(2,1)S(1)} %get-tuple-element.39), channel_id=1, source_target_pairs={{0,6},{2,4},{4,2},{6,0},{8,14},{10,12},{12,10},{14,8},{16,22},{18,... | collective-permute-start | bytes 417800 | tf_op jit(solution)/shard_map/ppermute | solution.py:229
  30.1 8.4 %collective-permute-start.6 = (bf16[2,16,2176]{2,1,0:T(8,128)(2,1)S(1)}, bf16[2,16,2176]{2,1,0:T(8,128)(2,1)S(1)}, u32[]{:S(2)}, u32[]{:S(2)}) collective-permute-start(bf16[2,16,2176]{2,1,0:T(8,128)(2,1)S(1)} %get-tuple-element.40), channel_id=1, source_target_pairs={{0,20},{2,22},{4,16},{6,18},{8,28},{10,30},{12,24},{14,26},{16,4},... | collective-permute-start | bytes 417800 | tf_op jit(solution)/shard_map/ppermute | solution.py:229
  30.7 10.8 %collective-permute-start.7 = (bf16[2,16,2176]{2,1,0:T(8,128)(2,1)S(1)}, bf16[2,16,2176]{2,1,0:T(8,128)(2,1)S(1)}, u32[]{:S(2)}, u32[]{:S(2)}) collective-permute-start(bf16[2,16,2176]{2,1,0:T(8,128)(2,1)S(1)} %get-tuple-element.43), channel_id=1, source_target_pairs={{0,18},{2,16},{4,22},{6,20},{8,26},{10,24},{12,30},{14,28},{16,2},... | collective-permute-start | bytes 417800 | tf_op jit(solution)/shard_map/ppermute | solution.py:229
  33.1 8.4 %collective-permute-start.8 = (bf16[2,16,2176]{2,1,0:T(8,128)(2,1)S(1)}, bf16[2,16,2176]{2,1,0:T(8,128)(2,1)S(1)}, u32[]{:S(2)}, u32[]{:S(2)}) collective-permute-start(bf16[2,16,2176]{2,1,0:T(8,128)(2,1)S(1)} %get-tuple-element.44), channel_id=1, source_target_pairs={{0,22},{2,20},{4,18},{6,16},{8,30},{10,28},{12,26},{14,24},{16,6},... | collective-permute-start | bytes 417800 | tf_op jit(solution)/shard_map/ppermute | solution.py:229
  34.4 4.1 %copy-start = (s32[8]{0:T(128)S(1)}, s32[8]{0:T(128)}, u32[]{:S(2)}) copy-start(s32[8]{0:T(128)} %count_ref.3) | copy-start | bytes 100
  43.2 1.6 %collective-permute-start.9 = (f32[4,112,128]{2,1,0:T(8,128)S(1)}, f32[4,112,128]{2,1,0:T(8,128)S(1)}, u32[]{:S(2)}, u32[]{:S(2)}) collective-permute-start(f32[4,112,128]{2,1,0:T(8,128)S(1)} %get-tuple-element.51.mine_ref), channel_id=1, source_target_pairs={{0,1},{1,0},{2,3},{3,2},{4,5},{5,4},{6,7},{7,6},{8,9},{9,8},{10,11... | collective-permute-start | bytes 688136 | tf_op jit(solution)/shard_map/ppermute | solution.py:272

commit v9 on v8

--- a/solution.py
+++ b/solution.py
@@ -130,6 +130,7 @@
     slot_of = lax.broadcasted_iota(jnp.int32, mine_ref.shape[1:], 1) // rank
     up = up_ref[...]
     up_thrice = jnp.concatenate([up, up, up], axis=0)
+    terms = []
     for step in range(mine_ref.shape[0]):
         shrunk = mine_ref[step] + theirs_ref[step]
         top = shrunk.astype(jnp.bfloat16)
@@ -138,13 +139,19 @@
         low = (rest - mid.astype(jnp.float32)).astype(jnp.bfloat16)
         zero = jnp.zeros_like(top)
         for slot in range(slot_count):
-            terms = jnp.concatenate(
-                [jnp.where(slot_of == slot, term, zero) for term in (top, mid, low)], axis=1
+            terms.append(
+                jnp.concatenate(
+                    [jnp.where(slot_of == slot, term, zero) for term in (top, mid, low)], axis=1
+                )
             )
-            expanded = jnp.dot(terms, up_thrice, preferred_element_type=jnp.float32)
-            at = pl.ds((step * slot_count + slot) * rows, rows)
-            total = base_ref[at, :] + base_other_ref[at, :]
-            done[step, pl.ds(slot * rows, rows), :] = (total + adapter_scale_factor * expanded).astype(done.dtype)
+    products = jnp.dot(
+        jnp.concatenate(terms, axis=0), up_thrice, preferred_element_type=jnp.float32
+    )
+    tall = slot_count * rows
+    for step in range(mine_ref.shape[0]):
+        at = slice(step * tall, (step + 1) * tall)
+        total = base_ref[at, :] + base_other_ref[at, :]
+        done[step] = (total + adapter_scale_factor * products[at]).astype(done.dtype)
         pltpu.make_async_copy(done.at[step], out_ref.at[step], sem.at[step]).start()
     for step in range(mine_ref.shape[0]):
         pltpu.make_async_copy(done.at[step], out_ref.at[step], sem.at[step]).wait()

time: 46.2 us -> 46.1 us (level)
  no operation moved by 1% of the time
where the time goes in v9:
time: 46.1 us; the launch traced here: 45.9 us
  starting transfers between devices  17.8 us (39%)
  Pallas kernels  17.5 us (38%)
  waiting for transfers between devices  10.4 us (23%)
    ppermute x7, starting transfers between devices, local(): got.append(lax.ppermute(send, ('rep', 'grp'), pairs))  8.82 us
    pallas_call x1, Pallas kernels, local(): pl.pallas_call(base_kernel, grid=(chunk_count,), out_shape=[jax.ShapeDtyp...  7.56 us
    all_to_all x1, starting transfers between devices, local(): held = lax.all_to_all(packed, 'grp', 0, 0, tiled=True)  7.29 us
    all_to_all x1, waiting for transfers between devices, local(): held = lax.all_to_all(packed, 'grp', 0, 0, tiled=True)  3.89 us
    pallas_call x2, Pallas kernels, local(): pl.pallas_call(functools.partial(shrink_kernel, halves, rank, [((0,) + OR...  3.32 us
    pallas_call x1, Pallas kernels, local(): pl.pallas_call(stage_kernel, out_shape=pltpu.VMEM(hidden.shape, bf16), in...  3.1 us
    ppermute x7, waiting for transfers between devices, local(): got.append(lax.ppermute(send, ('rep', 'grp'), pairs))  2.94 us
    ppermute x1, waiting for transfers between devices, local(): wanted.append(lax.ppermute(asked, 'rep', pairs))  2.08 us
  transfers between devices with their start and end apart: 11, of which 6 were waited for; matrix products, arithmetic and copies ran while one was open for 0% of the time, Pallas kernels for 27%

profile of v9, /device:TPU:0, one launch (start us, length us, event | category | flops | bytes accessed | tf_op | source)
XLA Modules:
  0.0 45.9 jit_solution(5425439966418272097)
XLA Ops:
  0.0 1.8 %pack.1 = bf16[8,16,2176]{2,1,0:T(8,128)(2,1)} custom-call(bf16[64,4096]{1,0:T(8,128)(2,1)} %bitcast.7, bf16[64,512]{1,0:T(8,128)(2,1)} %bitcast.8), custom_call_target="tpu_custom_call" | custom-call | tf_op jit(solution)/shard_map/pack/pallas_call | solution.py:175
  1.8 7.3 %all-to-all-start = ((bf16[8,16,2176]{2,1,0:T(8,128)(2,1)}), bf16[8,16,2176]{2,1,0:T(8,128)(2,1)S(1)}, u32[]{:S(2)}, u32[]{:S(2)}) async-start(bf16[8,16,2176]{2,1,0:T(8,128)(2,1)} %pack.1), calls=%async_computation | async-start | bytes 1114112 | tf_op jit(solution)/shard_map/all_to_all | solution.py:188
  9.1 7.6 %base.1 = (f32[896,256]{1,0:T(8,128)S(1)}, f32[896,256]{1,0:T(8,128)S(1)}) custom-call(bf16[4,224,4096]{2,1,0:T(8,128)(2,1)} %x_ref.2, bf16[4096,512]{1,0:T(8,128)(2,1)} %weight_ref.1), custom_call_target="tpu_custom_call" | custom-call | flops 3758096384 | bytes 9175040 | tf_op jit(solution)/shard_map/base/pallas_call | solution.py:198
  16.7 0.1 collective-permute-start.1
  16.8 1.6 %collective-permute-start = (s32[2,8]{1,0:T(2,128)S(1)}, s32[2,8]{1,0:T(2,128)S(1)}, u32[]{:S(2)}, u32[]{:S(2)}) collective-permute-start(s32[2,8]{1,0:T(2,128)S(1)} %bitcast.5), channel_id=1, source_target_pairs={{0,16},{16,0},{1,17},{17,1},{2,18},{18,2},{3,19},{19,3},{4,20},{20... | collective-permute-start | bytes 200 | tf_op jit(solution)/shard_map/ppermute | solution.py:193
  18.4 2.1 %collective-permute-done.refs_1_ = s32[2,8]{1,0:T(2,128)S(1)} collective-permute-done((s32[2,8]{1,0:T(2,128)S(1)}, s32[2,8]{1,0:T(2,128)S(1)}, u32[]{:S(2)}, u32[]{:S(2)}) %collective-permute-start) | collective-permute-done | bytes 96 | tf_op jit(solution)/shard_map/ppermute | solution.py:193
  20.4 3.9 %all-to-all-done.refs_2_ = bf16[8,16,2176]{2,1,0:T(8,128)(2,1)S(1)} async-done(((bf16[8,16,2176]{2,1,0:T(8,128)(2,1)}), bf16[8,16,2176]{2,1,0:T(8,128)(2,1)S(1)}, u32[]{:S(2)}, u32[]{:S(2)}) %all-to-all-start) | async-done | bytes 557088 | tf_op jit(solution)/shard_map/all_to_all | solution.py:188
  24.3 0.7 %select.1 = (bf16[2,16,2176]{2,1,0:T(8,128)(2,1)S(1)}, bf16[2,16,2176]{2,1,0:T(8,128)(2,1)S(1)}, bf16[2,16,2176]{2,1,0:T(8,128)(2,1)S(1)}, bf16[2,16,2176]{2,1,0...) custom-call(s32[8]{0:T(128)S(1)} %copy-done.2, ...), custom_call_target="tpu_custom_call" | custom-call | tf_op jit(solution)/shard_map/select/pallas_call | solution.py:221
  25.0 1.6 %collective-permute-start.2 = (bf16[2,16,2176]{2,1,0:T(8,128)(2,1)S(1)}, bf16[2,16,2176]{2,1,0:T(8,128)(2,1)S(1)}, u32[]{:S(2)}, u32[]{:S(2)}) collective-permute-start(bf16[2,16,2176]{2,1,0:T(8,128)(2,1)S(1)} %get-tuple-element.36), channel_id=1, source_target_pairs={{0,16},{2,18},{4,20},{6,22},{8,24},{10,26},{12,28},{14,30},{16,0},... | collective-permute-start | bytes 417800 | tf_op jit(solution)/shard_map/ppermute | solution.py:236
  26.6 0.7 %collective-permute-start.3 = (bf16[2,16,2176]{2,1,0:T(8,128)(2,1)S(1)}, bf16[2,16,2176]{2,1,0:T(8,128)(2,1)S(1)}, u32[]{:S(2)}, u32[]{:S(2)}) collective-permute-start(bf16[2,16,2176]{2,1,0:T(8,128)(2,1)S(1)} %get-tuple-element.37), channel_id=1, source_target_pairs={{0,4},{2,6},{4,0},{6,2},{8,12},{10,14},{12,8},{14,10},{16,20},{18,... | collective-permute-start | bytes 417800 | tf_op jit(solution)/shard_map/ppermute | solution.py:236
  27.3 0.7 %collective-permute-start.4 = (bf16[2,16,2176]{2,1,0:T(8,128)(2,1)S(1)}, bf16[2,16,2176]{2,1,0:T(8,128)(2,1)S(1)}, u32[]{:S(2)}, u32[]{:S(2)}) collective-permute-start(bf16[2,16,2176]{2,1,0:T(8,128)(2,1)S(1)} %get-tuple-element.38), channel_id=1, source_target_pairs={{0,2},{2,0},{4,6},{6,4},{8,10},{10,8},{12,14},{14,12},{16,18},{18,... | collective-permute-start | bytes 417800 | tf_op jit(solution)/shard_map/ppermute | solution.py:236
  28.0 2.0 %collective-permute-start.5 = (bf16[2,16,2176]{2,1,0:T(8,128)(2,1)S(1)}, bf16[2,16,2176]{2,1,0:T(8,128)(2,1)S(1)}, u32[]{:S(2)}, u32[]{:S(2)}) collective-permute-start(bf16[2,16,2176]{2,1,0:T(8,128)(2,1)S(1)} %get-tuple-element.39), channel_id=1, source_target_pairs={{0,6},{2,4},{4,2},{6,0},{8,14},{10,12},{12,10},{14,8},{16,22},{18,... | collective-permute-start | bytes 417800 | tf_op jit(solution)/shard_map/ppermute | solution.py:236
  30.1 0.7 %collective-permute-start.6 = (bf16[2,16,2176]{2,1,0:T(8,128)(2,1)S(1)}, bf16[2,16,2176]{2,1,0:T(8,128)(2,1)S(1)}, u32[]{:S(2)}, u32[]{:S(2)}) collective-permute-start(bf16[2,16,2176]{2,1,0:T(8,128)(2,1)S(1)} %get-tuple-element.40), channel_id=1, source_target_pairs={{0,20},{2,22},{4,16},{6,18},{8,28},{10,30},{12,24},{14,26},{16,4},... | collective-permute-start | bytes 417800 | tf_op jit(solution)/shard_map/ppermute | solution.py:236
  30.7 1.8 %collective-permute-start.7 = (bf16[2,16,2176]{2,1,0:T(8,128)(2,1)S(1)}, bf16[2,16,2176]{2,1,0:T(8,128)(2,1)S(1)}, u32[]{:S(2)}, u32[]{:S(2)}) collective-permute-start(bf16[2,16,2176]{2,1,0:T(8,128)(2,1)S(1)} %get-tuple-element.43), channel_id=1, source_target_pairs={{0,18},{2,16},{4,22},{6,20},{8,26},{10,24},{12,30},{14,28},{16,2},... | collective-permute-start | bytes 417800 | tf_op jit(solution)/shard_map/ppermute | solution.py:236
  32.5 0.6 %collective-permute-done.3.refs_2_ = bf16[2,16,2176]{2,1,0:T(8,128)(2,1)S(1)} collective-permute-done((bf16[2,16,2176]{2,1,0:T(8,128)(2,1)S(1)}, bf16[2,16,2176]{2,1,0:T(8,128)(2,1)S(1)}, u32[]{:S(2)}, u32[]{:S(2)}) %collective-permute-start.3) | collective-permute-done | bytes 139296 | tf_op jit(solution)/shard_map/ppermute | solution.py:236
  33.1 1.3 %collective-permute-start.8 = (bf16[2,16,2176]{2,1,0:T(8,128)(2,1)S(1)}, bf16[2,16,2176]{2,1,0:T(8,128)(2,1)S(1)}, u32[]{:S(2)}, u32[]{:S(2)}) collective-permute-start(bf16[2,16,2176]{2,1,0:T(8,128)(2,1)S(1)} %get-tuple-element.44), channel_id=1, source_target_pairs={{0,22},{2,20},{4,18},{6,16},{8,30},{10,28},{12,26},{14,24},{16,6},... | collective-permute-start | bytes 417800 | tf_op jit(solution)/shard_map/ppermute | solution.py:236
  34.4 3.1 %stage.1.x_ref = bf16[4,224,4096]{2,1,0:T(8,128)(2,1)S(1)} custom-call(bf16[4,224,4096]{2,1,0:T(8,128)(2,1)} %x_ref.2), custom_call_target="tpu_custom_call" | custom-call | bytes 14680064 | tf_op jit(solution)/shard_map/stage/pallas_call | solution.py:239
  37.5 0.9 %collective-permute-done.4.refs_0_ = bf16[2,16,2176]{2,1,0:T(8,128)(2,1)S(1)} collective-permute-done((bf16[2,16,2176]{2,1,0:T(8,128)(2,1)S(1)}, bf16[2,16,2176]{2,1,0:T(8,128)(2,1)S(1)}, u32[]{:S(2)}, u32[]{:S(2)}) %collective-permute-start.4) | collective-permute-done | bytes 139296 | tf_op jit(solution)/shard_map/ppermute | solution.py:236
  38.5 1.7 %shrink.2 = (f32[4,112,128]{2,1,0:T(8,128)S(1)}, bf16[128,128]{1,0:T(8,128)(2,1)S(1)}) custom-call(s32[8]{0:T(128)S(1)} %copy-done, bf16[4,224,4096]{2,1,0:T(8,128)(2,1)S(1)} %stage.1.x_ref, bf16[2,16,2176]{2,1,0:T(8,128)(2,1)S(1)} %get-tuple-element.45.refs_0_, bf16[2,16,2176]{2,1,0:T(8,128)(2,1)S(1)} %collective-permute-done.2.refs_1_, ...), custom_call_target="tpu_custom_call" | custom-call | flops 469762048 | bytes 3670016 | tf_op jit(solution)/shard_map/shrink/pallas_call | solution.py:259
  40.1 1.4 %collective-permute-done.7.refs_2_ = bf16[2,16,2176]{2,1,0:T(8,128)(2,1)S(1)} collective-permute-done((bf16[2,16,2176]{2,1,0:T(8,128)(2,1)S(1)}, bf16[2,16,2176]{2,1,0:T(8,128)(2,1)S(1)}, u32[]{:S(2)}, u32[]{:S(2)}) %collective-permute-start.7) | collective-permute-done | bytes 139296 | tf_op jit(solution)/shard_map/ppermute | solution.py:236
  41.6 1.7 %shrink.3 = (f32[4,112,128]{2,1,0:T(8,128)S(1)}, bf16[128,256]{1,0:T(8,128)(2,1)S(1)}) custom-call(s32[8]{0:T(128)S(1)} %copy-done, bf16[4,224,4096]{2,1,0:T(8,128)(2,1)S(1)} %stage.1.x_ref, bf16[2,16,2176]{2,1,0:T(8,128)(2,1)S(1)} %collective-permute-done.4.refs_0_, bf16[2,16,2176]{2,1,0:T(8,128)(2,1)S(1)} %collective-permute-done.5.refs_1_, ...), custom_call_target="tpu_custom_call" | custom-call | flops 469762048 | bytes 3670016 | tf_op jit(solution)/shard_map/shrink/pallas_call | solution.py:259
  43.2 0.1 collective-permute-start.9
  43.3 1.5 %collective-permute-done.9.theirs_ref = f32[4,112,128]{2,1,0:T(8,128)S(1)} collective-permute-done((f32[4,112,128]{2,1,0:T(8,128)S(1)}, f32[4,112,128]{2,1,0:T(8,128)S(1)}, u32[]{:S(2)}, u32[]{:S(2)}) %collective-permute-start.9) | collective-permute-done | bytes 229408 | tf_op jit(solution)/shard_map/ppermute | solution.py:279
  44.8 1.1 %expand.1 = bf16[4,224,256]{2,1,0:T(8,128)(2,1)} custom-call(f32[4,112,128]{2,1,0:T(8,128)S(1)} %get-tuple-element.51.mine_ref, f32[4,112,128]{2,1,0:T(8,128)S(1)} %collective-permute-done.9.theirs_ref, bf16[128,256]{1,0:T(8,128)(2,1)S(1)} %get-tuple-element.52.up_ref, f32[896,256]{1,0:T(8,128)S(1)} %get-tuple-element.53.base_ref, ...), custom_call_target="tpu_custom_call" | custom-call | tf_op jit(solution)/shard_map/expand/pallas_call | solution.py:281
  (11 shorter events, 0.0 us)
Async XLA Ops:
  1.8 15.0 %copy-start.1 = (s32[8,2]{0,1:T(2,128)S(1)}, s32[8,2]{0,1:T(2,128)}, u32[]{:S(2)}) copy-start(s32[8,2]{0,1:T(2,128)} %param.12) | copy-start | bytes 196
  1.8 22.5 %copy-start.2 = (s32[8]{0:T(128)S(1)}, s32[8]{0:T(128)}, u32[]{:S(2)}) copy-start(s32[8]{0:T(128)} %home_ref.1) | copy-start | bytes 100
  1.8 22.5 %all-to-all-start = ((bf16[8,16,2176]{2,1,0:T(8,128)(2,1)}), bf16[8,16,2176]{2,1,0:T(8,128)(2,1)S(1)}, u32[]{:S(2)}, u32[]{:S(2)}) async-start(bf16[8,16,2176]{2,1,0:T(8,128)(2,1)} %pack.1), calls=%async_computation | async-start | bytes 1114112 | tf_op jit(solution)/shard_map/all_to_all | solution.py:188
  16.7 3.7 %collective-permute-start.1 = (f32[896,256]{1,0:T(8,128)S(1)}, f32[896,256]{1,0:T(8,128)S(1)}, u32[]{:S(2)}, u32[]{:S(2)}) collective-permute-start(f32[896,256]{1,0:T(8,128)S(1)} %get-tuple-element.31), channel_id=1, source_target_pairs={{0,1},{1,0},{2,3},{3,2},{4,5},{5,4},{6,7},{7,6},{8,9},{9,8},{10,11... | collective-permute-start | bytes 2752520 | tf_op jit(solution)/shard_map/ppermute | solution.py:216
  16.8 3.6 %collective-permute-start = (s32[2,8]{1,0:T(2,128)S(1)}, s32[2,8]{1,0:T(2,128)S(1)}, u32[]{:S(2)}, u32[]{:S(2)}) collective-permute-start(s32[2,8]{1,0:T(2,128)S(1)} %bitcast.5), channel_id=1, source_target_pairs={{0,16},{16,0},{1,17},{17,1},{2,18},{18,2},{3,19},{19,3},{4,20},{20... | collective-permute-start | bytes 200 | tf_op jit(solution)/shard_map/ppermute | solution.py:193
  25.0 5.7 %collective-permute-start.2 = (bf16[2,16,2176]{2,1,0:T(8,128)(2,1)S(1)}, bf16[2,16,2176]{2,1,0:T(8,128)(2,1)S(1)}, u32[]{:S(2)}, u32[]{:S(2)}) collective-permute-start(bf16[2,16,2176]{2,1,0:T(8,128)(2,1)S(1)} %get-tuple-element.36), channel_id=1, source_target_pairs={{0,16},{2,18},{4,20},{6,22},{8,24},{10,26},{12,28},{14,30},{16,0},... | collective-permute-start | bytes 417800 | tf_op jit(solution)/shard_map/ppermute | solution.py:236
  26.6 6.5 %collective-permute-start.3 = (bf16[2,16,2176]{2,1,0:T(8,128)(2,1)S(1)}, bf16[2,16,2176]{2,1,0:T(8,128)(2,1)S(1)}, u32[]{:S(2)}, u32[]{:S(2)}) collective-permute-start(bf16[2,16,2176]{2,1,0:T(8,128)(2,1)S(1)} %get-tuple-element.37), channel_id=1, source_target_pairs={{0,4},{2,6},{4,0},{6,2},{8,12},{10,14},{12,8},{14,10},{16,20},{18,... | collective-permute-start | bytes 417800 | tf_op jit(solution)/shard_map/ppermute | solution.py:236
  27.3 11.2 %collective-permute-start.4 = (bf16[2,16,2176]{2,1,0:T(8,128)(2,1)S(1)}, bf16[2,16,2176]{2,1,0:T(8,128)(2,1)S(1)}, u32[]{:S(2)}, u32[]{:S(2)}) collective-permute-start(bf16[2,16,2176]{2,1,0:T(8,128)(2,1)S(1)} %get-tuple-element.38), channel_id=1, source_target_pairs={{0,2},{2,0},{4,6},{6,4},{8,10},{10,8},{12,14},{14,12},{16,18},{18,... | collective-permute-start | bytes 417800 | tf_op jit(solution)/shard_map/ppermute | solution.py:236
  28.0 10.4 %collective-permute-start.5 = (bf16[2,16,2176]{2,1,0:T(8,128)(2,1)S(1)}, bf16[2,16,2176]{2,1,0:T(8,128)(2,1)S(1)}, u32[]{:S(2)}, u32[]{:S(2)}) collective-permute-start(bf16[2,16,2176]{2,1,0:T(8,128)(2,1)S(1)} %get-tuple-element.39), channel_id=1, source_target_pairs={{0,6},{2,4},{4,2},{6,0},{8,14},{10,12},{12,10},{14,8},{16,22},{18,... | collective-permute-start | bytes 417800 | tf_op jit(solution)/shard_map/ppermute | solution.py:236
  30.1 8.4 %collective-permute-start.6 = (bf16[2,16,2176]{2,1,0:T(8,128)(2,1)S(1)}, bf16[2,16,2176]{2,1,0:T(8,128)(2,1)S(1)}, u32[]{:S(2)}, u32[]{:S(2)}) collective-permute-start(bf16[2,16,2176]{2,1,0:T(8,128)(2,1)S(1)} %get-tuple-element.40), channel_id=1, source_target_pairs={{0,20},{2,22},{4,16},{6,18},{8,28},{10,30},{12,24},{14,26},{16,4},... | collective-permute-start | bytes 417800 | tf_op jit(solution)/shard_map/ppermute | solution.py:236
  30.7 10.8 %collective-permute-start.7 = (bf16[2,16,2176]{2,1,0:T(8,128)(2,1)S(1)}, bf16[2,16,2176]{2,1,0:T(8,128)(2,1)S(1)}, u32[]{:S(2)}, u32[]{:S(2)}) collective-permute-start(bf16[2,16,2176]{2,1,0:T(8,128)(2,1)S(1)} %get-tuple-element.43), channel_id=1, source_target_pairs={{0,18},{2,16},{4,22},{6,20},{8,26},{10,24},{12,30},{14,28},{16,2},... | collective-permute-start | bytes 417800 | tf_op jit(solution)/shard_map/ppermute | solution.py:236
  33.1 8.4 %collective-permute-start.8 = (bf16[2,16,2176]{2,1,0:T(8,128)(2,1)S(1)}, bf16[2,16,2176]{2,1,0:T(8,128)(2,1)S(1)}, u32[]{:S(2)}, u32[]{:S(2)}) collective-permute-start(bf16[2,16,2176]{2,1,0:T(8,128)(2,1)S(1)} %get-tuple-element.44), channel_id=1, source_target_pairs={{0,22},{2,20},{4,18},{6,16},{8,30},{10,28},{12,26},{14,24},{16,6},... | collective-permute-start | bytes 417800 | tf_op jit(solution)/shard_map/ppermute | solution.py:236
  34.4 4.1 %copy-start = (s32[8]{0:T(128)S(1)}, s32[8]{0:T(128)}, u32[]{:S(2)}) copy-start(s32[8]{0:T(128)} %count_ref.3) | copy-start | bytes 100
  43.2 1.6 %collective-permute-start.9 = (f32[4,112,128]{2,1,0:T(8,128)S(1)}, f32[4,112,128]{2,1,0:T(8,128)S(1)}, u32[]{:S(2)}, u32[]{:S(2)}) collective-permute-start(f32[4,112,128]{2,1,0:T(8,128)S(1)} %get-tuple-element.51.mine_ref), channel_id=1, source_target_pairs={{0,1},{1,0},{2,3},{3,2},{4,5},{5,4},{6,7},{7,6},{8,9},{9,8},{10,11... | collective-permute-start | bytes 688136 | tf_op jit(solution)/shard_map/ppermute | solution.py:279
